TPU v7x, 32 devices: a whole 2x2x4 slice. The times are simulated.
32 devices in a mesh: group: 2 (over y), tile: 16 (over z, x, core).
Axes of the slice: x: 2, y: 2, z: 4, core: 2. Of those that a mesh axis runs over, the one named last changes fastest.
Arguments:
- increment: float32 [32, 221184], P(None, ('group', 'tile')), parts along dimension 1, may hold values from -6 to 6
- send_slots: int32 [110592, 4], P('tile'), may hold values from 0 to 2047, all different within a row; in each aligned block of 6912 rows (0 to 6911, 6912 to 13823, ...) at most 64 rows name the same one
- tent_weight: float32 [4, 110592], P(None, 'tile'), may hold values from 0.05 to 0.5
- coarse_cell: int32 [32768], P('tile'), may hold values from 0 to 3455
- diffusivity: float32 [288, 192], P('tile'), may hold values from 0.04 to 0.24
Outputs:
- result: float32 [32, 221184], P(None, ('group', 'tile')), parts along dimension 1
- coarse_field: float32 [32, 576, 192], P(None, ('group', 'tile')), parts along dimension 1
There are 2 independent parts, one for each index of `group`. A program takes and returns all parts, laid end to end along the dimension named above; an argument that names none is the same for every part. Nothing has to cross between parts.
Inputs may be any that keep to these rules, and one draw needn't show every extreme that they name: `send_slots`: each row names four different slots; among the rows of one device no slot is named by more than 64 rows, a bound that some block reaches; every slot is named by some row.
All inputs are finite; a program needn't handle non-finite values.
Results may differ from a plain program's by a relative error of at most 0.00002.
Values sent between devices are 32-bit elements; how exact they have to be, the bound alone decides.
No kernel may reach another device: no remote copies, remote signals or barrier semaphores. Data moves between devices by JAX's collectives and lax.ppermute only.
A program may use at most 64 MiB of HBM per device.

v0:
```python
import jax
import jax.numpy as jnp
from jax import lax
from jax.sharding import PartitionSpec as P

STEPS = 5


def padded_2(cells, sides, width):
    for axis, dim in sides:
        count = lax.axis_size(axis)
        head = lax.slice_in_dim(cells, 0, width, axis=dim)
        tail = lax.slice_in_dim(cells, cells.shape[dim] - width, cells.shape[dim], axis=dim)
        cells = jnp.concatenate(
            [
                lax.ppermute(tail, axis, [(i, (i + 1) % count) for i in range(count)]),
                cells,
                lax.ppermute(head, axis, [((i + 1) % count, i) for i in range(count)]),
            ],
            axis=dim,
        )
    return cells


def one_step(padded, coef_rows):
    inner = padded[:, 1:-1]
    spread = padded[:, 2:] + padded[:, :-2] + jnp.roll(inner, 1, 2) + jnp.roll(inner, -1, 2)
    return inner + coef_rows[None] * (spread - 4.0 * inner)


def diffuse_block(coarse, diffusivity):
    joined = jnp.concatenate([coarse, diffusivity[None]], 0)
    padded_all = padded_2(joined, (("tile", 1),), STEPS)
    padded = padded_all[:-1]
    coef_rows = padded_all[-1]
    for turn in range(STEPS):
        padded = one_step(padded, coef_rows[1:-1])
        coef_rows = coef_rows[1:-1]
    return padded


def gather_cells(received, coarse_cell, diffusivity):
    channels = received.shape[0]
    rows, width = diffusivity.shape
    coarse = jnp.zeros((channels, rows * width), jnp.float32).at[:, coarse_cell].add(received)
    coarse = diffuse_block(coarse.reshape(channels, rows, width), diffusivity)
    return (coarse, coarse.reshape(channels, -1)[:, coarse_cell])


def body(increment, send_slots, tent_weight, coarse_cell, diffusivity):
    channels = increment.shape[0]
    slot_count = coarse_cell.shape[0]
    send_buffer = jnp.zeros((channels, slot_count), jnp.float32)
    for corner in range(4):
        send_buffer = send_buffer.at[:, send_slots[:, corner]].add(
            tent_weight[corner][None, :] * increment
        )
    received = lax.all_to_all(send_buffer, "tile", split_axis=1, concat_axis=1, tiled=True)
    coarse, values = gather_cells(received, coarse_cell, diffusivity)
    returned = lax.all_to_all(values, "tile", split_axis=1, concat_axis=1, tiled=True)
    result = jnp.zeros_like(increment)
    for corner in range(4):
        result = result + tent_weight[corner][None, :] * returned[:, send_slots[:, corner]]
    return (result, coarse)


def solution(mesh):
    in_specs = (
        P(None, ("group", "tile")),
        P("tile", None),
        P(None, "tile"),
        P("tile"),
        P("tile", None),
    )
    out_specs = (P(None, ("group", "tile")), P(None, ("group", "tile"), None))
    return jax.shard_map(body, mesh=mesh, in_specs=in_specs, out_specs=out_specs, check_vma=False)
```

profile of v0, /device:TPU:0, one launch (start us, length us, event | category | flops | bytes accessed | tf_op | source)
XLA Modules:
  0.0 310.3 jit_solution(15977560183872191449)
XLA Ops:
  0.6 2.1 fusion.32
  6.3 2.4 copy.36
  8.7 2.4 copy.34
  11.1 2.5 copy.33
  13.6 2.4 copy.35
  16.0 39.3 %scatter_custom_fusion = f32[32,2048]{0,1:T(8,128)S(1)} fusion(s32[6912]{0:T(1024)S(1)} %copy-done.8, f32[6912,32]{1,0:T(8,128)} %copy.33, f32[]{:T(128)} %constant.5.clone.1), kind=kCustom, calls=%fused_computation.48 | custom fusion | flops 221184 | bytes 262656 | tf_op jit(solution)/shard_map/scatter-add | solution.py:55
  55.3 39.5 %scatter_fusion = f32[32,2048]{0,1:T(8,128)S(1)} fusion(f32[32,2048]{0,1:T(8,128)S(1)} %scatter_custom_fusion, s32[6912]{0:T(1024)S(1)} %copy-done.5, f32[6912,32]{1,0:T(8,128)} %copy.34), kind=kCustom, calls=%fused_computation.6 | custom fusion | flops 221184 | bytes 2681856 | tf_op jit(solution)/shard_map/scatter-add | solution.py:55
  94.8 39.5 %scatter_fusion.1 = f32[32,2048]{0,1:T(8,128)S(1)} fusion(f32[32,2048]{0,1:T(8,128)S(1)} %scatter_fusion, s32[6912]{0:T(1024)S(1)} %copy-done.7, f32[6912,32]{1,0:T(8,128)} %copy.35), kind=kCustom, calls=%fused_computation.7 | custom fusion | flops 221184 | bytes 2681856 | tf_op jit(solution)/shard_map/scatter-add | solution.py:55
  134.3 39.6 %scatter_fusion.2 = f32[32,2048]{0,1:T(8,128)S(1)} fusion(f32[32,2048]{0,1:T(8,128)S(1)} %scatter_fusion.1, s32[6912]{0:T(1024)S(1)} %copy-done.6, f32[6912,32]{1,0:T(8,128)} %copy.36), kind=kCustom, calls=%fused_computation.8 | custom fusion | flops 221184 | bytes 2681856 | tf_op jit(solution)/shard_map/scatter-add | solution.py:55
  175.0 7.5 %all-to-all-start = ((f32[32,16,128]{2,0,1:T(8,128)}), f32[32,16,128]{2,0,1:T(8,128)S(1)}, u32[]{:S(2)}, u32[]{:S(2)}) async-start(f32[32,16,128]{2,0,1:T(8,128)} %copy.37), calls=%async_computation | async-start | bytes 524288 | tf_op jit(solution)/shard_map/all_to_all | solution.py:58
  182.5 10.0 %all-to-all-done = f32[32,16,128]{2,0,1:T(8,128)S(1)} async-done(((f32[32,16,128]{2,0,1:T(8,128)}), f32[32,16,128]{2,0,1:T(8,128)S(1)}, u32[]{:S(2)}, u32[]{:S(2)}) %all-to-all-start) | async-done | bytes 262176 | tf_op jit(solution)/shard_map/all_to_all | solution.py:58
  193.9 12.3 %scatter_custom_fusion.4 = f32[32,3456]{0,1:T(8,128)S(1)} fusion(s32[2048]{0:T(1024)S(1)} %get-tuple-element.45, f32[2048,32]{1,0:T(8,128)} %copy.39, f32[]{:T(128)} %constant.5.clone.1), kind=kCustom, calls=%fused_computation.22 | custom fusion | flops 65536 | bytes 442880 | tf_op jit(solution)/shard_map/scatter-add | solution.py:45
  207.2 4.4 %collective-permute-start.1 = (f32[33,5,192]{2,1,0:T(8,128)S(1)}, f32[33,5,192]{2,1,0:T(8,128)S(1)}, u32[]{:S(2)}, u32[]{:S(2)}) collective-permute-start(f32[33,5,192]{2,1,0:T(8,128)S(1)} %get-tuple-element.31), channel_id=1, source_target_pairs={{1,0},{2,1},{3,2},{4,3},{5,4},{6,5},{7,6},{8,7},{9,8},{10,9},{11,1... | collective-permute-start | bytes 380168 | tf_op jit(solution)/shard_map/ppermute | solution.py:18
  211.6 4.2 %collective-permute-done = f32[33,5,192]{2,1,0:T(8,128)S(1)} collective-permute-done((f32[33,5,192]{2,1,0:T(8,128)S(1)}, f32[33,5,192]{2,1,0:T(8,128)S(1)}, u32[]{:S(2)}, u32[]{:S(2)}) %collective-permute-start) | collective-permute-done | bytes 126752 | tf_op jit(solution)/shard_map/ppermute | solution.py:16
  222.1 7.6 %gather_fusion = f32[2048,32]{1,0:T(8,128)} fusion(f32[32,3456]{0,1:T(8,128)S(1)} %bitcast.38, s32[2048]{0:T(1024)S(1)} %get-tuple-element.44), kind=kCustom, calls=%fused_computation | custom fusion | bytes 532480 | tf_op jit(solution)/shard_map/gather | solution.py:47
  229.6 2.2 copy.42
  231.9 5.7 %all-to-all-start.1 = ((f32[32,16,128]{2,0,1:T(8,128)}), f32[32,16,128]{2,0,1:T(8,128)S(1)}, u32[]{:S(2)}, u32[]{:S(2)}) async-start(f32[32,16,128]{2,0,1:T(8,128)} %copy.42), calls=%async_computation.1 | async-start | bytes 524288 | tf_op jit(solution)/shard_map/all_to_all | solution.py:60
  238.6 9.0 %all-to-all-done.1 = f32[32,16,128]{2,0,1:T(8,128)S(1)} async-done(((f32[32,16,128]{2,0,1:T(8,128)}), f32[32,16,128]{2,0,1:T(8,128)S(1)}, u32[]{:S(2)}, u32[]{:S(2)}) %all-to-all-start.1) | async-done | bytes 262176 | tf_op jit(solution)/shard_map/all_to_all | solution.py:60
  248.0 13.5 %gather_fusion.4 = f32[6912,32]{1,0:T(8,128)} fusion(f32[32,2048]{0,1:T(8,128)S(1)} %bitcast.33, s32[7168]{0:T(1024)S(1)} %get-tuple-element.46), kind=kCustom, calls=%fused_computation.4 | custom fusion | bytes 1797120 | tf_op jit(solution)/shard_map/gather | solution.py:63
  261.5 13.5 %gather_fusion.3 = f32[6912,32]{1,0:T(8,128)} fusion(f32[32,2048]{0,1:T(8,128)S(1)} %bitcast.34, s32[7168]{0:T(1024)S(1)} %get-tuple-element.47), kind=kCustom, calls=%fused_computation.3 | custom fusion | bytes 1797120 | tf_op jit(solution)/shard_map/gather | solution.py:63
  274.9 13.5 %gather_fusion.2 = f32[6912,32]{1,0:T(8,128)} fusion(f32[32,2048]{0,1:T(8,128)S(1)} %bitcast.35, s32[7168]{0:T(1024)S(1)} %get-tuple-element.48), kind=kCustom, calls=%fused_computation.2 | custom fusion | bytes 1797120 | tf_op jit(solution)/shard_map/gather | solution.py:63
  288.4 13.5 %gather_fusion.1 = f32[6912,32]{1,0:T(8,128)} fusion(f32[32,2048]{0,1:T(8,128)S(1)} %bitcast.36, s32[7168]{0:T(1024)S(1)} %get-tuple-element.49), kind=kCustom, calls=%fused_computation.1 | custom fusion | bytes 1797120 | tf_op jit(solution)/shard_map/gather | solution.py:63
  301.9 6.4 %add_bitcast_fusion = f32[32,6912]{0,1:T(8,128)S(1)} fusion(f32[6912,32]{1,0:T(8,128)} %gather_fusion.4, f32[6912,32]{1,0:T(8,128)} %gather_fusion.3, f32[6912,32]{1,0:T(8,128)} %gather_fusion.2, f32[6912,32]{1,0:T(8,128)} %gather_fusion.1, f32[6912]{0:T(1024)} %copy-done.1, f32[6912]{0:T(1024)} %copy-done.4, f32[6912]{0:T(1024)} %copy-done.2, f32[6912]{0:T(1024)} %copy-done.3), kind=kLoop, calls=%fused_computation.10 | loop fusion | flops 1548288 | bytes 4534272 | tf_op jit(solution)/shard_map/add | solution.py:63
  308.3 2.0 copy.44
  (55 shorter events, 14.3 us)
Async XLA Ops:
  4.2 0.6 copy-start.1
  4.2 2.1 copy-start.2
  4.2 2.1 copy-start.3
  4.2 2.1 copy-start.4
  11.1 4.9 %copy-start.8 = (s32[6912]{0:T(1024)S(1)}, s32[6912]{0:T(1024)}, u32[]{:S(2)}) copy-start(s32[6912]{0:T(1024)} %get-tuple-element.16) | copy-start | bytes 82948
  13.6 41.7 %copy-start.5 = (s32[6912]{0:T(1024)S(1)}, s32[6912]{0:T(1024)}, u32[]{:S(2)}) copy-start(s32[6912]{0:T(1024)} %get-tuple-element.15) | copy-start | bytes 82948
  55.3 39.5 %copy-start.7 = (s32[6912]{0:T(1024)S(1)}, s32[6912]{0:T(1024)}, u32[]{:S(2)}) copy-start(s32[6912]{0:T(1024)} %get-tuple-element.17) | copy-start | bytes 82948
  94.8 39.5 %copy-start.6 = (s32[6912]{0:T(1024)S(1)}, s32[6912]{0:T(1024)}, u32[]{:S(2)}) copy-start(s32[6912]{0:T(1024)} %get-tuple-element.14) | copy-start | bytes 82948
  134.3 48.2 %copy-start.9 = (s32[2048]{0:T(1024)S(1)}, s32[2048]{0:T(1024)}, u32[]{:S(2)}) copy-start(s32[2048]{0:T(1024)} %param.8) | copy-start | bytes 24580
  175.0 32.1 %copy-start = (f32[18,192]{1,0:T(8,128)S(1)}, f32[18,192]{1,0:T(8,128)}, u32[]{:S(2)}) copy-start(f32[18,192]{1,0:T(8,128)} %param.9) | copy-start | bytes 41476
  175.0 17.5 %all-to-all-start = ((f32[32,16,128]{2,0,1:T(8,128)}), f32[32,16,128]{2,0,1:T(8,128)S(1)}, u32[]{:S(2)}, u32[]{:S(2)}) async-start(f32[32,16,128]{2,0,1:T(8,128)} %copy.37), calls=%async_computation | async-start | bytes 524288 | tf_op jit(solution)/shard_map/all_to_all | solution.py:58
  207.1 8.7 %collective-permute-start = (f32[33,5,192]{2,1,0:T(8,128)S(1)}, f32[33,5,192]{2,1,0:T(8,128)S(1)}, u32[]{:S(2)}, u32[]{:S(2)}) collective-permute-start(f32[33,5,192]{2,1,0:T(8,128)S(1)} %get-tuple-element.30), channel_id=1, source_target_pairs={{0,1},{1,2},{2,3},{3,4},{4,5},{5,6},{6,7},{7,8},{8,9},{9,10},{10,1... | collective-permute-start | bytes 380168 | tf_op jit(solution)/shard_map/ppermute | solution.py:16
  207.2 8.7 %collective-permute-start.1 = (f32[33,5,192]{2,1,0:T(8,128)S(1)}, f32[33,5,192]{2,1,0:T(8,128)S(1)}, u32[]{:S(2)}, u32[]{:S(2)}) collective-permute-start(f32[33,5,192]{2,1,0:T(8,128)S(1)} %get-tuple-element.31), channel_id=1, source_target_pairs={{1,0},{2,1},{3,2},{4,3},{5,4},{6,5},{7,6},{8,7},{9,8},{10,9},{11,1... | collective-permute-start | bytes 380168 | tf_op jit(solution)/shard_map/ppermute | solution.py:18
  231.9 15.8 %all-to-all-start.1 = ((f32[32,16,128]{2,0,1:T(8,128)}), f32[32,16,128]{2,0,1:T(8,128)S(1)}, u32[]{:S(2)}, u32[]{:S(2)}) async-start(f32[32,16,128]{2,0,1:T(8,128)} %copy.42), calls=%async_computation.1 | async-start | bytes 524288 | tf_op jit(solution)/shard_map/all_to_all | solution.py:60
where the time goes:
time: 311 us; the launch traced here: 310 us
  other arithmetic  183 us (59%)
  local copies, waits for them, and re-layouts  85.2 us (27%)
  waiting for transfers between devices  23.3 us (7%)
  starting transfers between devices  17.7 us (6%)
    scatter-add x4, other arithmetic, body(): send_buffer.at[:, send_slots[:, corner]]  158 us
    gather x4, local copies, waits for them, and re-layouts, body(): returned[:, send_slots[:, corner]]  53.9 us
    scatter-add x1, other arithmetic, gather_cells(): jnp.zeros((channels, rows * width), jnp.float32).at[:, coarse_cell]  12.3 us
    all_to_all x1, waiting for transfers between devices, body(): lax.all_to_all(send_buffer, 'tile', split_axis=1, concat_axis=1, tiled=True)  10 us
    mul x4, local copies, waits for them, and re-layouts, body(): tent_weight[corner][None, :] * increment  9.74 us
    all_to_all x1, waiting for transfers between devices, body(): lax.all_to_all(values, 'tile', split_axis=1, concat_axis=1, tiled=True)  9.01 us
    gather x1, local copies, waits for them, and re-layouts, gather_cells(): return (coarse, coarse.reshape(channels, -1)[:, coarse_cell])  7.58 us
    all_to_all x1, starting transfers between devices, body(): lax.all_to_all(send_buffer, 'tile', split_axis=1, concat_axis=1, tiled=True)  7.49 us
  transfers between devices with their start and end apart: 4, of which 3 were waited for; matrix products, arithmetic and copies ran while one was open for 0% of the time, Pallas kernels for 0%

commit v1 on v0

v1 whole, which is shorter than its diff:
```python
import functools

import jax
import jax.numpy as jnp
from jax import lax
from jax.experimental import pallas as pl
from jax.experimental.pallas import tpu as pltpu
from jax.sharding import PartitionSpec as P

STEPS = 5
CORNERS = 4
LANES = 128
PLACES = 256
BF16 = jnp.bfloat16
F32 = jnp.float32
VMEM = pl.BlockSpec(memory_space=pltpu.VMEM)


def halves(values):
    high = values.astype(BF16)
    return high, (values - high.astype(F32)).astype(BF16)


def one_hot(places, length):
    rows = lax.broadcasted_iota(jnp.int32, (length, places.shape[1]), 0)
    return jnp.where(rows == places, 1.0, 0.0).astype(BF16)


def masked(values, marks, count):
    marks = jnp.broadcast_to(marks, values.shape)
    zero = jnp.zeros((), values.dtype)
    return jnp.concatenate([jnp.where(marks == k, values, zero) for k in range(count)], 0)


def dot_last(left, right):
    return lax.dot_general(left, right, (((1,), (1,)), ((), ())), preferred_element_type=F32)


def sum_to_slots(inc_ref, slot_ref, weight_ref, sent_ref, *, chunk):
    channels, fine = inc_ref.shape
    count = sent_ref.shape[0] * LANES // PLACES
    sent_ref[...] = jnp.zeros_like(sent_ref)

    def step(turn, carry):
        columns = pl.ds(pl.multiple_of(turn * chunk, LANES), chunk)
        inc = inc_ref[:, columns]
        left, right = [], []
        for corner in range(CORNERS):
            slots = slot_ref[corner : corner + 1, columns]
            parts = jnp.concatenate(halves(weight_ref[corner : corner + 1, columns] * inc), 0)
            left.append(masked(parts, slots // PLACES, count))
            right.append(one_hot(slots % PLACES, PLACES))
        sums = dot_last(jnp.concatenate(left, 1), jnp.concatenate(right, 1))
        for k in range(count):
            both = sums[2 * channels * k : 2 * channels * (k + 1)]
            both = both[:channels] + both[channels:]
            for part in range(PLACES // LANES):
                sent_ref[k * (PLACES // LANES) + part] += both[:, LANES * part : LANES * (part + 1)]
        return carry

    lax.fori_loop(0, fine // chunk, step, 0)


def wide_column(width):
    lanes = lax.broadcasted_iota(jnp.int32, (2 * LANES, 1), 0)
    extra = (2 * LANES - width) // 2
    return jnp.where(lanes < width, lanes, jnp.where(lanes < width + extra, lanes - width, lanes - 2 * LANES + width))


def add_to_cells(rec_ref, cell_ref, coarse_ref, head_ref, tail_ref, *, width):
    rows, channels, wide = coarse_ref.shape
    senders = rec_ref.shape[0]
    cells = jnp.concatenate([cell_ref[s : s + 1, :] for s in range(senders)], 1)
    values = jnp.concatenate([rec_ref[s] for s in range(senders)], 1)
    y = cells // width
    right = jnp.where(wide_column(width) == cells - y * width, 1.0, 0.0).astype(BF16)
    left = masked(jnp.concatenate(halves(values), 0), y, rows)
    sums = dot_last(left, right)
    for k in range(rows):
        both = sums[2 * channels * k : 2 * channels * (k + 1)]
        both = both[:channels] + both[channels:]
        coarse_ref[k] = both
        if k < STEPS:
            head_ref[k] = both
        if k >= rows - STEPS:
            tail_ref[k - rows + STEPS] = both


def diffuse_and_read(coarse_ref, before_ref, after_ref, coef_ref, cell_ref, field_ref, values_ref, one_ref, two_ref, *, width):
    rows, channels, wide = coarse_ref.shape
    senders = values_ref.shape[0]
    total = rows + 2 * STEPS
    one_ref[0:STEPS] = before_ref[...]
    one_ref[STEPS : STEPS + rows] = coarse_ref[...]
    one_ref[STEPS + rows : total] = after_ref[...]
    held, other = one_ref, two_ref
    for turn in range(1, STEPS + 1):
        for y in range(turn, total - turn):
            here = held[y]
            spread = held[y + 1] + held[y - 1] + pltpu.roll(here, 1, 1) + pltpu.roll(here, wide - 1, 1)
            other[y] = here + coef_ref[y : y + 1, :] * (spread - 4.0 * here)
        held, other = other, held
    final = held[STEPS : STEPS + rows]
    field_ref[...] = final[:, :, :width]
    left = jnp.concatenate(halves(final.reshape(rows * channels, wide)), 1)
    for s in range(0, senders, 2):
        cells = jnp.concatenate([cell_ref[s : s + 1, :], cell_ref[s + 1 : s + 2, :]], 1)
        y = cells // width
        right = one_hot(cells - y * width, wide)
        found = jnp.dot(left, jnp.concatenate([right, right], 0), preferred_element_type=F32)
        out = jnp.zeros((channels, 2 * LANES), F32)
        marks = jnp.broadcast_to(y, out.shape)
        for k in range(rows):
            out = jnp.where(marks == k, found[channels * k : channels * (k + 1)], out)
        values_ref[s] = out[:, :LANES]
        values_ref[s + 1] = out[:, LANES:]


def sum_from_slots(ret_ref, slot_ref, weight_ref, result_ref, table_ref, *, chunk):
    channels, fine = result_ref.shape
    count = ret_ref.shape[0] * LANES // PLACES
    group = PLACES // LANES
    for k in range(count):
        high, low = halves(jnp.concatenate([ret_ref[group * k + part] for part in range(group)], 1))
        table_ref[channels * k : channels * (k + 1), :PLACES] = high
        table_ref[channels * k : channels * (k + 1), PLACES:] = low

    def step(turn, carry):
        columns = pl.ds(pl.multiple_of(turn * chunk, LANES), chunk)
        total = jnp.zeros((channels, chunk), F32)
        for corner in range(CORNERS):
            slots = slot_ref[corner : corner + 1, columns]
            right = one_hot(slots % PLACES, PLACES)
            found = jnp.dot(table_ref[...], jnp.concatenate([right, right], 0), preferred_element_type=F32)
            marks = jnp.broadcast_to(slots // PLACES, total.shape)
            out = found[:channels]
            for k in range(1, count):
                out = jnp.where(marks == k, found[channels * k : channels * (k + 1)], out)
            total = total + weight_ref[corner : corner + 1, columns] * out
        result_ref[:, columns] = total
        return carry

    lax.fori_loop(0, fine // chunk, step, 0)


def chunk_of(fine, most):
    return max(c for c in range(LANES, most + 1, LANES) if fine % c == 0)


def call(kernel, out, scratch=()):
    return pl.pallas_call(
        kernel,
        out_shape=out,
        scratch_shapes=list(scratch),
        compiler_params=pltpu.CompilerParams(vmem_limit_bytes=48 << 20),
    )


def body(increment, send_slots, tent_weight, coarse_cell, diffusivity):
    channels, fine = increment.shape
    slot_count = coarse_cell.shape[0]
    rows, width = diffusivity.shape
    tiles = lax.axis_size("tile")
    share = slot_count // tiles
    blocks = slot_count // LANES
    wide = 2 * LANES
    ahead = [(i, (i + 1) % tiles) for i in range(tiles)]
    back = [((i + 1) % tiles, i) for i in range(tiles)]
    shape = jax.ShapeDtypeStruct
    slots = send_slots.T
    cells = coarse_cell.reshape(blocks, LANES)

    extra = (wide - width) // 2
    coef = jnp.concatenate([diffusivity, diffusivity[:, :extra], diffusivity[:, width - extra :]], 1)
    coef = jnp.concatenate(
        [lax.ppermute(coef[rows - STEPS :], "tile", ahead), coef, lax.ppermute(coef[:STEPS], "tile", back)], 0
    )

    sent = call(functools.partial(sum_to_slots, chunk=chunk_of(fine, 2304)), shape((blocks, channels, LANES), F32))(
        increment, slots, tent_weight
    )
    received = exchange(sent, tiles, share)
    coarse, head, tail = call(
        functools.partial(add_to_cells, width=width),
        [
            shape((rows, channels, wide), F32),
            shape((STEPS, channels, wide), F32),
            shape((STEPS, channels, wide), F32),
        ],
    )(received, cells)
    before = lax.ppermute(tail, "tile", ahead)
    after = lax.ppermute(head, "tile", back)
    padded = pltpu.VMEM((rows + 2 * STEPS, channels, wide), F32)
    field, values = call(
        functools.partial(diffuse_and_read, width=width),
        [shape((rows, channels, width), F32), shape((blocks, channels, LANES), F32)],
        [padded, padded],
    )(coarse, before, after, coef, cells)
    returned = exchange(values, tiles, share)
    result = call(
        functools.partial(sum_from_slots, chunk=chunk_of(fine, 768)),
        shape((channels, fine), F32),
        [pltpu.VMEM((channels * slot_count // PLACES, 2 * PLACES), BF16)],
    )(returned, slots, tent_weight)
    return (result, field.transpose(1, 0, 2))


def exchange(blocks, tiles, share):
    count, channels, lanes = blocks.shape
    if share == lanes:
        return lax.all_to_all(blocks, "tile", split_axis=0, concat_axis=0, tiled=True)
    flat = blocks.transpose(1, 0, 2).reshape(channels, count * lanes)
    flat = lax.all_to_all(flat, "tile", split_axis=1, concat_axis=1, tiled=True)
    return flat.reshape(channels, count, lanes).transpose(1, 0, 2)


def solution(mesh):
    in_specs = (
        P(None, ("group", "tile")),
        P("tile", None),
        P(None, "tile"),
        P("tile"),
        P("tile", None),
    )
    out_specs = (P(None, ("group", "tile")), P(None, ("group", "tile"), None))
    return jax.shard_map(body, mesh=mesh, in_specs=in_specs, out_specs=out_specs, check_vma=False)
```

time: 311 us -> 73.7 us (0.24)
  other arithmetic: 183 us -> 0.16 us
  local copies, waits for them, and re-layouts: 85.2 us -> 3.05 us
  Pallas kernels: 0 us -> 25.8 us
  blocking collectives: 0 us -> 15.8 us
  waiting for transfers between devices: 23.3 us -> 11.3 us
    scatter-add x5 -> x0, other arithmetic: 170 us -> none  [the longest x4 158 us: body(): send_buffer.at[:, send_slots[:, corner]]]
    gather x5 -> x0, local copies, waits for them, and re-layouts: 61.5 us -> none  [the longest x4 53.9 us: body(): returned[:, send_slots[:, corner]]]
    pallas_call x0 -> x4, Pallas kernels: none -> 25.8 us  [the longest x1 12.1 us: body(): call(functools.partial(sum_from_slots, chunk=chunk_of(fine, 768)), shape(...]
    all_to_all x0 -> x1, blocking collectives: none -> 15.8 us  [exchange(): lax.all_to_all(blocks, 'tile', split_axis=0, concat_axis=0, tiled=True)]
    mul x4 -> x0, local copies, waits for them, and re-layouts: 9.74 us -> none  [body(): tent_weight[corner][None, :] * increment]
    add x6 -> x0, other arithmetic: 9.19 us -> none  [the longest x1 6.39 us: body(): result + tent_weight[corner][None, :] * returned[:, send_slots[:, corner]]]
    all_to_all x2 -> x1, waiting for transfers between devices: 19 us -> 9.95 us  [exchange(): lax.all_to_all(blocks, 'tile', split_axis=0, concat_axis=0, tiled=True)]
    all_to_all x2 -> x1, starting transfers between devices: 13.2 us -> 7.49 us  [exchange(): lax.all_to_all(blocks, 'tile', split_axis=0, concat_axis=0, tiled=True)]
  transfers between devices with their start and end apart: 4 -> 5, of which waited for: 3 -> 2; matrix products, arithmetic and copies ran while one was open for 0% -> 0% of each run, Pallas kernels for 0% -> 0%
where the time goes in v1:
time: 73.7 us; the launch traced here: 73.3 us
  Pallas kernels  25.8 us (35%)
  starting transfers between devices  16.4 us (22%)
  blocking collectives  15.8 us (21%)
  waiting for transfers between devices  11.3 us (15%)
  local copies, waits for them, and re-layouts  3.05 us (4%)
    all_to_all x1, blocking collectives, exchange(): lax.all_to_all(blocks, 'tile', split_axis=0, concat_axis=0, tiled=True)  15.8 us
    pallas_call x1, Pallas kernels, body(): call(functools.partial(sum_from_slots, chunk=chunk_of(fine, 768)), shape(...  12.1 us
    all_to_all x1, waiting for transfers between devices, exchange(): lax.all_to_all(blocks, 'tile', split_axis=0, concat_axis=0, tiled=True)  9.95 us
    pallas_call x1, Pallas kernels, body(): call(functools.partial(sum_to_slots, chunk=chunk_of(fine, 2304)), shape((...  9.01 us
    all_to_all x1, starting transfers between devices, exchange(): lax.all_to_all(blocks, 'tile', split_axis=0, concat_axis=0, tiled=True)  7.49 us
    ppermute x1, starting transfers between devices, body(): lax.ppermute(coef[:STEPS], 'tile', back)  4.44 us
    ppermute x1, starting transfers between devices, body(): after = lax.ppermute(head, 'tile', back)  4.43 us
    pallas_call x1, Pallas kernels, body(): call(functools.partial(diffuse_and_read, width=width), [shape((rows, chan...  3.33 us
  transfers between devices with their start and end apart: 5, of which 2 were waited for; matrix products, arithmetic and copies ran while one was open for 0% of the time, Pallas kernels for 0%

profile of v1, /device:TPU:0, one launch (start us, length us, event | category | flops | bytes accessed | tf_op | source)
XLA Modules:
  0.0 73.3 jit_solution(13423684825538355393)
XLA Ops:
  0.6 1.2 %copy-done = f32[32,6912]{1,0:T(8,128)S(1)} copy-done((f32[32,6912]{1,0:T(8,128)S(1)}, f32[32,6912]{1,0:T(8,128)}, u32[]{:S(2)}) %copy-start) | copy-done | bytes 884760
  1.8 0.9 %copy-done.1 = s32[6912,4]{0,1:T(4,128)S(1)} copy-done((s32[6912,4]{0,1:T(4,128)S(1)}, s32[6912,4]{0,1:T(4,128)}, u32[]{:S(2)}) %copy-start.1) | copy-done | bytes 110616
  2.7 0.9 %copy-done.3 = f32[4,6912]{1,0:T(4,128)S(1)} copy-done((f32[4,6912]{1,0:T(4,128)S(1)}, f32[4,6912]{1,0:T(4,128)}, u32[]{:S(2)}) %copy-start.3) | copy-done | bytes 110616
  3.6 9.0 %shard_map.68 = f32[16,32,128]{2,1,0:T(8,128)} custom-call(f32[32,6912]{1,0:T(8,128)S(1)} %copy-done, s32[4,6912]{1,0:T(4,128)S(1)} %bitcast.3, f32[4,6912]{1,0:T(4,128)S(1)} %copy-done.3), custom_call_target="tpu_custom_call" | custom-call | tf_op jit(solution)/shard_map/pallas_call | solution.py:179
  12.6 7.5 %all-to-all-start = ((f32[16,32,128]{2,1,0:T(8,128)}), f32[16,32,128]{2,1,0:T(8,128)S(1)}, u32[]{:S(2)}, u32[]{:S(2)}) async-start(f32[16,32,128]{2,1,0:T(8,128)} %shard_map.68), calls=%async_computation | async-start | bytes 524288 | tf_op jit(solution)/shard_map/all_to_all | solution.py:211
  20.1 0.0 copy-start.5
  20.1 0.1 fusion
  20.2 10.0 %all-to-all-done.rec_ref = f32[16,32,128]{2,1,0:T(8,128)S(1)} async-done(((f32[16,32,128]{2,1,0:T(8,128)}), f32[16,32,128]{2,1,0:T(8,128)S(1)}, u32[]{:S(2)}, u32[]{:S(2)}) %all-to-all-start) | async-done | bytes 262176 | tf_op jit(solution)/shard_map/all_to_all | solution.py:211
  30.2 1.4 %shard_map.69 = (f32[18,32,256]{2,1,0:T(8,128)S(1)}, f32[5,32,256]{2,1,0:T(8,128)S(1)}, f32[5,32,256]{2,1,0:T(8,128)S(1)}) custom-call(f32[16,32,128]{2,1,0:T(8,128)S(1)} %all-to-all-done.rec_ref, s32[16,128]{1,0:T(8,128)S(1)} %bitcast.5), custom_call_target="tpu_custom_call" | custom-call | tf_op jit(solution)/shard_map/pallas_call | solution.py:183
  31.6 0.1 collective-permute-start
  31.7 4.4 %collective-permute-start.1 = (f32[5,32,256]{2,1,0:T(8,128)S(1)}, f32[5,32,256]{2,1,0:T(8,128)S(1)}, u32[]{:S(2)}, u32[]{:S(2)}) collective-permute-start(f32[5,32,256]{2,1,0:T(8,128)S(1)} %get-tuple-element.9), channel_id=1, source_target_pairs={{1,0},{2,1},{3,2},{4,3},{5,4},{6,5},{7,6},{8,7},{9,8},{10,9},{11,1... | collective-permute-start | bytes 491528 | tf_op jit(solution)/shard_map/ppermute | solution.py:192
  36.1 0.1 pad_maximum_fusion.3
  36.2 0.0 collective-permute-start.2
  36.2 4.4 %collective-permute-start.3 = (f32[5,256]{1,0:T(8,128)S(1)}, f32[5,256]{1,0:T(8,128)S(1)}, u32[]{:S(2)}, u32[]{:S(2)}) collective-permute-start(f32[5,256]{1,0:T(8,128)S(1)} %get-tuple-element.13), channel_id=1, source_target_pairs={{1,0},{2,1},{3,2},{4,3},{5,4},{6,5},{7,6},{8,7},{9,8},{10,9},{11,1... | collective-permute-start | bytes 15368 | tf_op jit(solution)/shard_map/ppermute | solution.py:176
  40.6 1.3 %collective-permute-done.2 = f32[5,256]{1,0:T(8,128)S(1)} collective-permute-done((f32[5,256]{1,0:T(8,128)S(1)}, f32[5,256]{1,0:T(8,128)S(1)}, u32[]{:S(2)}, u32[]{:S(2)}) %collective-permute-start.2) | collective-permute-done | bytes 5152 | tf_op jit(solution)/shard_map/ppermute | solution.py:176
  41.9 0.0 collective-permute-done.3
  42.0 0.1 pad_maximum_fusion.coef_ref
  42.1 0.0 collective-permute-done.before_ref
  42.1 0.0 collective-permute-done.1.after_ref
  42.1 3.3 %shard_map.70 = (f32[18,32,192]{2,1,0:T(8,128)}, f32[16,32,128]{2,1,0:T(8,128)S(1)}) custom-call(f32[18,32,256]{2,1,0:T(8,128)S(1)} %get-tuple-element.7.coarse_ref, f32[5,32,256]{2,1,0:T(8,128)S(1)} %collective-permute-done.before_ref, f32[5,32,256]{2,1,0:T(8,128)S(1)} %collective-permute-done.1.after_ref, f32[28,256]{1,0:T(8,128)S(1)} %pad_maximum_fusion.coef_ref, ...), custom_call_target="tpu_custom_call" | custom-call | tf_op jit(solution)/shard_map/pallas_call | solution.py:194
  45.4 0.0 copy-start.2
  45.4 0.0 copy-start.4
  45.4 15.8 %all_to_all.10.ret_ref = f32[16,32,128]{2,1,0:T(8,128)S(1)} all-to-all(f32[16,32,128]{2,1,0:T(8,128)S(1)} %get-tuple-element.10), channel_id=1, replica_groups=mesh['group'=2,'tile'=16] {'tile'}, dimensions={0} | all-to-all | bytes 524288 | tf_op jit(solution)/shard_map/all_to_all | solution.py:211
  61.2 12.1 %shard_map.71 = f32[32,6912]{1,0:T(8,128)} custom-call(f32[16,32,128]{2,1,0:T(8,128)S(1)} %all_to_all.10.ret_ref, s32[4,6912]{1,0:T(4,128)S(1)} %bitcast.4, f32[4,6912]{1,0:T(4,128)S(1)} %copy-done.4), custom_call_target="tpu_custom_call" | custom-call | tf_op jit(solution)/shard_map/pallas_call | solution.py:200
  (8 shorter events, 0.0 us)
Async XLA Ops:
  0.6 1.2 %copy-start = (f32[32,6912]{1,0:T(8,128)S(1)}, f32[32,6912]{1,0:T(8,128)}, u32[]{:S(2)}) copy-start(f32[32,6912]{1,0:T(8,128)} %inc_ref.1) | copy-start | bytes 2654212
  1.8 0.9 %copy-start.1 = (s32[6912,4]{0,1:T(4,128)S(1)}, s32[6912,4]{0,1:T(4,128)}, u32[]{:S(2)}) copy-start(s32[6912,4]{0,1:T(4,128)} %param.6) | copy-start | bytes 331780
  2.7 0.9 %copy-start.3 = (f32[4,6912]{1,0:T(4,128)S(1)}, f32[4,6912]{1,0:T(4,128)}, u32[]{:S(2)}) copy-start(f32[4,6912]{1,0:T(4,128)} %weight_ref.3) | copy-start | bytes 331780
  12.6 7.5 %copy-start.6 = (f32[18,192]{1,0:T(8,128)S(1)}, f32[18,192]{1,0:T(8,128)}, u32[]{:S(2)}) copy-start(f32[18,192]{1,0:T(8,128)} %param.9) | copy-start | bytes 41476
  12.6 17.5 %all-to-all-start = ((f32[16,32,128]{2,1,0:T(8,128)}), f32[16,32,128]{2,1,0:T(8,128)S(1)}, u32[]{:S(2)}, u32[]{:S(2)}) async-start(f32[16,32,128]{2,1,0:T(8,128)} %shard_map.68), calls=%async_computation | async-start | bytes 524288 | tf_op jit(solution)/shard_map/all_to_all | solution.py:211
  20.1 10.0 %copy-start.5 = (s32[2048]{0:T(1024)S(1)}, s32[2048]{0:T(1024)}, u32[]{:S(2)}) copy-start(s32[2048]{0:T(1024)} %param.8) | copy-start | bytes 24580
  31.6 10.5 %collective-permute-start = (f32[5,32,256]{2,1,0:T(8,128)S(1)}, f32[5,32,256]{2,1,0:T(8,128)S(1)}, u32[]{:S(2)}, u32[]{:S(2)}) collective-permute-start(f32[5,32,256]{2,1,0:T(8,128)S(1)} %get-tuple-element.8), channel_id=1, source_target_pairs={{0,1},{1,2},{2,3},{3,4},{4,5},{5,6},{6,7},{7,8},{8,9},{9,10},{10,1... | collective-permute-start | bytes 491528 | tf_op jit(solution)/shard_map/ppermute | solution.py:191
  31.7 10.4 %collective-permute-start.1 = (f32[5,32,256]{2,1,0:T(8,128)S(1)}, f32[5,32,256]{2,1,0:T(8,128)S(1)}, u32[]{:S(2)}, u32[]{:S(2)}) collective-permute-start(f32[5,32,256]{2,1,0:T(8,128)S(1)} %get-tuple-element.9), channel_id=1, source_target_pairs={{1,0},{2,1},{3,2},{4,3},{5,4},{6,5},{7,6},{8,7},{9,8},{10,9},{11,1... | collective-permute-start | bytes 491528 | tf_op jit(solution)/shard_map/ppermute | solution.py:192
  36.2 5.8 %collective-permute-start.2 = (f32[5,256]{1,0:T(8,128)S(1)}, f32[5,256]{1,0:T(8,128)S(1)}, u32[]{:S(2)}, u32[]{:S(2)}) collective-permute-start(f32[5,256]{1,0:T(8,128)S(1)} %get-tuple-element.12), channel_id=1, source_target_pairs={{0,1},{1,2},{2,3},{3,4},{4,5},{5,6},{6,7},{7,8},{8,9},{9,10},{10,1... | collective-permute-start | bytes 15368 | tf_op jit(solution)/shard_map/ppermute | solution.py:176
  36.2 5.8 %collective-permute-start.3 = (f32[5,256]{1,0:T(8,128)S(1)}, f32[5,256]{1,0:T(8,128)S(1)}, u32[]{:S(2)}, u32[]{:S(2)}) collective-permute-start(f32[5,256]{1,0:T(8,128)S(1)} %get-tuple-element.13), channel_id=1, source_target_pairs={{1,0},{2,1},{3,2},{4,3},{5,4},{6,5},{7,6},{8,7},{9,8},{10,9},{11,1... | collective-permute-start | bytes 15368 | tf_op jit(solution)/shard_map/ppermute | solution.py:176
  45.4 15.8 %copy-start.2 = (s32[6912,4]{0,1:T(4,128)S(1)}, s32[6912,4]{0,1:T(4,128)}, u32[]{:S(2)}) copy-start(s32[6912,4]{0,1:T(4,128)} %param.6) | copy-start | bytes 331780
  45.4 15.8 %copy-start.4 = (f32[4,6912]{1,0:T(4,128)S(1)}, f32[4,6912]{1,0:T(4,128)}, u32[]{:S(2)}) copy-start(f32[4,6912]{1,0:T(4,128)} %weight_ref.3) | copy-start | bytes 331780

commit v2 on v1

v2 whole, which is shorter than its diff:
```python
import functools

import jax
import jax.numpy as jnp
from jax import lax
from jax.experimental import pallas as pl
from jax.experimental.pallas import tpu as pltpu
from jax.sharding import PartitionSpec as P

STEPS = 5
CORNERS = 4
LANES = 128
PLACES = 256
EDGE = STEPS + (STEPS + 1) // 2
BF16 = jnp.bfloat16
F32 = jnp.float32
VMEM = pl.BlockSpec(memory_space=pltpu.VMEM)


def halves(values):
    high = values.astype(BF16)
    return high, (values - high.astype(F32)).astype(BF16)


def one_hot(places, length):
    rows = lax.broadcasted_iota(jnp.int32, (length, places.shape[1]), 0)
    return jnp.where(rows == places, 1.0, 0.0).astype(BF16)


def masked(values, marks, count):
    marks = jnp.broadcast_to(marks, values.shape)
    zero = jnp.zeros((), values.dtype)
    return jnp.concatenate([jnp.where(marks == k, values, zero) for k in range(count)], 0)


def dot_last(left, right):
    return lax.dot_general(left, right, (((1,), (1,)), ((), ())), preferred_element_type=F32)


def sum_to_slots(inc_ref, slot_ref, weight_ref, sent_ref):
    channels = inc_ref.shape[0]
    count = sent_ref.shape[0] * LANES // PLACES
    inc = inc_ref[...]
    left, right = [], []
    for corner in range(CORNERS):
        slots = slot_ref[corner : corner + 1, :]
        parts = jnp.concatenate(halves(weight_ref[corner : corner + 1, :] * inc), 0)
        left.append(masked(parts, slots // PLACES, count))
        right.append(one_hot(slots % PLACES, PLACES))
    sums = dot_last(jnp.concatenate(left, 1), jnp.concatenate(right, 1))

    @pl.when(pl.program_id(0) == 0)
    def _():
        sent_ref[...] = jnp.zeros_like(sent_ref)

    for k in range(count):
        both = sums[2 * channels * k : 2 * channels * (k + 1)]
        both = both[:channels] + both[channels:]
        for part in range(PLACES // LANES):
            sent_ref[k * (PLACES // LANES) + part] += both[:, LANES * part : LANES * (part + 1)]


def wide_column(width):
    lanes = lax.broadcasted_iota(jnp.int32, (2 * LANES, 1), 0)
    extra = (2 * LANES - width) // 2
    return jnp.where(lanes < width, lanes, jnp.where(lanes < width + extra, lanes - width, lanes - 2 * LANES + width))


def place_edge(edge_ref, rows, coefs, width):
    half = width - LANES
    for k, row in enumerate(rows):
        edge_ref[k] = row[:, :LANES]
    ends = [row[:, LANES:width] for row in rows]
    for k in range(0, STEPS - 1, 2):
        edge_ref[STEPS + k // 2] = jnp.concatenate([ends[k], ends[k + 1]], 1)
    edge_ref[EDGE - 1] = jnp.concatenate([ends[-1], jnp.zeros_like(ends[-1])], 1)
    for k, coef in enumerate(coefs):
        for part in range(3):
            edge_ref[EDGE - 1, 3 * k + part : 3 * k + part + 1, half:] = coef[:, half * part : half * (part + 1)]


def read_edge(edge_ref, k, width):
    half = width - LANES
    start = edge_ref[k]
    end = edge_ref[STEPS + k // 2, :, half * (k % 2) : half * (k % 2) + half]
    return widened([start, end], start, end, width)


def read_coef(edge_ref, k, width):
    half = width - LANES
    parts = [edge_ref[EDGE - 1, 3 * k + part : 3 * k + part + 1, half:] for part in range(3)]
    return widened(parts, parts[0], parts[2], width)


def widened(parts, start, end, width):
    extra = (2 * LANES - width) // 2
    return jnp.concatenate(parts + [start[:, :extra], end[:, end.shape[1] - extra :]], 1)


def add_to_cells(rec_ref, cell_ref, coef_ref, coarse_ref, head_ref, tail_ref, *, width):
    rows, channels, wide = coarse_ref.shape
    senders = rec_ref.shape[0]
    cells = jnp.concatenate([cell_ref[s : s + 1, :] for s in range(senders)], 1)
    values = jnp.concatenate([rec_ref[s] for s in range(senders)], 1)
    y = cells // width
    right = jnp.where(wide_column(width) == cells - y * width, 1.0, 0.0).astype(BF16)
    left = masked(jnp.concatenate(halves(values), 0), y, rows)
    sums = dot_last(left, right)
    full = []
    for k in range(rows):
        both = sums[2 * channels * k : 2 * channels * (k + 1)]
        both = both[:channels] + both[channels:]
        coarse_ref[k] = both
        full.append(both)
    coefs = [coef_ref[k : k + 1, :] for k in range(rows)]
    place_edge(head_ref, full[:STEPS], coefs[:STEPS], width)
    place_edge(tail_ref, full[rows - STEPS :], coefs[rows - STEPS :], width)


def diffuse_and_read(
    coarse_ref, before_ref, after_ref, own_ref, cell_ref, field_ref, values_ref, one_ref, two_ref, coef_ref, *, width
):
    rows, channels, wide = coarse_ref.shape
    senders = values_ref.shape[0]
    total = rows + 2 * STEPS
    own = own_ref[...]
    coef_ref[STEPS : STEPS + rows, :] = widened([own], own, own, width)
    one_ref[STEPS : STEPS + rows] = coarse_ref[...]
    for k in range(STEPS):
        one_ref[k] = read_edge(before_ref, k, width)
        one_ref[STEPS + rows + k] = read_edge(after_ref, k, width)
        coef_ref[k : k + 1, :] = read_coef(before_ref, k, width)
        coef_ref[STEPS + rows + k : STEPS + rows + k + 1, :] = read_coef(after_ref, k, width)
    held, other = one_ref, two_ref
    for turn in range(1, STEPS + 1):
        for y in range(turn, total - turn):
            here = held[y]
            spread = held[y + 1] + held[y - 1] + pltpu.roll(here, 1, 1) + pltpu.roll(here, wide - 1, 1)
            other[y] = here + coef_ref[y : y + 1, :] * (spread - 4.0 * here)
        held, other = other, held
    final = held[STEPS : STEPS + rows]
    field_ref[...] = final[:, :, :width]
    left = jnp.concatenate(halves(final.reshape(rows * channels, wide)), 1)
    for s in range(0, senders, 2):
        cells = jnp.concatenate([cell_ref[s : s + 1, :], cell_ref[s + 1 : s + 2, :]], 1)
        y = cells // width
        right = one_hot(cells - y * width, wide)
        found = jnp.dot(left, jnp.concatenate([right, right], 0), preferred_element_type=F32)
        out = jnp.zeros((channels, 2 * LANES), F32)
        marks = jnp.broadcast_to(y, out.shape)
        for k in range(rows):
            out = jnp.where(marks == k, found[channels * k : channels * (k + 1)], out)
        values_ref[s] = out[:, :LANES]
        values_ref[s + 1] = out[:, LANES:]


def by_product(table_ref, slot_ref, weight_ref, columns, channels):
    count = table_ref.shape[0] // (2 * channels)
    total = 0.0
    for corner in range(CORNERS):
        slots = slot_ref[corner : corner + 1, columns]
        found = jnp.dot(table_ref[...], one_hot(slots % PLACES, PLACES), preferred_element_type=F32)
        marks = jnp.broadcast_to(slots // PLACES, (channels, slots.shape[1]))
        out = None
        for k in range(count):
            both = found[2 * channels * k : 2 * channels * (k + 1)]
            both = both[:channels] + both[channels:]
            out = both if out is None else jnp.where(marks == k, both, out)
        total = total + weight_ref[corner : corner + 1, columns] * out
    return total


def by_lanes(ret_ref, slot_ref, weight_ref, columns):
    blocks, channels, _ = ret_ref.shape
    group = 8
    totals = [0.0] * (channels // group)
    for corner in range(CORNERS):
        slots = slot_ref[corner : corner + 1, columns]
        weight = weight_ref[corner : corner + 1, columns]
        lanes = jnp.broadcast_to(slots % LANES, (group, LANES))
        block = jnp.broadcast_to(slots // LANES, (group, LANES))
        marks = [block == k for k in range(blocks)]
        for c in range(channels // group):
            out = None
            for k in range(blocks):
                found = jnp.take_along_axis(ret_ref[k, group * c : group * (c + 1), :], lanes, axis=1)
                out = found if out is None else jnp.where(marks[k], found, out)
            totals[c] = totals[c] + weight * out
    return jnp.concatenate(totals, 0)


def sum_from_slots(ret_ref, slot_ref, weight_ref, result_ref, table_ref, *, plan):
    blocks, channels, _ = ret_ref.shape
    group = PLACES // LANES

    @pl.when(pl.program_id(0) == 0)
    def _():
        for k in range(blocks // group):
            both = halves(jnp.concatenate([ret_ref[group * k + part] for part in range(group)], 1))
            table_ref[2 * channels * k : 2 * channels * (k + 1), :] = jnp.concatenate(both, 0)

    at = 0
    for product, single in plan:
        columns = slice(at, at + product * LANES)
        result_ref[:, columns] = by_product(table_ref, slot_ref, weight_ref, columns, channels)
        for k in range(product, product + single):
            columns = slice(at + k * LANES, at + (k + 1) * LANES)
            result_ref[:, columns] = by_lanes(ret_ref, slot_ref, weight_ref, columns)
        at += (product + single) * LANES


def plan_of(blocks):
    turns = max(t for t in (3, 2, 1) if blocks % t == 0)
    size = blocks // turns
    return [(size - size // 3, size // 3)] * turns


def chunk_of(fine, most):
    return max(c for c in range(LANES, most + 1, LANES) if fine % c == 0)


def call(kernel, ins, out, scratch=(), grid=(), in_specs=VMEM, out_specs=VMEM):
    single = isinstance(in_specs, pl.BlockSpec)
    return pl.pallas_call(
        kernel,
        grid=grid,
        out_shape=out,
        in_specs=[in_specs] * len(ins) if single else in_specs,
        out_specs=[out_specs] * len(out) if isinstance(out, list) else out_specs,
        scratch_shapes=list(scratch),
        compiler_params=pltpu.CompilerParams(vmem_limit_bytes=56 << 20),
    )(*ins)


def body(increment, send_slots, tent_weight, coarse_cell, diffusivity):
    channels, fine = increment.shape
    slot_count = coarse_cell.shape[0]
    rows, width = diffusivity.shape
    tiles = lax.axis_size("tile")
    share = slot_count // tiles
    blocks = slot_count // LANES
    wide = 2 * LANES
    ahead = [(i, (i + 1) % tiles) for i in range(tiles)]
    back = [((i + 1) % tiles, i) for i in range(tiles)]
    shape = jax.ShapeDtypeStruct
    slots = send_slots.T
    cells = coarse_cell.reshape(blocks, LANES)
    chunk = chunk_of(fine, 2304)
    grid = (fine // chunk,)
    part = lambda n: pl.BlockSpec((n, chunk), lambda i: (0, i))
    whole = pl.BlockSpec((blocks, channels, LANES), lambda i: (0, 0, 0))

    sent = call(
        sum_to_slots,
        (increment, slots, tent_weight),
        shape((blocks, channels, LANES), F32),
        grid=grid,
        in_specs=[part(channels), part(CORNERS), part(CORNERS)],
        out_specs=whole,
    )
    received = exchange(sent, tiles, share)
    edge = shape((EDGE, channels, LANES), F32)
    coarse, head, tail = call(
        functools.partial(add_to_cells, width=width),
        (received, cells, diffusivity),
        [shape((rows, channels, wide), F32), edge, edge],
    )
    before = lax.ppermute(tail, "tile", ahead)
    after = lax.ppermute(head, "tile", back)
    padded = pltpu.VMEM((rows + 2 * STEPS, channels, wide), F32)
    field, values = call(
        functools.partial(diffuse_and_read, width=width),
        (coarse, before, after, diffusivity, cells),
        [shape((rows, channels, width), F32), shape((blocks, channels, LANES), F32)],
        [padded, padded, pltpu.VMEM((rows + 2 * STEPS, wide), F32)],
    )
    returned = exchange(values, tiles, share)
    result = call(
        functools.partial(sum_from_slots, plan=plan_of(chunk // LANES)),
        (returned, slots, tent_weight),
        shape((channels, fine), F32),
        [pltpu.VMEM((2 * channels * slot_count // PLACES, PLACES), BF16)],
        grid=grid,
        in_specs=[whole, part(CORNERS), part(CORNERS)],
        out_specs=part(channels),
    )
    return (result, field.transpose(1, 0, 2))


def exchange(blocks, tiles, share):
    count, channels, lanes = blocks.shape
    if share == lanes:
        return lax.all_to_all(blocks, "tile", split_axis=0, concat_axis=0, tiled=True)
    flat = blocks.transpose(1, 0, 2).reshape(channels, count * lanes)
    flat = lax.all_to_all(flat, "tile", split_axis=1, concat_axis=1, tiled=True)
    return flat.reshape(channels, count, lanes).transpose(1, 0, 2)


def solution(mesh):
    in_specs = (
        P(None, ("group", "tile")),
        P("tile", None),
        P(None, "tile"),
        P("tile"),
        P("tile", None),
    )
    out_specs = (P(None, ("group", "tile")), P(None, ("group", "tile"), None))
    return jax.shard_map(body, mesh=mesh, in_specs=in_specs, out_specs=out_specs, check_vma=False)
```

time: 73.7 us -> 68.9 us (0.935)
  blocking collectives: 15.8 us -> 33.4 us
  starting transfers between devices: 16.4 us -> 4.44 us
  waiting for transfers between devices: 11.3 us -> 2.86 us
  local copies, waits for them, and re-layouts: 3.05 us -> 0.69 us
    all_to_all x1 -> x2, blocking collectives: 15.8 us -> 33.4 us  [exchange(): lax.all_to_all(blocks, 'tile', split_axis=0, concat_axis=0, tiled=True)]
    all_to_all x1 -> x0, waiting for transfers between devices: 9.95 us -> none  [exchange(): lax.all_to_all(blocks, 'tile', split_axis=0, concat_axis=0, tiled=True)]
    all_to_all x1 -> x0, starting transfers between devices: 7.49 us -> none  [exchange(): lax.all_to_all(blocks, 'tile', split_axis=0, concat_axis=0, tiled=True)]
    ppermute x2 -> x0, starting transfers between devices: 4.44 us -> none  [the longest x1 4.44 us: body(): lax.ppermute(coef[:STEPS], 'tile', back)]
    ppermute x1, waiting for transfers between devices: 0.01 us -> 2.86 us  [body(): before = lax.ppermute(tail, 'tile', ahead)]
    unnamed x14 -> x4, local copies, waits for them, and re-layouts: 2.98 us -> 0.69 us
    ppermute x2 -> x0, waiting for transfers between devices: 1.37 us -> none  [the longest x1 1.33 us: body(): lax.ppermute(coef[rows - STEPS:], 'tile', ahead)]
  transfers between devices with their start and end apart: 5 -> 2, of which waited for: 2 -> 1; matrix products, arithmetic and copies ran while one was open for 0% -> 0% of each run, Pallas kernels for 0% -> 0%
where the time goes in v2:
time: 68.9 us; the launch traced here: 68.5 us
  blocking collectives  33.4 us (48%)
  Pallas kernels  26.4 us (38%)
  starting transfers between devices  4.44 us (6%)
  waiting for transfers between devices  2.86 us (4%)
  local copies, waits for them, and re-layouts  0.69 us (1%)
    all_to_all x2, blocking collectives, exchange(): lax.all_to_all(blocks, 'tile', split_axis=0, concat_axis=0, tiled=True)  33.4 us
    pallas_call x4, Pallas kernels, call(): pl.pallas_call(kernel, grid=grid, out_shape=out, in_specs=[in_specs] * le...  26.4 us
    ppermute x1, starting transfers between devices, body(): after = lax.ppermute(head, 'tile', back)  4.44 us
    ppermute x1, waiting for transfers between devices, body(): before = lax.ppermute(tail, 'tile', ahead)  2.86 us
  transfers between devices with their start and end apart: 2, of which 1 were waited for; matrix products, arithmetic and copies ran while one was open for 0% of the time, Pallas kernels for 0%

profile of v2, /device:TPU:0, one launch (start us, length us, event | category | flops | bytes accessed | tf_op | source)
XLA Modules:
  0.0 68.5 jit_solution(7895392650053225831)
XLA Ops:
  0.6 10.1 %shard_map.68 = f32[16,32,128]{2,1,0:T(8,128)} custom-call(f32[32,6912]{1,0:T(8,128)} %inc_ref.1, s32[4,6912]{1,0:T(4,128)} %bitcast.3, f32[4,6912]{1,0:T(4,128)} %weight_ref.3), custom_call_target="tpu_custom_call" | custom-call | tf_op jit(solution)/shard_map/pallas_call | solution.py:224
  10.8 17.5 %all_to_all.10.rec_ref = f32[16,32,128]{2,1,0:T(8,128)} all-to-all(f32[16,32,128]{2,1,0:T(8,128)} %shard_map.68), channel_id=1, replica_groups=mesh['group'=2,'tile'=16] {'tile'}, dimensions={0} | all-to-all | bytes 524288 | tf_op jit(solution)/shard_map/all_to_all | solution.py:293
  28.3 3.2 %shard_map.69 = (f32[18,32,256]{2,1,0:T(8,128)}, f32[8,32,128]{2,1,0:T(8,128)}, f32[8,32,128]{2,1,0:T(8,128)}) custom-call(f32[16,32,128]{2,1,0:T(8,128)} %all_to_all.10.rec_ref, s32[16,128]{1,0:T(8,128)} %bitcast.5, f32[18,192]{1,0:T(8,128)} %own_ref.1), custom_call_target="tpu_custom_call" | custom-call | tf_op jit(solution)/shard_map/pallas_call | solution.py:224
  31.5 0.0 collective-permute-start
  31.5 4.4 %collective-permute-start.1 = (f32[8,32,128]{2,1,0:T(8,128)}, f32[8,32,128]{2,1,0:T(8,128)S(1)}, u32[]{:S(2)}, u32[]{:S(2)}) collective-permute-start(f32[8,32,128]{2,1,0:T(8,128)} %get-tuple-element.9), channel_id=1, source_target_pairs={{1,0},{2,1},{3,2},{4,3},{5,4},{6,5},{7,6},{8,7},{9,8},{10,9},{11,1... | collective-permute-start | bytes 393224 | tf_op jit(solution)/shard_map/ppermute | solution.py:269
  36.0 2.9 %collective-permute-done.before_ref = f32[8,32,128]{2,1,0:T(8,128)S(1)} collective-permute-done((f32[8,32,128]{2,1,0:T(8,128)}, f32[8,32,128]{2,1,0:T(8,128)S(1)}, u32[]{:S(2)}, u32[]{:S(2)}) %collective-permute-start) | collective-permute-done | bytes 131104 | tf_op jit(solution)/shard_map/ppermute | solution.py:268
  38.8 0.0 copy-start
  38.8 0.0 collective-permute-done.1.after_ref
  38.8 0.0 copy-start.1
  38.8 0.6 copy-done
  39.5 0.1 copy-done.1
  39.5 5.3 %shard_map.70 = (f32[18,32,192]{2,1,0:T(8,128)}, f32[16,32,128]{2,1,0:T(8,128)}) custom-call(f32[18,32,256]{2,1,0:T(8,128)} %get-tuple-element.7.coarse_ref, f32[8,32,128]{2,1,0:T(8,128)} %copy-done, f32[8,32,128]{2,1,0:T(8,128)} %copy-done.1, f32[18,192]{1,0:T(8,128)} %own_ref.1, s32[16,128]{1,0:T(8,128)} %bitcast.6), custom_call_target="tpu_custom_call" | custom-call | tf_op jit(solution)/shard_map/pallas_call | solution.py:224
  44.8 15.9 %all_to_all.11.ret_ref = f32[16,32,128]{2,1,0:T(8,128)} all-to-all(f32[16,32,128]{2,1,0:T(8,128)} %get-tuple-element.10), channel_id=1, replica_groups=mesh['group'=2,'tile'=16] {'tile'}, dimensions={0} | all-to-all | bytes 524288 | tf_op jit(solution)/shard_map/all_to_all | solution.py:293
  60.7 7.8 %shard_map.71 = f32[32,6912]{1,0:T(8,128)} custom-call(f32[16,32,128]{2,1,0:T(8,128)} %all_to_all.11.ret_ref, s32[4,6912]{1,0:T(4,128)} %bitcast.4, f32[4,6912]{1,0:T(4,128)} %weight_ref.3), custom_call_target="tpu_custom_call" | custom-call | tf_op jit(solution)/shard_map/pallas_call | solution.py:224
Async XLA Ops:
  31.5 7.3 %collective-permute-start = (f32[8,32,128]{2,1,0:T(8,128)}, f32[8,32,128]{2,1,0:T(8,128)S(1)}, u32[]{:S(2)}, u32[]{:S(2)}) collective-permute-start(f32[8,32,128]{2,1,0:T(8,128)} %get-tuple-element.8), channel_id=1, source_target_pairs={{0,1},{1,2},{2,3},{3,4},{4,5},{5,6},{6,7},{7,8},{8,9},{9,10},{10,1... | collective-permute-start | bytes 393224 | tf_op jit(solution)/shard_map/ppermute | solution.py:268
  31.5 7.3 %collective-permute-start.1 = (f32[8,32,128]{2,1,0:T(8,128)}, f32[8,32,128]{2,1,0:T(8,128)S(1)}, u32[]{:S(2)}, u32[]{:S(2)}) collective-permute-start(f32[8,32,128]{2,1,0:T(8,128)} %get-tuple-element.9), channel_id=1, source_target_pairs={{1,0},{2,1},{3,2},{4,3},{5,4},{6,5},{7,6},{8,7},{9,8},{10,9},{11,1... | collective-permute-start | bytes 393224 | tf_op jit(solution)/shard_map/ppermute | solution.py:269
  38.8 0.6 copy-start
  38.8 0.7 %copy-start.1 = (f32[8,32,128]{2,1,0:T(8,128)}, f32[8,32,128]{2,1,0:T(8,128)S(1)}, u32[]{:S(2)}) copy-start(f32[8,32,128]{2,1,0:T(8,128)S(1)} %collective-permute-done.1.after_ref) | copy-start | bytes 393220

commit v3 on v2

--- a/solution.py
+++ b/solution.py
@@ -219,7 +219,7 @@
     return max(c for c in range(LANES, most + 1, LANES) if fine % c == 0)
 
 
-def call(kernel, ins, out, scratch=(), grid=(), in_specs=VMEM, out_specs=VMEM):
+def call(kernel, ins, out, scratch=(), grid=(), in_specs=VMEM, out_specs=VMEM, memory=16):
     single = isinstance(in_specs, pl.BlockSpec)
     return pl.pallas_call(
         kernel,
@@ -228,7 +228,7 @@
         in_specs=[in_specs] * len(ins) if single else in_specs,
         out_specs=[out_specs] * len(out) if isinstance(out, list) else out_specs,
         scratch_shapes=list(scratch),
-        compiler_params=pltpu.CompilerParams(vmem_limit_bytes=56 << 20),
+        compiler_params=pltpu.CompilerParams(vmem_limit_bytes=memory << 20),
     )(*ins)
 
 
@@ -257,6 +257,7 @@
         grid=grid,
         in_specs=[part(channels), part(CORNERS), part(CORNERS)],
         out_specs=whole,
+        memory=56,
     )
     received = exchange(sent, tiles, share)
     edge = shape((EDGE, channels, LANES), F32)
@@ -283,6 +284,7 @@
         grid=grid,
         in_specs=[whole, part(CORNERS), part(CORNERS)],
         out_specs=part(channels),
+        memory=32,
     )
     return (result, field.transpose(1, 0, 2))
 

time: 68.9 us -> 63.3 us (0.919)
  Pallas kernels: 26.4 us -> 21.8 us
    pallas_call x4, Pallas kernels: 26.4 us -> 21.8 us  [call(): pl.pallas_call(kernel, grid=grid, out_shape=out, in_specs=[in_specs] * le...]
where the time goes in v3:
time: 63.3 us; the launch traced here: 63 us
  blocking collectives  33.3 us (53%)
  Pallas kernels  21.8 us (34%)
  starting transfers between devices  4.47 us (7%)
  waiting for transfers between devices  2.65 us (4%)
  between operations  0.67 us (1%)
    all_to_all x2, blocking collectives, exchange(): lax.all_to_all(blocks, 'tile', split_axis=0, concat_axis=0, tiled=True)  33.3 us
    pallas_call x4, Pallas kernels, call(): pl.pallas_call(kernel, grid=grid, out_shape=out, in_specs=[in_specs] * le...  21.8 us
    ppermute x1, starting transfers between devices, body(): after = lax.ppermute(head, 'tile', back)  4.43 us
    ppermute x1, waiting for transfers between devices, body(): before = lax.ppermute(tail, 'tile', ahead)  2.65 us
  transfers between devices with their start and end apart: 2, of which 1 were waited for; matrix products, arithmetic and copies ran while one was open for 0% of the time, Pallas kernels for 0%

profile of v3, /device:TPU:0, one launch (start us, length us, event | category | flops | bytes accessed | tf_op | source)
XLA Modules:
  0.0 63.0 jit_solution(7875240904565467002)
XLA Ops:
  0.6 10.1 %shard_map.68 = f32[16,32,128]{2,1,0:T(8,128)} custom-call(f32[32,6912]{1,0:T(8,128)} %inc_ref.1, s32[4,6912]{1,0:T(4,128)} %bitcast.3, f32[4,6912]{1,0:T(4,128)} %weight_ref.3), custom_call_target="tpu_custom_call" | custom-call | tf_op jit(solution)/shard_map/pallas_call | solution.py:224
  10.8 0.0 copy-start.2
  10.8 0.0 copy-start.3
  10.8 17.5 %all_to_all.10.rec_ref = f32[16,32,128]{2,1,0:T(8,128)S(1)} all-to-all(f32[16,32,128]{2,1,0:T(8,128)} %shard_map.68), channel_id=1, replica_groups=mesh['group'=2,'tile'=16] {'tile'}, dimensions={0} | all-to-all | bytes 524288 | tf_op jit(solution)/shard_map/all_to_all | solution.py:295
  28.3 0.0 copy-done.2
  28.3 0.0 copy-done.3
  28.3 1.5 %shard_map.69 = (f32[18,32,256]{2,1,0:T(8,128)S(1)}, f32[8,32,128]{2,1,0:T(8,128)S(1)}, f32[8,32,128]{2,1,0:T(8,128)S(1)}) custom-call(f32[16,32,128]{2,1,0:T(8,128)S(1)} %all_to_all.10.rec_ref, s32[16,128]{1,0:T(8,128)S(1)} %bitcast.5, f32[18,192]{1,0:T(8,128)S(1)} %copy-done.2), custom_call_target="tpu_custom_call" | custom-call | tf_op jit(solution)/shard_map/pallas_call | solution.py:224
  29.8 0.0 collective-permute-start
  29.8 4.4 %collective-permute-start.1 = (f32[8,32,128]{2,1,0:T(8,128)S(1)}, f32[8,32,128]{2,1,0:T(8,128)S(1)}, u32[]{:S(2)}, u32[]{:S(2)}) collective-permute-start(f32[8,32,128]{2,1,0:T(8,128)S(1)} %get-tuple-element.9), channel_id=1, source_target_pairs={{1,0},{2,1},{3,2},{4,3},{5,4},{6,5},{7,6},{8,7},{9,8},{10,9},{11,1... | collective-permute-start | bytes 393224 | tf_op jit(solution)/shard_map/ppermute | solution.py:270
  34.3 2.6 %collective-permute-done.before_ref = f32[8,32,128]{2,1,0:T(8,128)S(1)} collective-permute-done((f32[8,32,128]{2,1,0:T(8,128)S(1)}, f32[8,32,128]{2,1,0:T(8,128)S(1)}, u32[]{:S(2)}, u32[]{:S(2)}) %collective-permute-start) | collective-permute-done | bytes 131104 | tf_op jit(solution)/shard_map/ppermute | solution.py:269
  36.9 0.0 collective-permute-done.1.after_ref
  36.9 3.4 %shard_map.70 = (f32[18,32,192]{2,1,0:T(8,128)}, f32[16,32,128]{2,1,0:T(8,128)S(1)}) custom-call(f32[18,32,256]{2,1,0:T(8,128)S(1)} %get-tuple-element.7.coarse_ref, f32[8,32,128]{2,1,0:T(8,128)S(1)} %collective-permute-done.before_ref, f32[8,32,128]{2,1,0:T(8,128)S(1)} %collective-permute-done.1.after_ref, f32[18,192]{1,0:T(8,128)S(1)} %copy-done.2, ...), custom_call_target="tpu_custom_call" | custom-call | tf_op jit(solution)/shard_map/pallas_call | solution.py:224
  40.3 0.0 copy-start
  40.3 0.0 copy-start.1
  40.3 15.8 %all_to_all.11.ret_ref = f32[16,32,128]{2,1,0:T(8,128)S(1)} all-to-all(f32[16,32,128]{2,1,0:T(8,128)S(1)} %get-tuple-element.10), channel_id=1, replica_groups=mesh['group'=2,'tile'=16] {'tile'}, dimensions={0} | all-to-all | bytes 524288 | tf_op jit(solution)/shard_map/all_to_all | solution.py:295
  56.1 0.0 copy-done
  56.1 0.0 copy-done.1
  56.1 6.8 %shard_map.71 = f32[32,6912]{1,0:T(8,128)} custom-call(f32[16,32,128]{2,1,0:T(8,128)S(1)} %all_to_all.11.ret_ref, s32[4,6912]{1,0:T(4,128)S(1)} %bitcast.4, f32[4,6912]{1,0:T(4,128)S(1)} %copy-done.1), custom_call_target="tpu_custom_call" | custom-call | tf_op jit(solution)/shard_map/pallas_call | solution.py:224
Async XLA Ops:
  10.8 17.5 %copy-start.2 = (f32[18,192]{1,0:T(8,128)S(1)}, f32[18,192]{1,0:T(8,128)}, u32[]{:S(2)}) copy-start(f32[18,192]{1,0:T(8,128)} %own_ref.1) | copy-start | bytes 41476
  10.8 17.5 %copy-start.3 = (s32[2048]{0:T(1024)S(1)}, s32[2048]{0:T(1024)}, u32[]{:S(2)}) copy-start(s32[2048]{0:T(1024)} %param.8) | copy-start | bytes 24580
  29.8 7.1 %collective-permute-start = (f32[8,32,128]{2,1,0:T(8,128)S(1)}, f32[8,32,128]{2,1,0:T(8,128)S(1)}, u32[]{:S(2)}, u32[]{:S(2)}) collective-permute-start(f32[8,32,128]{2,1,0:T(8,128)S(1)} %get-tuple-element.8), channel_id=1, source_target_pairs={{0,1},{1,2},{2,3},{3,4},{4,5},{5,6},{6,7},{7,8},{8,9},{9,10},{10,1... | collective-permute-start | bytes 393224 | tf_op jit(solution)/shard_map/ppermute | solution.py:269
  29.8 7.1 %collective-permute-start.1 = (f32[8,32,128]{2,1,0:T(8,128)S(1)}, f32[8,32,128]{2,1,0:T(8,128)S(1)}, u32[]{:S(2)}, u32[]{:S(2)}) collective-permute-start(f32[8,32,128]{2,1,0:T(8,128)S(1)} %get-tuple-element.9), channel_id=1, source_target_pairs={{1,0},{2,1},{3,2},{4,3},{5,4},{6,5},{7,6},{8,7},{9,8},{10,9},{11,1... | collective-permute-start | bytes 393224 | tf_op jit(solution)/shard_map/ppermute | solution.py:270
  40.3 15.8 %copy-start = (s32[6912,4]{0,1:T(4,128)S(1)}, s32[6912,4]{0,1:T(4,128)}, u32[]{:S(2)}) copy-start(s32[6912,4]{0,1:T(4,128)} %param.6) | copy-start | bytes 331780
  40.3 15.8 %copy-start.1 = (f32[4,6912]{1,0:T(4,128)S(1)}, f32[4,6912]{1,0:T(4,128)}, u32[]{:S(2)}) copy-start(f32[4,6912]{1,0:T(4,128)} %weight_ref.3) | copy-start | bytes 331780

commit v4 on v3

--- a/solution.py
+++ b/solution.py
@@ -97,7 +97,7 @@
     return jnp.concatenate(parts + [start[:, :extra], end[:, end.shape[1] - extra :]], 1)
 
 
-def add_to_cells(rec_ref, cell_ref, coef_ref, coarse_ref, head_ref, tail_ref, *, width):
+def add_to_cells(rec_ref, cell_ref, coef_ref, coarse_ref, near_ref, far_ref, *, width):
     rows, channels, wide = coarse_ref.shape
     senders = rec_ref.shape[0]
     cells = jnp.concatenate([cell_ref[s : s + 1, :] for s in range(senders)], 1)
@@ -113,12 +113,18 @@
         coarse_ref[k] = both
         full.append(both)
     coefs = [coef_ref[k : k + 1, :] for k in range(rows)]
-    place_edge(head_ref, full[:STEPS], coefs[:STEPS], width)
-    place_edge(tail_ref, full[rows - STEPS :], coefs[rows - STEPS :], width)
+    even = lax.axis_index("tile") % 2 == 0
+
+    def place(head_ref, tail_ref):
+        place_edge(head_ref, full[:STEPS], coefs[:STEPS], width)
+        place_edge(tail_ref, full[rows - STEPS :], coefs[rows - STEPS :], width)
+
+    pl.when(even)(lambda: place(far_ref, near_ref))
+    pl.when(jnp.logical_not(even))(lambda: place(near_ref, far_ref))
 
 
 def diffuse_and_read(
-    coarse_ref, before_ref, after_ref, own_ref, cell_ref, field_ref, values_ref, one_ref, two_ref, coef_ref, *, width
+    coarse_ref, near_ref, far_ref, own_ref, cell_ref, field_ref, values_ref, one_ref, two_ref, coef_ref, *, width
 ):
     rows, channels, wide = coarse_ref.shape
     senders = values_ref.shape[0]
@@ -126,11 +132,17 @@
     own = own_ref[...]
     coef_ref[STEPS : STEPS + rows, :] = widened([own], own, own, width)
     one_ref[STEPS : STEPS + rows] = coarse_ref[...]
-    for k in range(STEPS):
-        one_ref[k] = read_edge(before_ref, k, width)
-        one_ref[STEPS + rows + k] = read_edge(after_ref, k, width)
-        coef_ref[k : k + 1, :] = read_coef(before_ref, k, width)
-        coef_ref[STEPS + rows + k : STEPS + rows + k + 1, :] = read_coef(after_ref, k, width)
+    even = lax.axis_index("tile") % 2 == 0
+
+    def read(before_ref, after_ref):
+        for k in range(STEPS):
+            one_ref[k] = read_edge(before_ref, k, width)
+            one_ref[STEPS + rows + k] = read_edge(after_ref, k, width)
+            coef_ref[k : k + 1, :] = read_coef(before_ref, k, width)
+            coef_ref[STEPS + rows + k : STEPS + rows + k + 1, :] = read_coef(after_ref, k, width)
+
+    pl.when(even)(lambda: read(far_ref, near_ref))
+    pl.when(jnp.logical_not(even))(lambda: read(near_ref, far_ref))
     held, other = one_ref, two_ref
     for turn in range(1, STEPS + 1):
         for y in range(turn, total - turn):
@@ -240,8 +252,8 @@
     share = slot_count // tiles
     blocks = slot_count // LANES
     wide = 2 * LANES
-    ahead = [(i, (i + 1) % tiles) for i in range(tiles)]
-    back = [((i + 1) % tiles, i) for i in range(tiles)]
+    on_chip = [(i, i ^ 1) for i in range(tiles)]
+    off_chip = [(i, (i + 2 * (i % 2) - 1) % tiles) for i in range(tiles)]
     shape = jax.ShapeDtypeStruct
     slots = send_slots.T
     cells = coarse_cell.reshape(blocks, LANES)
@@ -261,17 +273,17 @@
     )
     received = exchange(sent, tiles, share)
     edge = shape((EDGE, channels, LANES), F32)
-    coarse, head, tail = call(
+    coarse, near, far = call(
         functools.partial(add_to_cells, width=width),
         (received, cells, diffusivity),
         [shape((rows, channels, wide), F32), edge, edge],
     )
-    before = lax.ppermute(tail, "tile", ahead)
-    after = lax.ppermute(head, "tile", back)
+    far = lax.ppermute(far, "tile", off_chip)
+    near = lax.ppermute(near, "tile", on_chip)
     padded = pltpu.VMEM((rows + 2 * STEPS, channels, wide), F32)
     field, values = call(
         functools.partial(diffuse_and_read, width=width),
-        (coarse, before, after, diffusivity, cells),
+        (coarse, near, far, diffusivity, cells),
         [shape((rows, channels, width), F32), shape((blocks, channels, LANES), F32)],
         [padded, padded, pltpu.VMEM((rows + 2 * STEPS, wide), F32)],
     )

time: 63.3 us -> 60.8 us (0.961)
  waiting for transfers between devices: 2.65 us -> 5.46 us
  blocking collectives: 33.3 us -> 30.5 us
  starting transfers between devices: 4.47 us -> 1.77 us
    ppermute x2, waiting for transfers between devices: 2.65 us -> 5.46 us  [the longest x1 5.46 us: body(): far = lax.ppermute(far, 'tile', off_chip)]
    all_to_all x2, blocking collectives: 33.3 us -> 30.5 us  [exchange(): lax.all_to_all(blocks, 'tile', split_axis=0, concat_axis=0, tiled=True)]
    ppermute x2, starting transfers between devices: 4.47 us -> 1.77 us  [the longest x1 1.69 us: body(): far = lax.ppermute(far, 'tile', off_chip)]
where the time goes in v4:
time: 60.8 us; the launch traced here: 60.4 us
  blocking collectives  30.5 us (50%)
  Pallas kernels  22 us (36%)
  waiting for transfers between devices  5.46 us (9%)
  starting transfers between devices  1.77 us (3%)
  between operations  0.67 us (1%)
    all_to_all x2, blocking collectives, exchange(): lax.all_to_all(blocks, 'tile', split_axis=0, concat_axis=0, tiled=True)  30.5 us
    pallas_call x4, Pallas kernels, call(): pl.pallas_call(kernel, grid=grid, out_shape=out, in_specs=[in_specs] * le...  22 us
    ppermute x1, waiting for transfers between devices, body(): far = lax.ppermute(far, 'tile', off_chip)  5.46 us
    ppermute x1, starting transfers between devices, body(): far = lax.ppermute(far, 'tile', off_chip)  1.69 us
  transfers between devices with their start and end apart: 2, of which 1 were waited for; matrix products, arithmetic and copies ran while one was open for 0% of the time, Pallas kernels for 0%

profile of v4, /device:TPU:0, one launch (start us, length us, event | category | flops | bytes accessed | tf_op | source)
XLA Modules:
  0.0 60.4 jit_solution(4174327047750827449)
XLA Ops:
  0.6 10.1 %shard_map.68 = f32[16,32,128]{2,1,0:T(8,128)} custom-call(f32[32,6912]{1,0:T(8,128)} %inc_ref.1, s32[4,6912]{1,0:T(4,128)} %bitcast.3, f32[4,6912]{1,0:T(4,128)} %weight_ref.3), custom_call_target="tpu_custom_call" | custom-call | tf_op jit(solution)/shard_map/pallas_call | solution.py:236
  10.8 0.0 copy-start.2
  10.8 0.0 copy-start.3
  10.8 17.5 %all_to_all.10.rec_ref = f32[16,32,128]{2,1,0:T(8,128)S(1)} all-to-all(f32[16,32,128]{2,1,0:T(8,128)} %shard_map.68), channel_id=1, replica_groups=mesh['group'=2,'tile'=16] {'tile'}, dimensions={0} | all-to-all | bytes 524288 | tf_op jit(solution)/shard_map/all_to_all | solution.py:307
  28.3 0.0 copy-done.2
  28.3 0.0 copy-done.3
  28.3 1.5 %shard_map.69 = (f32[18,32,256]{2,1,0:T(8,128)S(1)}, f32[8,32,128]{2,1,0:T(8,128)S(1)}, f32[8,32,128]{2,1,0:T(8,128)S(1)}) custom-call(f32[16,32,128]{2,1,0:T(8,128)S(1)} %all_to_all.10.rec_ref, s32[16,128]{1,0:T(8,128)S(1)} %bitcast.5, f32[18,192]{1,0:T(8,128)S(1)} %copy-done.2), custom_call_target="tpu_custom_call" | custom-call | tf_op jit(solution)/shard_map/pallas_call | solution.py:236
  29.8 0.1 collective-permute-start
  29.9 1.7 %collective-permute-start.1 = (f32[8,32,128]{2,1,0:T(8,128)S(1)}, f32[8,32,128]{2,1,0:T(8,128)S(1)}, u32[]{:S(2)}, u32[]{:S(2)}) collective-permute-start(f32[8,32,128]{2,1,0:T(8,128)S(1)} %get-tuple-element.9), channel_id=1, source_target_pairs={{0,15},{1,2},{2,1},{3,4},{4,3},{5,6},{6,5},{7,8},{8,7},{9,10},{10,... | collective-permute-start | bytes 393224 | tf_op jit(solution)/shard_map/ppermute | solution.py:281
  31.6 0.0 collective-permute-done.near_ref
  31.6 5.5 %collective-permute-done.1.far_ref = f32[8,32,128]{2,1,0:T(8,128)S(1)} collective-permute-done((f32[8,32,128]{2,1,0:T(8,128)S(1)}, f32[8,32,128]{2,1,0:T(8,128)S(1)}, u32[]{:S(2)}, u32[]{:S(2)}) %collective-permute-start.1) | collective-permute-done | bytes 131104 | tf_op jit(solution)/shard_map/ppermute | solution.py:281
  37.1 3.5 %shard_map.70 = (f32[18,32,192]{2,1,0:T(8,128)}, f32[16,32,128]{2,1,0:T(8,128)S(1)}) custom-call(f32[18,32,256]{2,1,0:T(8,128)S(1)} %get-tuple-element.7.coarse_ref, f32[8,32,128]{2,1,0:T(8,128)S(1)} %collective-permute-done.near_ref, f32[8,32,128]{2,1,0:T(8,128)S(1)} %collective-permute-done.1.far_ref, f32[18,192]{1,0:T(8,128)S(1)} %copy-done.2, ...), custom_call_target="tpu_custom_call" | custom-call | tf_op jit(solution)/shard_map/pallas_call | solution.py:236
  40.6 0.0 copy-start
  40.6 0.0 copy-start.1
  40.6 13.0 %all_to_all.11.ret_ref = f32[16,32,128]{2,1,0:T(8,128)S(1)} all-to-all(f32[16,32,128]{2,1,0:T(8,128)S(1)} %get-tuple-element.10), channel_id=1, replica_groups=mesh['group'=2,'tile'=16] {'tile'}, dimensions={0} | all-to-all | bytes 524288 | tf_op jit(solution)/shard_map/all_to_all | solution.py:307
  53.6 0.0 copy-done
  53.6 0.0 copy-done.1
  53.6 6.8 %shard_map.71 = f32[32,6912]{1,0:T(8,128)} custom-call(f32[16,32,128]{2,1,0:T(8,128)S(1)} %all_to_all.11.ret_ref, s32[4,6912]{1,0:T(4,128)S(1)} %bitcast.4, f32[4,6912]{1,0:T(4,128)S(1)} %copy-done.1), custom_call_target="tpu_custom_call" | custom-call | tf_op jit(solution)/shard_map/pallas_call | solution.py:236
Async XLA Ops:
  10.8 17.5 %copy-start.2 = (f32[18,192]{1,0:T(8,128)S(1)}, f32[18,192]{1,0:T(8,128)}, u32[]{:S(2)}) copy-start(f32[18,192]{1,0:T(8,128)} %own_ref.1) | copy-start | bytes 41476
  10.8 17.5 %copy-start.3 = (s32[2048]{0:T(1024)S(1)}, s32[2048]{0:T(1024)}, u32[]{:S(2)}) copy-start(s32[2048]{0:T(1024)} %param.8) | copy-start | bytes 24580
  29.8 1.8 %collective-permute-start = (f32[8,32,128]{2,1,0:T(8,128)S(1)}, f32[8,32,128]{2,1,0:T(8,128)S(1)}, u32[]{:S(2)}, u32[]{:S(2)}) collective-permute-start(f32[8,32,128]{2,1,0:T(8,128)S(1)} %get-tuple-element.8), channel_id=1, source_target_pairs={{0,1},{1,0},{2,3},{3,2},{4,5},{5,4},{6,7},{7,6},{8,9},{9,8},{10,11... | collective-permute-start | bytes 393224 | tf_op jit(solution)/shard_map/ppermute | solution.py:282
  29.9 7.2 %collective-permute-start.1 = (f32[8,32,128]{2,1,0:T(8,128)S(1)}, f32[8,32,128]{2,1,0:T(8,128)S(1)}, u32[]{:S(2)}, u32[]{:S(2)}) collective-permute-start(f32[8,32,128]{2,1,0:T(8,128)S(1)} %get-tuple-element.9), channel_id=1, source_target_pairs={{0,15},{1,2},{2,1},{3,4},{4,3},{5,6},{6,5},{7,8},{8,7},{9,10},{10,... | collective-permute-start | bytes 393224 | tf_op jit(solution)/shard_map/ppermute | solution.py:281
  40.6 13.0 %copy-start = (s32[6912,4]{0,1:T(4,128)S(1)}, s32[6912,4]{0,1:T(4,128)}, u32[]{:S(2)}) copy-start(s32[6912,4]{0,1:T(4,128)} %param.6) | copy-start | bytes 331780
  40.6 13.0 %copy-start.1 = (f32[4,6912]{1,0:T(4,128)S(1)}, f32[4,6912]{1,0:T(4,128)}, u32[]{:S(2)}) copy-start(f32[4,6912]{1,0:T(4,128)} %weight_ref.3) | copy-start | bytes 331780

commit v5 on v4

--- a/solution.py
+++ b/solution.py
@@ -123,15 +123,60 @@
     pl.when(jnp.logical_not(even))(lambda: place(near_ref, far_ref))
 
 
-def diffuse_and_read(
-    coarse_ref, near_ref, far_ref, own_ref, cell_ref, field_ref, values_ref, one_ref, two_ref, coef_ref, *, width
+def stepped(above, here, below, coef):
+    wide = here.shape[-1]
+    spread = below + above + pltpu.roll(here, 1, 1) + pltpu.roll(here, wide - 1, 1)
+    return here + coef * (spread - 4.0 * here)
+
+
+def kept_rows(turn, total):
+    first, last = STEPS + turn, total - STEPS - turn
+    return [first, first + 1, last - 2, last - 1]
+
+
+def read_rows(final_rows, ys, cell_ref, values_ref, base, width):
+    senders, channels, _ = values_ref.shape
+    left = jnp.concatenate([jnp.concatenate(halves(row), 0) for row in final_rows], 0)
+    for s in range(0, senders, 2):
+        cells = jnp.concatenate([cell_ref[s : s + 1, :], cell_ref[s + 1 : s + 2, :]], 1)
+        y = cells // width
+        found = jnp.dot(left, one_hot(cells - y * width, left.shape[1]), preferred_element_type=F32)
+        out = base(s)
+        marks = jnp.broadcast_to(y, out.shape)
+        for k, row in enumerate(ys):
+            both = found[2 * channels * k : 2 * channels * (k + 1)]
+            out = jnp.where(marks == row, both[:channels] + both[channels:], out)
+        values_ref[s] = out[:, :LANES]
+        values_ref[s + 1] = out[:, LANES:]
+
+
+def diffuse_inner(coarse_ref, own_ref, cell_ref, kept_ref, inner_ref, values_ref, one_ref, two_ref, coef_ref, *, width):
+    rows, channels, wide = coarse_ref.shape
+    own = own_ref[...]
+    coef_ref[...] = widened([own], own, own, width)
+    held, other, last = coarse_ref, one_ref, two_ref
+    for turn in range(1, STEPS + 1):
+        for y in range(turn, rows - turn):
+            other[y] = stepped(held[y - 1], held[y], held[y + 1], coef_ref[y : y + 1, :])
+        if turn < STEPS:
+            for place, y in enumerate(kept_rows(turn, rows + 2 * STEPS)):
+                kept_ref[turn - 1, place] = other[y - STEPS]
+        held, other, last = other, last, other
+    ys = range(STEPS, rows - STEPS)
+    for y in ys:
+        inner_ref[y - STEPS] = held[y]
+    nothing = lambda s: jnp.zeros((channels, 2 * LANES), F32)
+    read_rows([held[y] for y in ys], ys, cell_ref, values_ref, nothing, width)
+
+
+def diffuse_outer(
+    coarse_ref, near_ref, far_ref, own_ref, cell_ref, kept_ref, inner_ref, part_ref,
+    field_ref, values_ref, one_ref, two_ref, coef_ref, *, width
 ):
     rows, channels, wide = coarse_ref.shape
-    senders = values_ref.shape[0]
     total = rows + 2 * STEPS
     own = own_ref[...]
     coef_ref[STEPS : STEPS + rows, :] = widened([own], own, own, width)
-    one_ref[STEPS : STEPS + rows] = coarse_ref[...]
     even = lax.axis_index("tile") % 2 == 0
 
     def read(before_ref, after_ref):
@@ -145,25 +190,23 @@
     pl.when(jnp.logical_not(even))(lambda: read(near_ref, far_ref))
     held, other = one_ref, two_ref
     for turn in range(1, STEPS + 1):
-        for y in range(turn, total - turn):
-            here = held[y]
-            spread = held[y + 1] + held[y - 1] + pltpu.roll(here, 1, 1) + pltpu.roll(here, wide - 1, 1)
-            other[y] = here + coef_ref[y : y + 1, :] * (spread - 4.0 * here)
+
+        def row(y):
+            if turn == 1 and STEPS <= y < STEPS + rows:
+                return coarse_ref[y - STEPS]
+            kept = kept_rows(turn - 1, total) if turn > 1 else []
+            return kept_ref[turn - 2, kept.index(y)] if y in kept else held[y]
+
+        for start in (turn, total - STEPS - turn):
+            for y in range(start, start + STEPS):
+                other[y] = stepped(row(y - 1), row(y), row(y + 1), coef_ref[y : y + 1, :])
         held, other = other, held
-    final = held[STEPS : STEPS + rows]
-    field_ref[...] = final[:, :, :width]
-    left = jnp.concatenate(halves(final.reshape(rows * channels, wide)), 1)
-    for s in range(0, senders, 2):
-        cells = jnp.concatenate([cell_ref[s : s + 1, :], cell_ref[s + 1 : s + 2, :]], 1)
-        y = cells // width
-        right = one_hot(cells - y * width, wide)
-        found = jnp.dot(left, jnp.concatenate([right, right], 0), preferred_element_type=F32)
-        out = jnp.zeros((channels, 2 * LANES), F32)
-        marks = jnp.broadcast_to(y, out.shape)
-        for k in range(rows):
-            out = jnp.where(marks == k, found[channels * k : channels * (k + 1)], out)
-        values_ref[s] = out[:, :LANES]
-        values_ref[s + 1] = out[:, LANES:]
+    ys = list(range(STEPS)) + list(range(rows - STEPS, rows))
+    for y in range(rows):
+        source = held[y + STEPS] if y in ys else inner_ref[y - STEPS]
+        field_ref[y] = source[:, :width]
+    base = lambda s: jnp.concatenate([part_ref[s], part_ref[s + 1]], 1)
+    read_rows([held[y + STEPS] for y in ys], ys, cell_ref, values_ref, base, width)
 
 
 def by_product(table_ref, slot_ref, weight_ref, columns, channels):
@@ -231,7 +274,7 @@
     return max(c for c in range(LANES, most + 1, LANES) if fine % c == 0)
 
 
-def call(kernel, ins, out, scratch=(), grid=(), in_specs=VMEM, out_specs=VMEM, memory=16):
+def call(kernel, ins, out, scratch=(), grid=(), in_specs=VMEM, out_specs=VMEM, memory=16, cost=None):
     single = isinstance(in_specs, pl.BlockSpec)
     return pl.pallas_call(
         kernel,
@@ -240,6 +283,7 @@
         in_specs=[in_specs] * len(ins) if single else in_specs,
         out_specs=[out_specs] * len(out) if isinstance(out, list) else out_specs,
         scratch_shapes=list(scratch),
+        cost_estimate=cost,
         compiler_params=pltpu.CompilerParams(vmem_limit_bytes=memory << 20),
     )(*ins)
 
@@ -280,11 +324,20 @@
     )
     far = lax.ppermute(far, "tile", off_chip)
     near = lax.ppermute(near, "tile", on_chip)
+    slot_blocks = shape((blocks, channels, LANES), F32)
+    own = pltpu.VMEM((rows, channels, wide), F32)
+    kept, inner, found = call(
+        functools.partial(diffuse_inner, width=width),
+        (coarse, diffusivity, cells),
+        [shape((STEPS - 1, 4, channels, wide), F32), shape((rows - 2 * STEPS, channels, wide), F32), slot_blocks],
+        [own, own, pltpu.VMEM((rows, wide), F32)],
+        cost=pl.CostEstimate(flops=2 * slot_count * wide * wide * 2, bytes_accessed=8 << 20, transcendentals=0),
+    )
     padded = pltpu.VMEM((rows + 2 * STEPS, channels, wide), F32)
     field, values = call(
-        functools.partial(diffuse_and_read, width=width),
-        (coarse, near, far, diffusivity, cells),
-        [shape((rows, channels, width), F32), shape((blocks, channels, LANES), F32)],
+        functools.partial(diffuse_outer, width=width),
+        (coarse, near, far, diffusivity, cells, kept, inner, found),
+        [shape((rows, channels, width), F32), slot_blocks],
         [padded, padded, pltpu.VMEM((rows + 2 * STEPS, wide), F32)],
     )
     returned = exchange(values, tiles, share)

time: 60.8 us -> 59.9 us (0.985)
  waiting for transfers between devices: 5.46 us -> 3.63 us
  Pallas kernels: 22 us -> 23 us
    ppermute x1, waiting for transfers between devices: 5.46 us -> 3.63 us  [body(): far = lax.ppermute(far, 'tile', off_chip)]
    pallas_call x4 -> x5, Pallas kernels: 22 us -> 23 us  [call(): pl.pallas_call(kernel, grid=grid, out_shape=out, in_specs=[in_specs] * le...]
  transfers between devices with their start and end apart: 2 -> 2, of which waited for: 1 -> 1; matrix products, arithmetic and copies ran while one was open for 0% -> 0% of each run, Pallas kernels for 0% -> 3%
where the time goes in v5:
time: 59.9 us; the launch traced here: 59.6 us
  blocking collectives  30.5 us (51%)
  Pallas kernels  23 us (38%)
  waiting for transfers between devices  3.63 us (6%)
  starting transfers between devices  1.77 us (3%)
  between operations  0.66 us (1%)
    all_to_all x2, blocking collectives, exchange(): lax.all_to_all(blocks, 'tile', split_axis=0, concat_axis=0, tiled=True)  30.5 us
    pallas_call x5, Pallas kernels, call(): pl.pallas_call(kernel, grid=grid, out_shape=out, in_specs=[in_specs] * le...  23 us
    ppermute x1, waiting for transfers between devices, body(): far = lax.ppermute(far, 'tile', off_chip)  3.63 us
    ppermute x1, starting transfers between devices, body(): far = lax.ppermute(far, 'tile', off_chip)  1.69 us
  transfers between devices with their start and end apart: 2, of which 1 were waited for; matrix products, arithmetic and copies ran while one was open for 0% of the time, Pallas kernels for 3%

profile of v5, /device:TPU:0, one launch (start us, length us, event | category | flops | bytes accessed | tf_op | source)
XLA Modules:
  0.0 59.6 jit_solution(8762437990473421521)
XLA Ops:
  0.6 10.1 %shard_map.68 = f32[16,32,128]{2,1,0:T(8,128)} custom-call(f32[32,6912]{1,0:T(8,128)} %inc_ref.1, s32[4,6912]{1,0:T(4,128)} %bitcast.3, f32[4,6912]{1,0:T(4,128)} %weight_ref.3), custom_call_target="tpu_custom_call" | custom-call | tf_op jit(solution)/shard_map/pallas_call | solution.py:279
  10.8 0.0 copy-start.2
  10.8 0.0 copy-start.3
  10.8 17.5 %all_to_all.10.rec_ref = f32[16,32,128]{2,1,0:T(8,128)S(1)} all-to-all(f32[16,32,128]{2,1,0:T(8,128)} %shard_map.68), channel_id=1, replica_groups=mesh['group'=2,'tile'=16] {'tile'}, dimensions={0} | all-to-all | bytes 524288 | tf_op jit(solution)/shard_map/all_to_all | solution.py:360
  28.3 0.0 copy-done.2
  28.3 0.0 copy-done.3
  28.3 1.5 %shard_map.69 = (f32[18,32,256]{2,1,0:T(8,128)S(1)}, f32[8,32,128]{2,1,0:T(8,128)S(1)}, f32[8,32,128]{2,1,0:T(8,128)S(1)}) custom-call(f32[16,32,128]{2,1,0:T(8,128)S(1)} %all_to_all.10.rec_ref, s32[16,128]{1,0:T(8,128)S(1)} %bitcast.5, f32[18,192]{1,0:T(8,128)S(1)} %copy-done.2), custom_call_target="tpu_custom_call" | custom-call | tf_op jit(solution)/shard_map/pallas_call | solution.py:279
  29.8 0.1 collective-permute-start
  29.9 1.7 %collective-permute-start.1 = (f32[8,32,128]{2,1,0:T(8,128)S(1)}, f32[8,32,128]{2,1,0:T(8,128)S(1)}, u32[]{:S(2)}, u32[]{:S(2)}) collective-permute-start(f32[8,32,128]{2,1,0:T(8,128)S(1)} %get-tuple-element.12), channel_id=1, source_target_pairs={{0,15},{1,2},{2,1},{3,4},{4,3},{5,6},{6,5},{7,8},{8,7},{9,10},{10,... | collective-permute-start | bytes 393224 | tf_op jit(solution)/shard_map/ppermute | solution.py:325
  31.6 1.8 %shard_map.70 = (f32[4,4,32,256]{3,2,1,0:T(8,128)S(1)}, f32[8,32,256]{2,1,0:T(8,128)S(1)}, f32[16,32,128]{2,1,0:T(8,128)S(1)}) custom-call(f32[18,32,256]{2,1,0:T(8,128)S(1)} %get-tuple-element.10.coarse_ref, f32[18,192]{1,0:T(8,128)S(1)} %copy-done.2, s32[16,128]{1,0:T(8,128)S(1)} %bitcast.6), custom_call_target="tpu_custom_call" | custom-call | flops 536870912 | bytes 8388608 | tf_op jit(solution)/shard_map/pallas_call | solution.py:279
  33.4 0.0 collective-permute-done.near_ref
  33.5 3.6 %collective-permute-done.1.far_ref = f32[8,32,128]{2,1,0:T(8,128)S(1)} collective-permute-done((f32[8,32,128]{2,1,0:T(8,128)S(1)}, f32[8,32,128]{2,1,0:T(8,128)S(1)}, u32[]{:S(2)}, u32[]{:S(2)}) %collective-permute-start.1) | collective-permute-done | bytes 131104 | tf_op jit(solution)/shard_map/ppermute | solution.py:325
  37.1 2.7 %shard_map.71 = (f32[18,32,192]{2,1,0:T(8,128)}, f32[16,32,128]{2,1,0:T(8,128)S(1)}) custom-call(f32[18,32,256]{2,1,0:T(8,128)S(1)} %get-tuple-element.10.coarse_ref, f32[8,32,128]{2,1,0:T(8,128)S(1)} %collective-permute-done.near_ref, f32[8,32,128]{2,1,0:T(8,128)S(1)} %collective-permute-done.1.far_ref, f32[18,192]{1,0:T(8,128)S(1)} %copy-done.2, ...), custom_call_target="tpu_custom_call" | custom-call | tf_op jit(solution)/shard_map/pallas_call | solution.py:279
  39.8 0.0 copy-start
  39.8 0.0 copy-start.1
  39.8 13.0 %all_to_all.11.ret_ref = f32[16,32,128]{2,1,0:T(8,128)S(1)} all-to-all(f32[16,32,128]{2,1,0:T(8,128)S(1)} %get-tuple-element.16), channel_id=1, replica_groups=mesh['group'=2,'tile'=16] {'tile'}, dimensions={0} | all-to-all | bytes 524288 | tf_op jit(solution)/shard_map/all_to_all | solution.py:360
  52.8 0.0 copy-done
  52.8 0.0 copy-done.1
  52.8 6.8 %shard_map.72 = f32[32,6912]{1,0:T(8,128)} custom-call(f32[16,32,128]{2,1,0:T(8,128)S(1)} %all_to_all.11.ret_ref, s32[4,6912]{1,0:T(4,128)S(1)} %bitcast.4, f32[4,6912]{1,0:T(4,128)S(1)} %copy-done.1), custom_call_target="tpu_custom_call" | custom-call | tf_op jit(solution)/shard_map/pallas_call | solution.py:279
Async XLA Ops:
  10.8 17.5 %copy-start.2 = (f32[18,192]{1,0:T(8,128)S(1)}, f32[18,192]{1,0:T(8,128)}, u32[]{:S(2)}) copy-start(f32[18,192]{1,0:T(8,128)} %own_ref.3) | copy-start | bytes 41476
  10.8 17.5 %copy-start.3 = (s32[2048]{0:T(1024)S(1)}, s32[2048]{0:T(1024)}, u32[]{:S(2)}) copy-start(s32[2048]{0:T(1024)} %param.8) | copy-start | bytes 24580
  29.8 3.6 %collective-permute-start = (f32[8,32,128]{2,1,0:T(8,128)S(1)}, f32[8,32,128]{2,1,0:T(8,128)S(1)}, u32[]{:S(2)}, u32[]{:S(2)}) collective-permute-start(f32[8,32,128]{2,1,0:T(8,128)S(1)} %get-tuple-element.11), channel_id=1, source_target_pairs={{0,1},{1,0},{2,3},{3,2},{4,5},{5,4},{6,7},{7,6},{8,9},{9,8},{10,11... | collective-permute-start | bytes 393224 | tf_op jit(solution)/shard_map/ppermute | solution.py:326
  29.9 7.2 %collective-permute-start.1 = (f32[8,32,128]{2,1,0:T(8,128)S(1)}, f32[8,32,128]{2,1,0:T(8,128)S(1)}, u32[]{:S(2)}, u32[]{:S(2)}) collective-permute-start(f32[8,32,128]{2,1,0:T(8,128)S(1)} %get-tuple-element.12), channel_id=1, source_target_pairs={{0,15},{1,2},{2,1},{3,4},{4,3},{5,6},{6,5},{7,8},{8,7},{9,10},{10,... | collective-permute-start | bytes 393224 | tf_op jit(solution)/shard_map/ppermute | solution.py:325
  39.8 13.0 %copy-start = (s32[6912,4]{0,1:T(4,128)S(1)}, s32[6912,4]{0,1:T(4,128)}, u32[]{:S(2)}) copy-start(s32[6912,4]{0,1:T(4,128)} %param.6) | copy-start | bytes 331780
  39.8 13.0 %copy-start.1 = (f32[4,6912]{1,0:T(4,128)S(1)}, f32[4,6912]{1,0:T(4,128)}, u32[]{:S(2)}) copy-start(f32[4,6912]{1,0:T(4,128)} %weight_ref.3) | copy-start | bytes 331780

commit v6 on v5

--- a/solution.py
+++ b/solution.py
@@ -27,10 +27,10 @@
     return jnp.where(rows == places, 1.0, 0.0).astype(BF16)
 
 
-def masked(values, marks, count):
+def masked(values, marks, wanted):
     marks = jnp.broadcast_to(marks, values.shape)
     zero = jnp.zeros((), values.dtype)
-    return jnp.concatenate([jnp.where(marks == k, values, zero) for k in range(count)], 0)
+    return jnp.concatenate([jnp.where(marks == k, values, zero) for k in wanted], 0)
 
 
 def dot_last(left, right):
@@ -45,7 +45,7 @@
     for corner in range(CORNERS):
         slots = slot_ref[corner : corner + 1, :]
         parts = jnp.concatenate(halves(weight_ref[corner : corner + 1, :] * inc), 0)
-        left.append(masked(parts, slots // PLACES, count))
+        left.append(masked(parts, slots // PLACES, range(count)))
         right.append(one_hot(slots % PLACES, PLACES))
     sums = dot_last(jnp.concatenate(left, 1), jnp.concatenate(right, 1))
 
@@ -97,27 +97,35 @@
     return jnp.concatenate(parts + [start[:, :extra], end[:, end.shape[1] - extra :]], 1)
 
 
-def add_to_cells(rec_ref, cell_ref, coef_ref, coarse_ref, near_ref, far_ref, *, width):
-    rows, channels, wide = coarse_ref.shape
-    senders = rec_ref.shape[0]
+def cell_sums(rec_ref, cell_ref, ys, width):
+    senders, channels, _ = rec_ref.shape
     cells = jnp.concatenate([cell_ref[s : s + 1, :] for s in range(senders)], 1)
     values = jnp.concatenate([rec_ref[s] for s in range(senders)], 1)
     y = cells // width
     right = jnp.where(wide_column(width) == cells - y * width, 1.0, 0.0).astype(BF16)
-    left = masked(jnp.concatenate(halves(values), 0), y, rows)
-    sums = dot_last(left, right)
+    sums = dot_last(masked(jnp.concatenate(halves(values), 0), y, ys), right)
     full = []
-    for k in range(rows):
+    for k in range(len(ys)):
         both = sums[2 * channels * k : 2 * channels * (k + 1)]
-        both = both[:channels] + both[channels:]
-        coarse_ref[k] = both
-        full.append(both)
+        full.append(both[:channels] + both[channels:])
+    return full
+
+
+def edges_of(rows):
+    return list(range(STEPS)) + list(range(rows - STEPS, rows))
+
+
+def sum_edges(rec_ref, cell_ref, coef_ref, edges_ref, near_ref, far_ref, *, width):
+    rows = coef_ref.shape[0]
+    full = cell_sums(rec_ref, cell_ref, edges_of(rows), width)
+    for k, row in enumerate(full):
+        edges_ref[k] = row
     coefs = [coef_ref[k : k + 1, :] for k in range(rows)]
     even = lax.axis_index("tile") % 2 == 0
 
     def place(head_ref, tail_ref):
         place_edge(head_ref, full[:STEPS], coefs[:STEPS], width)
-        place_edge(tail_ref, full[rows - STEPS :], coefs[rows - STEPS :], width)
+        place_edge(tail_ref, full[STEPS:], coefs[rows - STEPS :], width)
 
     pl.when(even)(lambda: place(far_ref, near_ref))
     pl.when(jnp.logical_not(even))(lambda: place(near_ref, far_ref))
@@ -150,11 +158,18 @@
         values_ref[s + 1] = out[:, LANES:]
 
 
-def diffuse_inner(coarse_ref, own_ref, cell_ref, kept_ref, inner_ref, values_ref, one_ref, two_ref, coef_ref, *, width):
-    rows, channels, wide = coarse_ref.shape
+def diffuse_inner(
+    rec_ref, edges_ref, own_ref, cell_ref, kept_ref, inner_ref, values_ref, start_ref, one_ref, two_ref, coef_ref, *, width
+):
+    rows, channels, wide = start_ref.shape
     own = own_ref[...]
     coef_ref[...] = widened([own], own, own, width)
-    held, other, last = coarse_ref, one_ref, two_ref
+    for k, y in enumerate(edges_of(rows)):
+        start_ref[y] = edges_ref[k]
+    ys = range(STEPS, rows - STEPS)
+    for y, row in zip(ys, cell_sums(rec_ref, cell_ref, ys, width)):
+        start_ref[y] = row
+    held, other, last = start_ref, one_ref, two_ref
     for turn in range(1, STEPS + 1):
         for y in range(turn, rows - turn):
             other[y] = stepped(held[y - 1], held[y], held[y + 1], coef_ref[y : y + 1, :])
@@ -162,7 +177,6 @@
             for place, y in enumerate(kept_rows(turn, rows + 2 * STEPS)):
                 kept_ref[turn - 1, place] = other[y - STEPS]
         held, other, last = other, last, other
-    ys = range(STEPS, rows - STEPS)
     for y in ys:
         inner_ref[y - STEPS] = held[y]
     nothing = lambda s: jnp.zeros((channels, 2 * LANES), F32)
@@ -170,10 +184,10 @@
 
 
 def diffuse_outer(
-    coarse_ref, near_ref, far_ref, own_ref, cell_ref, kept_ref, inner_ref, part_ref,
-    field_ref, values_ref, one_ref, two_ref, coef_ref, *, width
+    edges_ref, near_ref, far_ref, own_ref, cell_ref, kept_ref, part_ref,
+    outer_ref, values_ref, one_ref, two_ref, coef_ref, *, width
 ):
-    rows, channels, wide = coarse_ref.shape
+    rows = own_ref.shape[0]
     total = rows + 2 * STEPS
     own = own_ref[...]
     coef_ref[STEPS : STEPS + rows, :] = widened([own], own, own, width)
@@ -188,12 +202,13 @@
 
     pl.when(even)(lambda: read(far_ref, near_ref))
     pl.when(jnp.logical_not(even))(lambda: read(near_ref, far_ref))
+    ys = edges_of(rows)
     held, other = one_ref, two_ref
     for turn in range(1, STEPS + 1):
 
         def row(y):
-            if turn == 1 and STEPS <= y < STEPS + rows:
-                return coarse_ref[y - STEPS]
+            if turn == 1 and y - STEPS in ys:
+                return edges_ref[ys.index(y - STEPS)]
             kept = kept_rows(turn - 1, total) if turn > 1 else []
             return kept_ref[turn - 2, kept.index(y)] if y in kept else held[y]
 
@@ -201,12 +216,19 @@
             for y in range(start, start + STEPS):
                 other[y] = stepped(row(y - 1), row(y), row(y + 1), coef_ref[y : y + 1, :])
         held, other = other, held
-    ys = list(range(STEPS)) + list(range(rows - STEPS, rows))
+    final = [held[y + STEPS] for y in ys]
+    for k, row in enumerate(final):
+        outer_ref[k] = row
+    base = lambda s: jnp.concatenate([part_ref[s], part_ref[s + 1]], 1)
+    read_rows(final, ys, cell_ref, values_ref, base, width)
+
+
+def join_rows(inner_ref, outer_ref, field_ref):
+    rows, _, width = field_ref.shape
+    ys = edges_of(rows)
     for y in range(rows):
-        source = held[y + STEPS] if y in ys else inner_ref[y - STEPS]
-        field_ref[y] = source[:, :width]
-    base = lambda s: jnp.concatenate([part_ref[s], part_ref[s + 1]], 1)
-    read_rows([held[y + STEPS] for y in ys], ys, cell_ref, values_ref, base, width)
+        row = outer_ref[ys.index(y)] if y in ys else inner_ref[y - STEPS]
+        field_ref[y] = row[:, :width]
 
 
 def by_product(table_ref, slot_ref, weight_ref, columns, channels):
@@ -317,30 +339,36 @@
     )
     received = exchange(sent, tiles, share)
     edge = shape((EDGE, channels, LANES), F32)
-    coarse, near, far = call(
-        functools.partial(add_to_cells, width=width),
-        (received, cells, diffusivity),
-        [shape((rows, channels, wide), F32), edge, edge],
+    slot_blocks = shape((blocks, channels, LANES), F32)
+    edge_rows = shape((2 * STEPS, channels, wide), F32)
+    edges, near, far = call(
+        functools.partial(sum_edges, width=width), (received, cells, diffusivity), [edge_rows, edge, edge]
     )
     far = lax.ppermute(far, "tile", off_chip)
     near = lax.ppermute(near, "tile", on_chip)
-    slot_blocks = shape((blocks, channels, LANES), F32)
     own = pltpu.VMEM((rows, channels, wide), F32)
     kept, inner, found = call(
         functools.partial(diffuse_inner, width=width),
-        (coarse, diffusivity, cells),
+        (received, edges, diffusivity, cells),
         [shape((STEPS - 1, 4, channels, wide), F32), shape((rows - 2 * STEPS, channels, wide), F32), slot_blocks],
-        [own, own, pltpu.VMEM((rows, wide), F32)],
-        cost=pl.CostEstimate(flops=2 * slot_count * wide * wide * 2, bytes_accessed=8 << 20, transcendentals=0),
+        [own, own, own, pltpu.VMEM((rows, wide), F32)],
+        cost=pl.CostEstimate(flops=4 * slot_count * wide * wide, bytes_accessed=8 << 20, transcendentals=0),
     )
     padded = pltpu.VMEM((rows + 2 * STEPS, channels, wide), F32)
-    field, values = call(
+    outer, values = call(
         functools.partial(diffuse_outer, width=width),
-        (coarse, near, far, diffusivity, cells, kept, inner, found),
-        [shape((rows, channels, width), F32), slot_blocks],
+        (edges, near, far, diffusivity, cells, kept, found),
+        [edge_rows, slot_blocks],
         [padded, padded, pltpu.VMEM((rows + 2 * STEPS, wide), F32)],
     )
+    field = call(
+        join_rows,
+        (inner, outer),
+        shape((rows, channels, width), F32),
+        cost=pl.CostEstimate(flops=rows * channels * wide, bytes_accessed=4 << 20, transcendentals=0),
+    )
     returned = exchange(values, tiles, share)
+    field, tent_weight = lax.optimization_barrier((field, tent_weight))
     result = call(
         functools.partial(sum_from_slots, plan=plan_of(chunk // LANES)),
         (returned, slots, tent_weight),

time: 59.9 us -> 59.9 us (level)
  blocking collectives: 30.5 us -> 17.5 us
  waiting for transfers between devices: 3.63 us -> 11.3 us
  starting transfers between devices: 1.77 us -> 5.3 us
  Pallas kernels: 23 us -> 24.7 us
    all_to_all x2 -> x1, blocking collectives: 30.5 us -> 17.5 us  [exchange(): lax.all_to_all(blocks, 'tile', split_axis=0, concat_axis=0, tiled=True)]
    all_to_all x0 -> x1, waiting for transfers between devices: none -> 9.13 us  [exchange(): lax.all_to_all(blocks, 'tile', split_axis=0, concat_axis=0, tiled=True)]
    all_to_all x0 -> x1, starting transfers between devices: none -> 3.53 us  [exchange(): lax.all_to_all(blocks, 'tile', split_axis=0, concat_axis=0, tiled=True)]
    pallas_call x5 -> x6, Pallas kernels: 23 us -> 24.7 us  [call(): pl.pallas_call(kernel, grid=grid, out_shape=out, in_specs=[in_specs] * le...]
    ppermute x1, waiting for transfers between devices: 3.63 us -> 2.21 us  [body(): far = lax.ppermute(far, 'tile', off_chip)]
  transfers between devices with their start and end apart: 2 -> 3, of which waited for: 1 -> 2; matrix products, arithmetic and copies ran while one was open for 0% -> 0% of each run, Pallas kernels for 3% -> 7%
where the time goes in v6:
time: 59.9 us; the launch traced here: 59.5 us
  Pallas kernels  24.7 us (41%)
  blocking collectives  17.5 us (29%)
  waiting for transfers between devices  11.3 us (19%)
  starting transfers between devices  5.3 us (9%)
  between operations  0.68 us (1%)
    pallas_call x6, Pallas kernels, call(): pl.pallas_call(kernel, grid=grid, out_shape=out, in_specs=[in_specs] * le...  24.7 us
    all_to_all x1, blocking collectives, exchange(): lax.all_to_all(blocks, 'tile', split_axis=0, concat_axis=0, tiled=True)  17.5 us
    all_to_all x1, waiting for transfers between devices, exchange(): lax.all_to_all(blocks, 'tile', split_axis=0, concat_axis=0, tiled=True)  9.13 us
    all_to_all x1, starting transfers between devices, exchange(): lax.all_to_all(blocks, 'tile', split_axis=0, concat_axis=0, tiled=True)  3.53 us
    ppermute x1, waiting for transfers between devices, body(): far = lax.ppermute(far, 'tile', off_chip)  2.21 us
    ppermute x1, starting transfers between devices, body(): far = lax.ppermute(far, 'tile', off_chip)  1.69 us
  transfers between devices with their start and end apart: 3, of which 2 were waited for; matrix products, arithmetic and copies ran while one was open for 0% of the time, Pallas kernels for 7%

profile of v6, /device:TPU:0, one launch (start us, length us, event | category | flops | bytes accessed | tf_op | source)
XLA Modules:
  0.0 59.5 jit_solution(9334906604683660209)
XLA Ops:
  0.6 10.1 %shard_map.68 = f32[16,32,128]{2,1,0:T(8,128)} custom-call(f32[32,6912]{1,0:T(8,128)} %inc_ref.1, s32[4,6912]{1,0:T(4,128)} %bitcast.3, f32[4,6912]{1,0:T(4,128)} %weight_ref.2), custom_call_target="tpu_custom_call" | custom-call | tf_op jit(solution)/shard_map/pallas_call | solution.py:301
  10.8 0.0 copy-start.2
  10.8 0.0 copy-start.3
  10.8 17.5 %all_to_all.10.rec_ref = f32[16,32,128]{2,1,0:T(8,128)S(1)} all-to-all(f32[16,32,128]{2,1,0:T(8,128)} %shard_map.68), channel_id=1, replica_groups=mesh['group'=2,'tile'=16] {'tile'}, dimensions={0} | all-to-all | bytes 524288 | tf_op jit(solution)/shard_map/all_to_all | solution.py:388
  28.3 0.0 copy-done.2
  28.3 0.0 copy-done.3
  28.3 1.0 %shard_map.69 = (f32[10,32,256]{2,1,0:T(8,128)S(1)}, f32[8,32,128]{2,1,0:T(8,128)S(1)}, f32[8,32,128]{2,1,0:T(8,128)S(1)}) custom-call(f32[16,32,128]{2,1,0:T(8,128)S(1)} %all_to_all.10.rec_ref, s32[16,128]{1,0:T(8,128)S(1)} %bitcast.5, f32[18,192]{1,0:T(8,128)S(1)} %copy-done.2), custom_call_target="tpu_custom_call" | custom-call | tf_op jit(solution)/shard_map/pallas_call | solution.py:301
  29.3 0.1 collective-permute-start
  29.4 1.7 %collective-permute-start.1 = (f32[8,32,128]{2,1,0:T(8,128)S(1)}, f32[8,32,128]{2,1,0:T(8,128)S(1)}, u32[]{:S(2)}, u32[]{:S(2)}) collective-permute-start(f32[8,32,128]{2,1,0:T(8,128)S(1)} %get-tuple-element.14), channel_id=1, source_target_pairs={{0,15},{1,2},{2,1},{3,4},{4,3},{5,6},{6,5},{7,8},{8,7},{9,10},{10,... | collective-permute-start | bytes 393224 | tf_op jit(solution)/shard_map/ppermute | solution.py:347
  31.1 3.2 %shard_map.70 = (f32[4,4,32,256]{3,2,1,0:T(8,128)S(1)}, f32[8,32,256]{2,1,0:T(8,128)S(1)}, f32[16,32,128]{2,1,0:T(8,128)S(1)}) custom-call(f32[16,32,128]{2,1,0:T(8,128)S(1)} %all_to_all.10.rec_ref, f32[10,32,256]{2,1,0:T(8,128)S(1)} %get-tuple-element.12.edges_ref, f32[18,192]{1,0:T(8,128)S(1)} %copy-done.2, s32[16,128]{1,0:T(8,128)S(1)} %bitcast.6), custom_call_target="tpu_custom_call" | custom-call | flops 536870912 | bytes 8388608 | tf_op jit(solution)/shard_map/pallas_call | solution.py:301
  34.3 0.0 collective-permute-done.near_ref
  34.3 2.2 %collective-permute-done.1.far_ref = f32[8,32,128]{2,1,0:T(8,128)S(1)} collective-permute-done((f32[8,32,128]{2,1,0:T(8,128)S(1)}, f32[8,32,128]{2,1,0:T(8,128)S(1)}, u32[]{:S(2)}, u32[]{:S(2)}) %collective-permute-start.1) | collective-permute-done | bytes 131104 | tf_op jit(solution)/shard_map/ppermute | solution.py:347
  36.5 2.7 %shard_map.71 = (f32[10,32,256]{2,1,0:T(8,128)S(1)}, f32[16,32,128]{2,1,0:T(8,128)}) custom-call(f32[10,32,256]{2,1,0:T(8,128)S(1)} %get-tuple-element.12.edges_ref, f32[8,32,128]{2,1,0:T(8,128)S(1)} %collective-permute-done.near_ref, f32[8,32,128]{2,1,0:T(8,128)S(1)} %collective-permute-done.1.far_ref, f32[18,192]{1,0:T(8,128)S(1)} %copy-done.2, ...), custom_call_target="tpu_custom_call" | custom-call | tf_op jit(solution)/shard_map/pallas_call | solution.py:301
  39.2 3.5 %all-to-all-start.1 = ((f32[16,32,128]{2,1,0:T(8,128)}), f32[16,32,128]{2,1,0:T(8,128)S(1)}, u32[]{:S(2)}, u32[]{:S(2)}) async-start(f32[16,32,128]{2,1,0:T(8,128)} %get-tuple-element.17), calls=%async_computation.1 | async-start | bytes 524288 | tf_op jit(solution)/shard_map/all_to_all | solution.py:388
  42.7 0.0 copy-start
  42.7 0.0 copy-start.1
  42.8 0.9 %shard_map.72 = f32[18,32,192]{2,1,0:T(8,128)} custom-call(f32[8,32,256]{2,1,0:T(8,128)S(1)} %get-tuple-element.18.inner_ref, f32[10,32,256]{2,1,0:T(8,128)S(1)} %get-tuple-element.19.outer_ref), custom_call_target="tpu_custom_call" | custom-call | flops 147456 | bytes 4194304 | tf_op jit(solution)/shard_map/pallas_call | solution.py:301
  43.6 9.1 %all-to-all-done.1.ret_ref = f32[16,32,128]{2,1,0:T(8,128)S(1)} async-done(((f32[16,32,128]{2,1,0:T(8,128)}), f32[16,32,128]{2,1,0:T(8,128)S(1)}, u32[]{:S(2)}, u32[]{:S(2)}) %all-to-all-start.1) | async-done | bytes 262176 | tf_op jit(solution)/shard_map/all_to_all | solution.py:388
  52.7 0.0 copy-done
  52.7 0.0 copy-done.1
  52.7 6.8 %shard_map.73 = f32[32,6912]{1,0:T(8,128)} custom-call(f32[16,32,128]{2,1,0:T(8,128)S(1)} %all-to-all-done.1.ret_ref, s32[4,6912]{1,0:T(4,128)S(1)} %bitcast.4, f32[4,6912]{1,0:T(4,128)S(1)} %copy-done.1), custom_call_target="tpu_custom_call" | custom-call | tf_op jit(solution)/shard_map/pallas_call | solution.py:301
Async XLA Ops:
  10.8 17.5 %copy-start.2 = (f32[18,192]{1,0:T(8,128)S(1)}, f32[18,192]{1,0:T(8,128)}, u32[]{:S(2)}) copy-start(f32[18,192]{1,0:T(8,128)} %own_ref.3) | copy-start | bytes 41476
  10.8 17.5 %copy-start.3 = (s32[2048]{0:T(1024)S(1)}, s32[2048]{0:T(1024)}, u32[]{:S(2)}) copy-start(s32[2048]{0:T(1024)} %param.8) | copy-start | bytes 24580
  29.3 5.0 %collective-permute-start = (f32[8,32,128]{2,1,0:T(8,128)S(1)}, f32[8,32,128]{2,1,0:T(8,128)S(1)}, u32[]{:S(2)}, u32[]{:S(2)}) collective-permute-start(f32[8,32,128]{2,1,0:T(8,128)S(1)} %get-tuple-element.13), channel_id=1, source_target_pairs={{0,1},{1,0},{2,3},{3,2},{4,5},{5,4},{6,7},{7,6},{8,9},{9,8},{10,11... | collective-permute-start | bytes 393224 | tf_op jit(solution)/shard_map/ppermute | solution.py:348
  29.4 7.2 %collective-permute-start.1 = (f32[8,32,128]{2,1,0:T(8,128)S(1)}, f32[8,32,128]{2,1,0:T(8,128)S(1)}, u32[]{:S(2)}, u32[]{:S(2)}) collective-permute-start(f32[8,32,128]{2,1,0:T(8,128)S(1)} %get-tuple-element.14), channel_id=1, source_target_pairs={{0,15},{1,2},{2,1},{3,4},{4,3},{5,6},{6,5},{7,8},{8,7},{9,10},{10,... | collective-permute-start | bytes 393224 | tf_op jit(solution)/shard_map/ppermute | solution.py:347
  39.2 13.5 %all-to-all-start.1 = ((f32[16,32,128]{2,1,0:T(8,128)}), f32[16,32,128]{2,1,0:T(8,128)S(1)}, u32[]{:S(2)}, u32[]{:S(2)}) async-start(f32[16,32,128]{2,1,0:T(8,128)} %get-tuple-element.17), calls=%async_computation.1 | async-start | bytes 524288 | tf_op jit(solution)/shard_map/all_to_all | solution.py:388
  42.7 10.0 %copy-start = (s32[6912,4]{0,1:T(4,128)S(1)}, s32[6912,4]{0,1:T(4,128)}, u32[]{:S(2)}) copy-start(s32[6912,4]{0,1:T(4,128)} %param.6) | copy-start | bytes 331780
  42.7 10.0 %copy-start.1 = (f32[4,6912]{1,0:T(4,128)S(1)}, f32[4,6912]{1,0:T(4,128)}, u32[]{:S(2)}) copy-start(f32[4,6912]{1,0:T(4,128)} %weight_ref.2) | copy-start | bytes 331780

commit v7 on v6

--- a/solution.py
+++ b/solution.py
@@ -60,41 +60,67 @@
             sent_ref[k * (PLACES // LANES) + part] += both[:, LANES * part : LANES * (part + 1)]
 
 
-def wide_column(width):
-    lanes = lax.broadcasted_iota(jnp.int32, (2 * LANES, 1), 0)
-    extra = (2 * LANES - width) // 2
-    return jnp.where(lanes < width, lanes, jnp.where(lanes < width + extra, lanes - width, lanes - 2 * LANES + width))
+def column_at(lanes, width):
+    half, extra = width // 2, (LANES - width // 2) // 2
+    odd = lanes // LANES
+    at = lanes % LANES
+    at = jnp.where(at < half, at, jnp.where(at < half + extra, at - half, at - LANES + half))
+    return 2 * at + odd
+
+
+def lane_of(x):
+    return LANES * (x % 2) + x // 2
+
+
+def narrowed(row, width):
+    half = width // 2
+    return jnp.concatenate([row[:, :half], row[:, LANES : LANES + half]], 1)
+
+
+def widened(row):
+    half = row.shape[1] // 2
+    extra = (LANES - half) // 2
+    out = []
+    for part in (row[:, :half], row[:, half:]):
+        out += [part, part[:, :extra], part[:, half - extra :]]
+    return jnp.concatenate(out, 1)
+
+
+def spread_columns(plain, width):
+    sides = [plain[:, :LANES], jnp.concatenate([plain[:, LANES:width], plain[:, : 2 * LANES - width]], 1)]
+    out = []
+    for odd in range(2):
+        x = column_at(lax.broadcasted_iota(jnp.int32, sides[0].shape, 1) + odd * LANES, width)
+        found = [jnp.take_along_axis(side, x % LANES, axis=1) for side in sides]
+        out.append(jnp.where(x < LANES, found[0], found[1]))
+    return jnp.concatenate(out, 1)
 
 
 def place_edge(edge_ref, rows, coefs, width):
     half = width - LANES
+    rows = [narrowed(row, width) for row in rows]
     for k, row in enumerate(rows):
         edge_ref[k] = row[:, :LANES]
-    ends = [row[:, LANES:width] for row in rows]
+    ends = [row[:, LANES:] for row in rows]
     for k in range(0, STEPS - 1, 2):
         edge_ref[STEPS + k // 2] = jnp.concatenate([ends[k], ends[k + 1]], 1)
     edge_ref[EDGE - 1] = jnp.concatenate([ends[-1], jnp.zeros_like(ends[-1])], 1)
     for k, coef in enumerate(coefs):
+        coef = narrowed(coef, width)
         for part in range(3):
             edge_ref[EDGE - 1, 3 * k + part : 3 * k + part + 1, half:] = coef[:, half * part : half * (part + 1)]
 
 
 def read_edge(edge_ref, k, width):
     half = width - LANES
-    start = edge_ref[k]
     end = edge_ref[STEPS + k // 2, :, half * (k % 2) : half * (k % 2) + half]
-    return widened([start, end], start, end, width)
+    return widened(jnp.concatenate([edge_ref[k], end], 1))
 
 
 def read_coef(edge_ref, k, width):
     half = width - LANES
     parts = [edge_ref[EDGE - 1, 3 * k + part : 3 * k + part + 1, half:] for part in range(3)]
-    return widened(parts, parts[0], parts[2], width)
-
-
-def widened(parts, start, end, width):
-    extra = (2 * LANES - width) // 2
-    return jnp.concatenate(parts + [start[:, :extra], end[:, end.shape[1] - extra :]], 1)
+    return widened(jnp.concatenate(parts, 1))
 
 
 def cell_sums(rec_ref, cell_ref, ys, width):
@@ -102,7 +128,8 @@
     cells = jnp.concatenate([cell_ref[s : s + 1, :] for s in range(senders)], 1)
     values = jnp.concatenate([rec_ref[s] for s in range(senders)], 1)
     y = cells // width
-    right = jnp.where(wide_column(width) == cells - y * width, 1.0, 0.0).astype(BF16)
+    columns = column_at(lax.broadcasted_iota(jnp.int32, (2 * LANES, 1), 0), width)
+    right = jnp.where(columns == cells - y * width, 1.0, 0.0).astype(BF16)
     sums = dot_last(masked(jnp.concatenate(halves(values), 0), y, ys), right)
     full = []
     for k in range(len(ys)):
@@ -115,8 +142,12 @@
     return list(range(STEPS)) + list(range(rows - STEPS, rows))
 
 
-def sum_edges(rec_ref, cell_ref, coef_ref, edges_ref, near_ref, far_ref, *, width):
-    rows = coef_ref.shape[0]
+def sum_edges(rec_ref, cell_ref, own_ref, edges_ref, near_ref, far_ref, coef_ref, plain_ref, *, width):
+    rows = own_ref.shape[0]
+    plain_ref[...] = jnp.zeros_like(plain_ref)
+    plain_ref[:rows] = own_ref[...]
+    for k in range(0, plain_ref.shape[0], 8):
+        coef_ref[k : k + 8, :] = spread_columns(plain_ref[k : k + 8, :], width)
     full = cell_sums(rec_ref, cell_ref, edges_of(rows), width)
     for k, row in enumerate(full):
         edges_ref[k] = row
@@ -132,8 +163,9 @@
 
 
 def stepped(above, here, below, coef):
-    wide = here.shape[-1]
-    spread = below + above + pltpu.roll(here, 1, 1) + pltpu.roll(here, wide - 1, 1)
+    even, odd = here[:, :LANES], here[:, LANES:]
+    sides = jnp.concatenate([pltpu.roll(odd, 1, 1) + odd, even + pltpu.roll(even, LANES - 1, 1)], 1)
+    spread = below + above + sides
     return here + coef * (spread - 4.0 * here)
 
 
@@ -148,7 +180,7 @@
     for s in range(0, senders, 2):
         cells = jnp.concatenate([cell_ref[s : s + 1, :], cell_ref[s + 1 : s + 2, :]], 1)
         y = cells // width
-        found = jnp.dot(left, one_hot(cells - y * width, left.shape[1]), preferred_element_type=F32)
+        found = jnp.dot(left, one_hot(lane_of(cells - y * width), left.shape[1]), preferred_element_type=F32)
         out = base(s)
         marks = jnp.broadcast_to(y, out.shape)
         for k, row in enumerate(ys):
@@ -159,11 +191,9 @@
 
 
 def diffuse_inner(
-    rec_ref, edges_ref, own_ref, cell_ref, kept_ref, inner_ref, values_ref, start_ref, one_ref, two_ref, coef_ref, *, width
+    rec_ref, edges_ref, coef_ref, cell_ref, kept_ref, inner_ref, values_ref, start_ref, one_ref, two_ref, *, width
 ):
     rows, channels, wide = start_ref.shape
-    own = own_ref[...]
-    coef_ref[...] = widened([own], own, own, width)
     for k, y in enumerate(edges_of(rows)):
         start_ref[y] = edges_ref[k]
     ys = range(STEPS, rows - STEPS)
@@ -187,10 +217,9 @@
     edges_ref, near_ref, far_ref, own_ref, cell_ref, kept_ref, part_ref,
     outer_ref, values_ref, one_ref, two_ref, coef_ref, *, width
 ):
-    rows = own_ref.shape[0]
-    total = rows + 2 * STEPS
-    own = own_ref[...]
-    coef_ref[STEPS : STEPS + rows, :] = widened([own], own, own, width)
+    total = coef_ref.shape[0]
+    rows = total - 2 * STEPS
+    coef_ref[STEPS : STEPS + rows, :] = own_ref[:rows, :]
     even = lax.axis_index("tile") % 2 == 0
 
     def read(before_ref, after_ref):
@@ -224,11 +253,20 @@
 
 
 def join_rows(inner_ref, outer_ref, field_ref):
-    rows, _, width = field_ref.shape
+    rows, channels, width = field_ref.shape
     ys = edges_of(rows)
+    group = 8
+    lanes = lax.broadcasted_iota(jnp.int32, (group, LANES), 1)
     for y in range(rows):
-        row = outer_ref[ys.index(y)] if y in ys else inner_ref[y - STEPS]
-        field_ref[y] = row[:, :width]
+        row_ref = outer_ref.at[ys.index(y)] if y in ys else inner_ref.at[y - STEPS]
+        for c in range(0, channels, group):
+            even, odd = row_ref[c : c + group, :LANES], row_ref[c : c + group, LANES:]
+            for start in range(0, width, LANES):
+                at = (start + lanes) // 2
+                found = [jnp.take_along_axis(part, at, axis=1) for part in (even, odd)]
+                size = min(LANES, width - start)
+                out = jnp.where(lanes % 2 == 0, found[0], found[1])
+                field_ref[y, c : c + group, start : start + size] = out[:, :size]
 
 
 def by_product(table_ref, slot_ref, weight_ref, columns, channels):
@@ -341,23 +379,27 @@
     edge = shape((EDGE, channels, LANES), F32)
     slot_blocks = shape((blocks, channels, LANES), F32)
     edge_rows = shape((2 * STEPS, channels, wide), F32)
-    edges, near, far = call(
-        functools.partial(sum_edges, width=width), (received, cells, diffusivity), [edge_rows, edge, edge]
+    tall = -(-rows // 8) * 8
+    edges, near, far, coef = call(
+        functools.partial(sum_edges, width=width),
+        (received, cells, diffusivity),
+        [edge_rows, edge, edge, shape((tall, wide), F32)],
+        [pltpu.VMEM((tall, width), F32)],
     )
     far = lax.ppermute(far, "tile", off_chip)
     near = lax.ppermute(near, "tile", on_chip)
     own = pltpu.VMEM((rows, channels, wide), F32)
     kept, inner, found = call(
         functools.partial(diffuse_inner, width=width),
-        (received, edges, diffusivity, cells),
+        (received, edges, coef, cells),
         [shape((STEPS - 1, 4, channels, wide), F32), shape((rows - 2 * STEPS, channels, wide), F32), slot_blocks],
-        [own, own, own, pltpu.VMEM((rows, wide), F32)],
+        [own, own, own],
         cost=pl.CostEstimate(flops=4 * slot_count * wide * wide, bytes_accessed=8 << 20, transcendentals=0),
     )
     padded = pltpu.VMEM((rows + 2 * STEPS, channels, wide), F32)
     outer, values = call(
         functools.partial(diffuse_outer, width=width),
-        (edges, near, far, diffusivity, cells, kept, found),
+        (edges, near, far, coef, cells, kept, found),
         [edge_rows, slot_blocks],
         [padded, padded, pltpu.VMEM((rows + 2 * STEPS, wide), F32)],
     )

time: 59.9 us -> 60.3 us (level)
  Pallas kernels: 24.7 us -> 25.4 us
    pallas_call x6, Pallas kernels: 24.7 us -> 25.4 us  [call(): pl.pallas_call(kernel, grid=grid, out_shape=out, in_specs=[in_specs] * le...]
    all_to_all x1, waiting for transfers between devices: 9.13 us -> 8.42 us  [exchange(): lax.all_to_all(blocks, 'tile', split_axis=0, concat_axis=0, tiled=True)]
  transfers between devices with their start and end apart: 3 -> 3, of which waited for: 2 -> 2; matrix products, arithmetic and copies ran while one was open for 0% -> 0% of each run, Pallas kernels for 7% -> 8%
where the time goes in v7:
time: 60.3 us; the launch traced here: 59.9 us
  Pallas kernels  25.4 us (42%)
  blocking collectives  17.5 us (29%)
  waiting for transfers between devices  10.9 us (18%)
  starting transfers between devices  5.3 us (9%)
  between operations  0.68 us (1%)
    pallas_call x6, Pallas kernels, call(): pl.pallas_call(kernel, grid=grid, out_shape=out, in_specs=[in_specs] * le...  25.4 us
    all_to_all x1, blocking collectives, exchange(): lax.all_to_all(blocks, 'tile', split_axis=0, concat_axis=0, tiled=True)  17.5 us
    all_to_all x1, waiting for transfers between devices, exchange(): lax.all_to_all(blocks, 'tile', split_axis=0, concat_axis=0, tiled=True)  8.42 us
    all_to_all x1, starting transfers between devices, exchange(): lax.all_to_all(blocks, 'tile', split_axis=0, concat_axis=0, tiled=True)  3.53 us
    ppermute x1, waiting for transfers between devices, body(): far = lax.ppermute(far, 'tile', off_chip)  2.5 us
    ppermute x1, starting transfers between devices, body(): far = lax.ppermute(far, 'tile', off_chip)  1.7 us
  transfers between devices with their start and end apart: 3, of which 2 were waited for; matrix products, arithmetic and copies ran while one was open for 0% of the time, Pallas kernels for 8%

profile of v7, /device:TPU:0, one launch (start us, length us, event | category | flops | bytes accessed | tf_op | source)
XLA Modules:
  0.0 59.9 jit_solution(12410331567891938727)
XLA Ops:
  0.6 10.1 %shard_map.68 = f32[16,32,128]{2,1,0:T(8,128)} custom-call(f32[32,6912]{1,0:T(8,128)} %inc_ref.1, s32[4,6912]{1,0:T(4,128)} %bitcast.3, f32[4,6912]{1,0:T(4,128)} %weight_ref.2), custom_call_target="tpu_custom_call" | custom-call | tf_op jit(solution)/shard_map/pallas_call | solution.py:339
  10.8 0.0 copy-start.2
  10.8 0.0 copy-start.3
  10.8 17.5 %all_to_all.10.rec_ref = f32[16,32,128]{2,1,0:T(8,128)S(1)} all-to-all(f32[16,32,128]{2,1,0:T(8,128)} %shard_map.68), channel_id=1, replica_groups=mesh['group'=2,'tile'=16] {'tile'}, dimensions={0} | all-to-all | bytes 524288 | tf_op jit(solution)/shard_map/all_to_all | solution.py:430
  28.3 0.0 copy-done.2
  28.3 0.0 copy-done.3
  28.3 1.1 %shard_map.69 = (f32[10,32,256]{2,1,0:T(8,128)S(1)}, f32[8,32,128]{2,1,0:T(8,128)S(1)}, f32[8,32,128]{2,1,0:T(8,128)S(1)}, f32[24,256]{1,0:T(8,128)S(1)}) custom-call(f32[16,32,128]{2,1,0:T(8,128)S(1)} %all_to_all.10.rec_ref, s32[16,128]{1,0:T(8,128)S(1)} %bitcast.5, f32[18,192]{1,0:T(8,128)S(1)} %copy-done.3), custom_call_target="tpu_custom_call" | custom-call | tf_op jit(solution)/shard_map/pallas_call | solution.py:339
  29.4 0.1 collective-permute-start
  29.5 1.7 %collective-permute-start.1 = (f32[8,32,128]{2,1,0:T(8,128)S(1)}, f32[8,32,128]{2,1,0:T(8,128)S(1)}, u32[]{:S(2)}, u32[]{:S(2)}) collective-permute-start(f32[8,32,128]{2,1,0:T(8,128)S(1)} %get-tuple-element.15), channel_id=1, source_target_pairs={{0,15},{1,2},{2,1},{3,4},{4,3},{5,6},{6,5},{7,8},{8,7},{9,10},{10,... | collective-permute-start | bytes 393224 | tf_op jit(solution)/shard_map/ppermute | solution.py:389
  31.2 3.0 %shard_map.70 = (f32[4,4,32,256]{3,2,1,0:T(8,128)S(1)}, f32[8,32,256]{2,1,0:T(8,128)S(1)}, f32[16,32,128]{2,1,0:T(8,128)S(1)}) custom-call(f32[16,32,128]{2,1,0:T(8,128)S(1)} %all_to_all.10.rec_ref, f32[10,32,256]{2,1,0:T(8,128)S(1)} %get-tuple-element.13.edges_ref, f32[24,256]{1,0:T(8,128)S(1)} %get-tuple-element.16.coef_ref.own_ref, s32[16,128]{1,0:T(8,128)S(1)} %bitcast.6), custom_call_target="tpu_custom_call" | custom-call | flops 536870912 | bytes 8388608 | tf_op jit(solution)/shard_map/pallas_call | solution.py:339
  34.1 0.0 collective-permute-done.near_ref
  34.1 2.5 %collective-permute-done.1.far_ref = f32[8,32,128]{2,1,0:T(8,128)S(1)} collective-permute-done((f32[8,32,128]{2,1,0:T(8,128)S(1)}, f32[8,32,128]{2,1,0:T(8,128)S(1)}, u32[]{:S(2)}, u32[]{:S(2)}) %collective-permute-start.1) | collective-permute-done | bytes 131104 | tf_op jit(solution)/shard_map/ppermute | solution.py:389
  36.6 2.9 %shard_map.71 = (f32[10,32,256]{2,1,0:T(8,128)S(1)}, f32[16,32,128]{2,1,0:T(8,128)}) custom-call(f32[10,32,256]{2,1,0:T(8,128)S(1)} %get-tuple-element.13.edges_ref, f32[8,32,128]{2,1,0:T(8,128)S(1)} %collective-permute-done.near_ref, f32[8,32,128]{2,1,0:T(8,128)S(1)} %collective-permute-done.1.far_ref, f32[24,256]{1,0:T(8,128)S(1)} %get-tuple-element.16.coef_ref.own_ref, ...), custom_call_target="tpu_custom_call" | custom-call | tf_op jit(solution)/shard_map/pallas_call | solution.py:339
  39.5 3.5 %all-to-all-start.1 = ((f32[16,32,128]{2,1,0:T(8,128)}), f32[16,32,128]{2,1,0:T(8,128)S(1)}, u32[]{:S(2)}, u32[]{:S(2)}) async-start(f32[16,32,128]{2,1,0:T(8,128)} %get-tuple-element.19), calls=%async_computation.1 | async-start | bytes 524288 | tf_op jit(solution)/shard_map/all_to_all | solution.py:430
  43.1 0.0 copy-start
  43.1 0.0 copy-start.1
  43.1 1.6 %shard_map.72 = f32[18,32,192]{2,1,0:T(8,128)} custom-call(f32[8,32,256]{2,1,0:T(8,128)S(1)} %get-tuple-element.20.inner_ref, f32[10,32,256]{2,1,0:T(8,128)S(1)} %get-tuple-element.21.outer_ref), custom_call_target="tpu_custom_call" | custom-call | flops 147456 | bytes 4194304 | tf_op jit(solution)/shard_map/pallas_call | solution.py:339
  44.7 8.4 %all-to-all-done.1.ret_ref = f32[16,32,128]{2,1,0:T(8,128)S(1)} async-done(((f32[16,32,128]{2,1,0:T(8,128)}), f32[16,32,128]{2,1,0:T(8,128)S(1)}, u32[]{:S(2)}, u32[]{:S(2)}) %all-to-all-start.1) | async-done | bytes 262176 | tf_op jit(solution)/shard_map/all_to_all | solution.py:430
  53.1 0.0 copy-done
  53.1 0.0 copy-done.1
  53.1 6.8 %shard_map.73 = f32[32,6912]{1,0:T(8,128)} custom-call(f32[16,32,128]{2,1,0:T(8,128)S(1)} %all-to-all-done.1.ret_ref, s32[4,6912]{1,0:T(4,128)S(1)} %bitcast.4, f32[4,6912]{1,0:T(4,128)S(1)} %copy-done.1), custom_call_target="tpu_custom_call" | custom-call | tf_op jit(solution)/shard_map/pallas_call | solution.py:339
Async XLA Ops:
  10.8 17.5 %copy-start.2 = (s32[2048]{0:T(1024)S(1)}, s32[2048]{0:T(1024)}, u32[]{:S(2)}) copy-start(s32[2048]{0:T(1024)} %param.8) | copy-start | bytes 24580
  10.8 17.5 %copy-start.3 = (f32[18,192]{1,0:T(8,128)S(1)}, f32[18,192]{1,0:T(8,128)}, u32[]{:S(2)}) copy-start(f32[18,192]{1,0:T(8,128)} %own_ref.1) | copy-start | bytes 41476
  29.4 4.7 %collective-permute-start = (f32[8,32,128]{2,1,0:T(8,128)S(1)}, f32[8,32,128]{2,1,0:T(8,128)S(1)}, u32[]{:S(2)}, u32[]{:S(2)}) collective-permute-start(f32[8,32,128]{2,1,0:T(8,128)S(1)} %get-tuple-element.14), channel_id=1, source_target_pairs={{0,1},{1,0},{2,3},{3,2},{4,5},{5,4},{6,7},{7,6},{8,9},{9,8},{10,11... | collective-permute-start | bytes 393224 | tf_op jit(solution)/shard_map/ppermute | solution.py:390
  29.5 7.2 %collective-permute-start.1 = (f32[8,32,128]{2,1,0:T(8,128)S(1)}, f32[8,32,128]{2,1,0:T(8,128)S(1)}, u32[]{:S(2)}, u32[]{:S(2)}) collective-permute-start(f32[8,32,128]{2,1,0:T(8,128)S(1)} %get-tuple-element.15), channel_id=1, source_target_pairs={{0,15},{1,2},{2,1},{3,4},{4,3},{5,6},{6,5},{7,8},{8,7},{9,10},{10,... | collective-permute-start | bytes 393224 | tf_op jit(solution)/shard_map/ppermute | solution.py:389
  39.5 13.5 %all-to-all-start.1 = ((f32[16,32,128]{2,1,0:T(8,128)}), f32[16,32,128]{2,1,0:T(8,128)S(1)}, u32[]{:S(2)}, u32[]{:S(2)}) async-start(f32[16,32,128]{2,1,0:T(8,128)} %get-tuple-element.19), calls=%async_computation.1 | async-start | bytes 524288 | tf_op jit(solution)/shard_map/all_to_all | solution.py:430
  43.1 10.0 %copy-start = (s32[6912,4]{0,1:T(4,128)S(1)}, s32[6912,4]{0,1:T(4,128)}, u32[]{:S(2)}) copy-start(s32[6912,4]{0,1:T(4,128)} %param.6) | copy-start | bytes 331780
  43.1 10.0 %copy-start.1 = (f32[4,6912]{1,0:T(4,128)S(1)}, f32[4,6912]{1,0:T(4,128)}, u32[]{:S(2)}) copy-start(f32[4,6912]{1,0:T(4,128)} %weight_ref.2) | copy-start | bytes 331780

commit v8 on v6

--- a/solution.py
+++ b/solution.py
@@ -115,20 +115,29 @@
     return list(range(STEPS)) + list(range(rows - STEPS, rows))
 
 
-def sum_edges(rec_ref, cell_ref, coef_ref, edges_ref, near_ref, far_ref, *, width):
+def edge_starts(rows):
+    even = lax.axis_index("tile") % 2 == 0
+    return jnp.where(even, 0, rows - STEPS), jnp.where(even, rows - STEPS, 0)
+
+
+def sum_far(rec_ref, cell_ref, coef_ref, far_rows_ref, far_ref, *, width):
+    start, _ = edge_starts(coef_ref.shape[0])
+    full = cell_sums(rec_ref, cell_ref, [start + k for k in range(STEPS)], width)
+    for k, row in enumerate(full):
+        far_rows_ref[k] = row
+    place_edge(far_ref, full, [coef_ref[pl.ds(start + k, 1), :] for k in range(STEPS)], width)
+
+
+def sum_rest(rec_ref, cell_ref, coef_ref, far_rows_ref, start_ref, near_ref, *, width):
     rows = coef_ref.shape[0]
-    full = cell_sums(rec_ref, cell_ref, edges_of(rows), width)
-    for k, row in enumerate(full):
-        edges_ref[k] = row
-    coefs = [coef_ref[k : k + 1, :] for k in range(rows)]
-    even = lax.axis_index("tile") % 2 == 0
-
-    def place(head_ref, tail_ref):
-        place_edge(head_ref, full[:STEPS], coefs[:STEPS], width)
-        place_edge(tail_ref, full[STEPS:], coefs[rows - STEPS :], width)
-
-    pl.when(even)(lambda: place(far_ref, near_ref))
-    pl.when(jnp.logical_not(even))(lambda: place(near_ref, far_ref))
+    far, near = edge_starts(rows)
+    ys = [near + k for k in range(STEPS)] + list(range(STEPS, rows - STEPS))
+    full = cell_sums(rec_ref, cell_ref, ys, width)
+    for y, row in zip(ys, full):
+        start_ref[y] = row
+    for k in range(STEPS):
+        start_ref[far + k] = far_rows_ref[k]
+    place_edge(near_ref, full[:STEPS], [coef_ref[pl.ds(near + k, 1), :] for k in range(STEPS)], width)
 
 
 def stepped(above, here, below, coef):
@@ -159,16 +168,12 @@
 
 
 def diffuse_inner(
-    rec_ref, edges_ref, own_ref, cell_ref, kept_ref, inner_ref, values_ref, start_ref, one_ref, two_ref, coef_ref, *, width
+    start_ref, own_ref, cell_ref, kept_ref, inner_ref, values_ref, one_ref, two_ref, coef_ref, *, width
 ):
     rows, channels, wide = start_ref.shape
     own = own_ref[...]
     coef_ref[...] = widened([own], own, own, width)
-    for k, y in enumerate(edges_of(rows)):
-        start_ref[y] = edges_ref[k]
     ys = range(STEPS, rows - STEPS)
-    for y, row in zip(ys, cell_sums(rec_ref, cell_ref, ys, width)):
-        start_ref[y] = row
     held, other, last = start_ref, one_ref, two_ref
     for turn in range(1, STEPS + 1):
         for y in range(turn, rows - turn):
@@ -184,7 +189,7 @@
 
 
 def diffuse_outer(
-    edges_ref, near_ref, far_ref, own_ref, cell_ref, kept_ref, part_ref,
+    start_ref, near_ref, far_ref, own_ref, cell_ref, kept_ref, part_ref,
     outer_ref, values_ref, one_ref, two_ref, coef_ref, *, width
 ):
     rows = own_ref.shape[0]
@@ -208,7 +213,7 @@
 
         def row(y):
             if turn == 1 and y - STEPS in ys:
-                return edges_ref[ys.index(y - STEPS)]
+                return start_ref[y - STEPS]
             kept = kept_rows(turn - 1, total) if turn > 1 else []
             return kept_ref[turn - 2, kept.index(y)] if y in kept else held[y]
 
@@ -221,14 +226,6 @@
         outer_ref[k] = row
     base = lambda s: jnp.concatenate([part_ref[s], part_ref[s + 1]], 1)
     read_rows(final, ys, cell_ref, values_ref, base, width)
-
-
-def join_rows(inner_ref, outer_ref, field_ref):
-    rows, _, width = field_ref.shape
-    ys = edges_of(rows)
-    for y in range(rows):
-        row = outer_ref[ys.index(y)] if y in ys else inner_ref[y - STEPS]
-        field_ref[y] = row[:, :width]
 
 
 def by_product(table_ref, slot_ref, weight_ref, columns, channels):
@@ -266,8 +263,19 @@
     return jnp.concatenate(totals, 0)
 
 
-def sum_from_slots(ret_ref, slot_ref, weight_ref, result_ref, table_ref, *, plan):
+def sum_from_slots(
+    ret_ref, slot_ref, weight_ref, inner_ref, outer_ref, result_ref, field_ref, table_ref, *, plan
+):
     blocks, channels, _ = ret_ref.shape
+    some, _, width = field_ref.shape
+    inner = inner_ref.shape[0]
+    for k in range(some):
+        y = pl.program_id(0) * some + k
+        edge = jnp.where(y < STEPS, y, y - inner)
+        is_inner = (y >= STEPS) & (y < STEPS + inner)
+        within = jnp.clip(y - STEPS, 0, inner - 1)
+        row = jnp.where(is_inner, inner_ref[within], outer_ref[jnp.clip(edge, 0, 2 * STEPS - 1)])
+        field_ref[k] = row[:, :width]
     group = PLACES // LANES
 
     @pl.when(pl.program_id(0) == 0)
@@ -303,7 +311,7 @@
         grid=grid,
         out_shape=out,
         in_specs=[in_specs] * len(ins) if single else in_specs,
-        out_specs=[out_specs] * len(out) if isinstance(out, list) else out_specs,
+        out_specs=[out_specs] * len(out) if single and isinstance(out, list) else out_specs,
         scratch_shapes=list(scratch),
         cost_estimate=cost,
         compiler_params=pltpu.CompilerParams(vmem_limit_bytes=memory << 20),
@@ -341,42 +349,46 @@
     edge = shape((EDGE, channels, LANES), F32)
     slot_blocks = shape((blocks, channels, LANES), F32)
     edge_rows = shape((2 * STEPS, channels, wide), F32)
-    edges, near, far = call(
-        functools.partial(sum_edges, width=width), (received, cells, diffusivity), [edge_rows, edge, edge]
+    far_rows, far = call(
+        functools.partial(sum_far, width=width),
+        (received, cells, diffusivity),
+        [shape((STEPS, channels, wide), F32), edge],
     )
     far = lax.ppermute(far, "tile", off_chip)
+    start, near = call(
+        functools.partial(sum_rest, width=width),
+        (received, cells, diffusivity, far_rows),
+        [shape((rows, channels, wide), F32), edge],
+        cost=pl.CostEstimate(flops=2 * slot_count * wide * wide, bytes_accessed=4 << 20, transcendentals=0),
+    )
     near = lax.ppermute(near, "tile", on_chip)
     own = pltpu.VMEM((rows, channels, wide), F32)
     kept, inner, found = call(
         functools.partial(diffuse_inner, width=width),
-        (received, edges, diffusivity, cells),
+        (start, diffusivity, cells),
         [shape((STEPS - 1, 4, channels, wide), F32), shape((rows - 2 * STEPS, channels, wide), F32), slot_blocks],
-        [own, own, own, pltpu.VMEM((rows, wide), F32)],
+        [own, own, pltpu.VMEM((rows, wide), F32)],
         cost=pl.CostEstimate(flops=4 * slot_count * wide * wide, bytes_accessed=8 << 20, transcendentals=0),
     )
     padded = pltpu.VMEM((rows + 2 * STEPS, channels, wide), F32)
     outer, values = call(
         functools.partial(diffuse_outer, width=width),
-        (edges, near, far, diffusivity, cells, kept, found),
+        (start, near, far, diffusivity, cells, kept, found),
         [edge_rows, slot_blocks],
         [padded, padded, pltpu.VMEM((rows + 2 * STEPS, wide), F32)],
     )
-    field = call(
-        join_rows,
-        (inner, outer),
-        shape((rows, channels, width), F32),
-        cost=pl.CostEstimate(flops=rows * channels * wide, bytes_accessed=4 << 20, transcendentals=0),
-    )
     returned = exchange(values, tiles, share)
-    field, tent_weight = lax.optimization_barrier((field, tent_weight))
-    result = call(
+    turns = fine // chunk
+    some = rows // turns if rows % turns == 0 else rows
+    all_of = lambda count: pl.BlockSpec((count, channels, wide), lambda i: (0, 0, 0))
+    result, field = call(
         functools.partial(sum_from_slots, plan=plan_of(chunk // LANES)),
-        (returned, slots, tent_weight),
-        shape((channels, fine), F32),
+        (returned, slots, tent_weight, inner, outer),
+        [shape((channels, fine), F32), shape((rows, channels, width), F32)],
         [pltpu.VMEM((2 * channels * slot_count // PLACES, PLACES), BF16)],
         grid=grid,
-        in_specs=[whole, part(CORNERS), part(CORNERS)],
-        out_specs=part(channels),
+        in_specs=[whole, part(CORNERS), part(CORNERS), all_of(rows - 2 * STEPS), all_of(2 * STEPS)],
+        out_specs=[part(channels), pl.BlockSpec((some, channels, width), lambda i: (i, 0, 0))],
         memory=32,
     )
     return (result, field.transpose(1, 0, 2))

time: 59.9 us -> 58.1 us (0.970)
  blocking collectives: 17.5 us -> 30.3 us
  waiting for transfers between devices: 11.3 us -> 2.72 us
  starting transfers between devices: 5.3 us -> 1.49 us
  Pallas kernels: 24.7 us -> 22.6 us
    all_to_all x1 -> x2, blocking collectives: 17.5 us -> 30.3 us  [exchange(): lax.all_to_all(blocks, 'tile', split_axis=0, concat_axis=0, tiled=True)]
    all_to_all x1 -> x0, waiting for transfers between devices: 9.13 us -> none  [exchange(): lax.all_to_all(blocks, 'tile', split_axis=0, concat_axis=0, tiled=True)]
    all_to_all x1 -> x0, starting transfers between devices: 3.53 us -> none  [exchange(): lax.all_to_all(blocks, 'tile', split_axis=0, concat_axis=0, tiled=True)]
    pallas_call x6, Pallas kernels: 24.7 us -> 22.6 us  [call(): pl.pallas_call(kernel, grid=grid, out_shape=out, in_specs=[in_specs] * le...]
  transfers between devices with their start and end apart: 3 -> 2, of which waited for: 2 -> 1; matrix products, arithmetic and copies ran while one was open for 0% -> 0% of each run, Pallas kernels for 7% -> 5%
where the time goes in v8:
time: 58.1 us; the launch traced here: 57.8 us
  blocking collectives  30.3 us (52%)
  Pallas kernels  22.6 us (39%)
  waiting for transfers between devices  2.72 us (5%)
  starting transfers between devices  1.49 us (3%)
  between operations  0.67 us (1%)
    all_to_all x2, blocking collectives, exchange(): lax.all_to_all(blocks, 'tile', split_axis=0, concat_axis=0, tiled=True)  30.3 us
    pallas_call x6, Pallas kernels, call(): pl.pallas_call(kernel, grid=grid, out_shape=out, in_specs=[in_specs] * le...  22.6 us
    ppermute x1, waiting for transfers between devices, body(): far = lax.ppermute(far, 'tile', off_chip)  2.72 us
    ppermute x1, starting transfers between devices, body(): far = lax.ppermute(far, 'tile', off_chip)  1.42 us
  transfers between devices with their start and end apart: 2, of which 1 were waited for; matrix products, arithmetic and copies ran while one was open for 0% of the time, Pallas kernels for 5%

profile of v8, /device:TPU:0, one launch (start us, length us, event | category | flops | bytes accessed | tf_op | source)
XLA Modules:
  0.0 57.8 jit_solution(967348989074480015)
XLA Ops:
  0.6 10.1 %shard_map.68 = f32[16,32,128]{2,1,0:T(8,128)} custom-call(f32[32,6912]{1,0:T(8,128)} %inc_ref.1, s32[4,6912]{1,0:T(4,128)} %bitcast.3, f32[4,6912]{1,0:T(4,128)} %weight_ref.3), custom_call_target="tpu_custom_call" | custom-call | tf_op jit(solution)/shard_map/pallas_call | solution.py:309
  10.8 0.0 copy-start.2
  10.8 0.0 copy-start.3
  10.8 17.5 %all_to_all.10.rec_ref = f32[16,32,128]{2,1,0:T(8,128)S(1)} all-to-all(f32[16,32,128]{2,1,0:T(8,128)} %shard_map.68), channel_id=1, replica_groups=mesh['group'=2,'tile'=16] {'tile'}, dimensions={0} | all-to-all | bytes 524288 | tf_op jit(solution)/shard_map/all_to_all | solution.py:400
  28.3 0.0 copy-done.2
  28.3 0.0 copy-done.3
  28.3 0.6 %shard_map.69 = (f32[5,32,256]{2,1,0:T(8,128)S(1)}, f32[8,32,128]{2,1,0:T(8,128)S(1)}) custom-call(f32[16,32,128]{2,1,0:T(8,128)S(1)} %all_to_all.10.rec_ref, s32[16,128]{1,0:T(8,128)S(1)} %bitcast.5, f32[18,192]{1,0:T(8,128)S(1)} %copy-done.2), custom_call_target="tpu_custom_call" | custom-call | tf_op jit(solution)/shard_map/pallas_call | solution.py:309
  28.9 1.4 %collective-permute-start.1 = (f32[8,32,128]{2,1,0:T(8,128)S(1)}, f32[8,32,128]{2,1,0:T(8,128)S(1)}, u32[]{:S(2)}, u32[]{:S(2)}) collective-permute-start(f32[8,32,128]{2,1,0:T(8,128)S(1)} %get-tuple-element.16), channel_id=1, source_target_pairs={{0,15},{1,2},{2,1},{3,4},{4,3},{5,6},{6,5},{7,8},{8,7},{9,10},{10,... | collective-permute-start | bytes 393224 | tf_op jit(solution)/shard_map/ppermute | solution.py:357
  30.3 1.1 %shard_map.70 = (f32[18,32,256]{2,1,0:T(8,128)S(1)}, f32[8,32,128]{2,1,0:T(8,128)S(1)}) custom-call(f32[16,32,128]{2,1,0:T(8,128)S(1)} %all_to_all.10.rec_ref, s32[16,128]{1,0:T(8,128)S(1)} %bitcast.6, f32[18,192]{1,0:T(8,128)S(1)} %copy-done.2, f32[5,32,256]{2,1,0:T(8,128)S(1)} %get-tuple-element.13.far_rows_ref), custom_call_target="tpu_custom_call" | custom-call | flops 268435456 | bytes 4194304 | tf_op jit(solution)/shard_map/pallas_call | solution.py:309
  31.4 0.1 collective-permute-start
  31.5 1.8 %shard_map.71 = (f32[4,4,32,256]{3,2,1,0:T(8,128)S(1)}, f32[8,32,256]{2,1,0:T(8,128)S(1)}, f32[16,32,128]{2,1,0:T(8,128)S(1)}) custom-call(f32[18,32,256]{2,1,0:T(8,128)S(1)} %get-tuple-element.14.start_ref, f32[18,192]{1,0:T(8,128)S(1)} %copy-done.2, s32[16,128]{1,0:T(8,128)S(1)} %bitcast.7), custom_call_target="tpu_custom_call" | custom-call | flops 536870912 | bytes 8388608 | tf_op jit(solution)/shard_map/pallas_call | solution.py:309
  33.3 2.7 %collective-permute-done.1.far_ref = f32[8,32,128]{2,1,0:T(8,128)S(1)} collective-permute-done((f32[8,32,128]{2,1,0:T(8,128)S(1)}, f32[8,32,128]{2,1,0:T(8,128)S(1)}, u32[]{:S(2)}, u32[]{:S(2)}) %collective-permute-start.1) | collective-permute-done | bytes 131104 | tf_op jit(solution)/shard_map/ppermute | solution.py:357
  36.1 0.0 collective-permute-done.near_ref
  36.1 1.9 %shard_map.72 = (f32[10,32,256]{2,1,0:T(8,128)S(1)}, f32[16,32,128]{2,1,0:T(8,128)S(1)}) custom-call(f32[18,32,256]{2,1,0:T(8,128)S(1)} %get-tuple-element.14.start_ref, f32[8,32,128]{2,1,0:T(8,128)S(1)} %collective-permute-done.near_ref, f32[8,32,128]{2,1,0:T(8,128)S(1)} %collective-permute-done.1.far_ref, f32[18,192]{1,0:T(8,128)S(1)} %copy-done.2, ...), custom_call_target="tpu_custom_call" | custom-call | tf_op jit(solution)/shard_map/pallas_call | solution.py:309
  38.0 0.0 copy-start
  38.0 0.0 copy-start.1
  38.0 12.8 %all_to_all.11.ret_ref = f32[16,32,128]{2,1,0:T(8,128)S(1)} all-to-all(f32[16,32,128]{2,1,0:T(8,128)S(1)} %get-tuple-element.19), channel_id=1, replica_groups=mesh['group'=2,'tile'=16] {'tile'}, dimensions={0} | all-to-all | bytes 524288 | tf_op jit(solution)/shard_map/all_to_all | solution.py:400
  50.8 0.0 copy-done
  50.8 0.0 copy-done.1
  50.8 7.0 %shard_map.73 = (f32[32,6912]{1,0:T(8,128)}, f32[18,32,192]{2,1,0:T(8,128)}) custom-call(f32[16,32,128]{2,1,0:T(8,128)S(1)} %all_to_all.11.ret_ref, s32[4,6912]{1,0:T(4,128)S(1)} %bitcast.4, f32[4,6912]{1,0:T(4,128)S(1)} %copy-done.1, f32[8,32,256]{2,1,0:T(8,128)S(1)} %get-tuple-element.20.inner_ref, f32[10,32,256]{2,1,0:T(8,128)S(1)} %get-tuple-element.21.outer_ref), custom_call_target="tpu_custom_call" | custom-call | tf_op jit(solution)/shard_map/pallas_call | solution.py:309
Async XLA Ops:
  10.8 17.5 %copy-start.2 = (f32[18,192]{1,0:T(8,128)S(1)}, f32[18,192]{1,0:T(8,128)}, u32[]{:S(2)}) copy-start(f32[18,192]{1,0:T(8,128)} %own_ref.3) | copy-start | bytes 41476
  10.8 17.5 %copy-start.3 = (s32[2048]{0:T(1024)S(1)}, s32[2048]{0:T(1024)}, u32[]{:S(2)}) copy-start(s32[2048]{0:T(1024)} %param.8) | copy-start | bytes 24580
  28.9 7.1 %collective-permute-start.1 = (f32[8,32,128]{2,1,0:T(8,128)S(1)}, f32[8,32,128]{2,1,0:T(8,128)S(1)}, u32[]{:S(2)}, u32[]{:S(2)}) collective-permute-start(f32[8,32,128]{2,1,0:T(8,128)S(1)} %get-tuple-element.16), channel_id=1, source_target_pairs={{0,15},{1,2},{2,1},{3,4},{4,3},{5,6},{6,5},{7,8},{8,7},{9,10},{10,... | collective-permute-start | bytes 393224 | tf_op jit(solution)/shard_map/ppermute | solution.py:357
  31.4 4.6 %collective-permute-start = (f32[8,32,128]{2,1,0:T(8,128)S(1)}, f32[8,32,128]{2,1,0:T(8,128)S(1)}, u32[]{:S(2)}, u32[]{:S(2)}) collective-permute-start(f32[8,32,128]{2,1,0:T(8,128)S(1)} %get-tuple-element.15), channel_id=1, source_target_pairs={{0,1},{1,0},{2,3},{3,2},{4,5},{5,4},{6,7},{7,6},{8,9},{9,8},{10,11... | collective-permute-start | bytes 393224 | tf_op jit(solution)/shard_map/ppermute | solution.py:364
  38.0 12.8 %copy-start = (s32[6912,4]{0,1:T(4,128)S(1)}, s32[6912,4]{0,1:T(4,128)}, u32[]{:S(2)}) copy-start(s32[6912,4]{0,1:T(4,128)} %param.6) | copy-start | bytes 331780
  38.0 12.8 %copy-start.1 = (f32[4,6912]{1,0:T(4,128)S(1)}, f32[4,6912]{1,0:T(4,128)}, u32[]{:S(2)}) copy-start(f32[4,6912]{1,0:T(4,128)} %weight_ref.3) | copy-start | bytes 331780

commit v9 on v8

--- a/solution.py
+++ b/solution.py
@@ -111,33 +111,20 @@
     return full
 
 
-def edges_of(rows):
-    return list(range(STEPS)) + list(range(rows - STEPS, rows))
-
-
 def edge_starts(rows):
     even = lax.axis_index("tile") % 2 == 0
     return jnp.where(even, 0, rows - STEPS), jnp.where(even, rows - STEPS, 0)
 
 
-def sum_far(rec_ref, cell_ref, coef_ref, far_rows_ref, far_ref, *, width):
-    start, _ = edge_starts(coef_ref.shape[0])
-    full = cell_sums(rec_ref, cell_ref, [start + k for k in range(STEPS)], width)
+def sum_edges(rec_ref, cell_ref, coef_ref, edges_ref, far_ref, near_ref, *, width):
+    starts = edge_starts(coef_ref.shape[0])
+    ys = [start + k for start in starts for k in range(STEPS)]
+    full = cell_sums(rec_ref, cell_ref, ys, width)
     for k, row in enumerate(full):
-        far_rows_ref[k] = row
-    place_edge(far_ref, full, [coef_ref[pl.ds(start + k, 1), :] for k in range(STEPS)], width)
-
-
-def sum_rest(rec_ref, cell_ref, coef_ref, far_rows_ref, start_ref, near_ref, *, width):
-    rows = coef_ref.shape[0]
-    far, near = edge_starts(rows)
-    ys = [near + k for k in range(STEPS)] + list(range(STEPS, rows - STEPS))
-    full = cell_sums(rec_ref, cell_ref, ys, width)
-    for y, row in zip(ys, full):
-        start_ref[y] = row
-    for k in range(STEPS):
-        start_ref[far + k] = far_rows_ref[k]
-    place_edge(near_ref, full[:STEPS], [coef_ref[pl.ds(near + k, 1), :] for k in range(STEPS)], width)
+        edges_ref[k] = row
+    for edge_ref, at in ((far_ref, 0), (near_ref, STEPS)):
+        coefs = [coef_ref[pl.ds(y, 1), :] for y in ys[at : at + STEPS]]
+        place_edge(edge_ref, full[at : at + STEPS], coefs, width)
 
 
 def stepped(above, here, below, coef):
@@ -167,13 +154,10 @@
         values_ref[s + 1] = out[:, LANES:]
 
 
-def diffuse_inner(
-    start_ref, own_ref, cell_ref, kept_ref, inner_ref, values_ref, one_ref, two_ref, coef_ref, *, width
-):
-    rows, channels, wide = start_ref.shape
+def inner_rows(start_ref, own_ref, kept_ref, one_ref, two_ref, coef_ref, width):
+    rows = start_ref.shape[0]
     own = own_ref[...]
     coef_ref[...] = widened([own], own, own, width)
-    ys = range(STEPS, rows - STEPS)
     held, other, last = start_ref, one_ref, two_ref
     for turn in range(1, STEPS + 1):
         for y in range(turn, rows - turn):
@@ -182,50 +166,70 @@
             for place, y in enumerate(kept_rows(turn, rows + 2 * STEPS)):
                 kept_ref[turn - 1, place] = other[y - STEPS]
         held, other, last = other, last, other
-    for y in ys:
-        inner_ref[y - STEPS] = held[y]
-    nothing = lambda s: jnp.zeros((channels, 2 * LANES), F32)
-    read_rows([held[y] for y in ys], ys, cell_ref, values_ref, nothing, width)
-
-
-def diffuse_outer(
-    start_ref, near_ref, far_ref, own_ref, cell_ref, kept_ref, part_ref,
-    outer_ref, values_ref, one_ref, two_ref, coef_ref, *, width
-):
+    return [held[y] for y in range(STEPS, rows - STEPS)]
+
+
+def side_rows(start_ref, edge_ref, own_ref, kept_ref, one_ref, two_ref, coef_ref, width, first):
     rows = own_ref.shape[0]
-    total = rows + 2 * STEPS
-    own = own_ref[...]
-    coef_ref[STEPS : STEPS + rows, :] = widened([own], own, own, width)
-    even = lax.axis_index("tile") % 2 == 0
-
-    def read(before_ref, after_ref):
-        for k in range(STEPS):
-            one_ref[k] = read_edge(before_ref, k, width)
-            one_ref[STEPS + rows + k] = read_edge(after_ref, k, width)
-            coef_ref[k : k + 1, :] = read_coef(before_ref, k, width)
-            coef_ref[STEPS + rows + k : STEPS + rows + k + 1, :] = read_coef(after_ref, k, width)
-
-    pl.when(even)(lambda: read(far_ref, near_ref))
-    pl.when(jnp.logical_not(even))(lambda: read(near_ref, far_ref))
-    ys = edges_of(rows)
+    head = first == 0
+    flip = lambda ahead, behind: jnp.where(head, ahead, behind)
+    for k in range(STEPS):
+        place = flip(k, STEPS - 1 - k)
+        one_ref[place] = read_edge(edge_ref, k, width)
+        coef_ref[pl.ds(place, 1), :] = read_coef(edge_ref, k, width)
+        own = own_ref[pl.ds(flip(k, rows - 1 - k), 1), :]
+        coef_ref[STEPS + k : STEPS + k + 1, :] = widened([own], own, own, width)
     held, other = one_ref, two_ref
     for turn in range(1, STEPS + 1):
 
-        def row(y):
-            if turn == 1 and y - STEPS in ys:
-                return start_ref[y - STEPS]
-            kept = kept_rows(turn - 1, total) if turn > 1 else []
-            return kept_ref[turn - 2, kept.index(y)] if y in kept else held[y]
-
-        for start in (turn, total - STEPS - turn):
-            for y in range(start, start + STEPS):
-                other[y] = stepped(row(y - 1), row(y), row(y + 1), coef_ref[y : y + 1, :])
+        def row(u):
+            if turn == 1 and u >= STEPS:
+                return start_ref[flip(u - STEPS, rows - 1 - u + STEPS)]
+            if u >= STEPS + turn - 1:
+                k = u - STEPS - turn + 1
+                return kept_ref[turn - 2, flip(k, 3 - k)]
+            return held[u]
+
+        for u in range(turn, turn + STEPS):
+            other[u] = stepped(row(u - 1), row(u), row(u + 1), coef_ref[u : u + 1, :])
         held, other = other, held
-    final = [held[y + STEPS] for y in ys]
-    for k, row in enumerate(final):
-        outer_ref[k] = row
+    return [held[flip(STEPS + k, 2 * STEPS - 1 - k)] for k in range(STEPS)]
+
+
+def diffuse_most(
+    rec_ref, edges_ref, edge_ref, own_ref, cell_ref, start_ref, kept_ref, inner_ref, side_ref, values_ref,
+    one_ref, two_ref, coef_ref, side_one_ref, side_two_ref, side_coef_ref, *, width
+):
+    rows, channels, _ = start_ref.shape
+    far, first = edge_starts(rows)
+    for k in range(STEPS):
+        start_ref[far + k] = edges_ref[k]
+        start_ref[first + k] = edges_ref[STEPS + k]
+    within = range(STEPS, rows - STEPS)
+    for y, row in zip(within, cell_sums(rec_ref, cell_ref, within, width)):
+        start_ref[y] = row
+    inner = inner_rows(start_ref, own_ref, kept_ref, one_ref, two_ref, coef_ref, width)
+    side = side_rows(
+        start_ref, edge_ref, own_ref, kept_ref, side_one_ref, side_two_ref, side_coef_ref, width, first
+    )
+    for k, row in enumerate(inner):
+        inner_ref[k] = row
+    for k, row in enumerate(side):
+        side_ref[k] = row
+    ys = list(range(STEPS, rows - STEPS)) + [first + k for k in range(STEPS)]
+    nothing = lambda s: jnp.zeros((channels, 2 * LANES), F32)
+    read_rows(inner + side, ys, cell_ref, values_ref, nothing, width)
+
+
+def diffuse_last(
+    kept_ref, part_ref, start_ref, edge_ref, own_ref, cell_ref, side_ref, values_ref, one_ref, two_ref, coef_ref, *, width
+):
+    first, _ = edge_starts(own_ref.shape[0])
+    side = side_rows(start_ref, edge_ref, own_ref, kept_ref, one_ref, two_ref, coef_ref, width, first)
+    for k, row in enumerate(side):
+        side_ref[k] = row
     base = lambda s: jnp.concatenate([part_ref[s], part_ref[s + 1]], 1)
-    read_rows(final, ys, cell_ref, values_ref, base, width)
+    read_rows(side, [first + k for k in range(STEPS)], cell_ref, values_ref, base, width)
 
 
 def by_product(table_ref, slot_ref, weight_ref, columns, channels):
@@ -264,17 +268,18 @@
 
 
 def sum_from_slots(
-    ret_ref, slot_ref, weight_ref, inner_ref, outer_ref, result_ref, field_ref, table_ref, *, plan
+    ret_ref, slot_ref, weight_ref, inner_ref, near_ref, far_ref, result_ref, field_ref, table_ref, *, plan
 ):
     blocks, channels, _ = ret_ref.shape
     some, _, width = field_ref.shape
     inner = inner_ref.shape[0]
+    far, _ = edge_starts(inner + 2 * STEPS)
     for k in range(some):
         y = pl.program_id(0) * some + k
-        edge = jnp.where(y < STEPS, y, y - inner)
+        at = jnp.clip(jnp.where(y < STEPS, y, y - STEPS - inner), 0, STEPS - 1)
         is_inner = (y >= STEPS) & (y < STEPS + inner)
-        within = jnp.clip(y - STEPS, 0, inner - 1)
-        row = jnp.where(is_inner, inner_ref[within], outer_ref[jnp.clip(edge, 0, 2 * STEPS - 1)])
+        edge = jnp.where((y < STEPS) == (far == 0), far_ref[at], near_ref[at])
+        row = jnp.where(is_inner, inner_ref[jnp.clip(y - STEPS, 0, inner - 1)], edge)
         field_ref[k] = row[:, :width]
     group = PLACES // LANES
 
@@ -348,34 +353,35 @@
     received = exchange(sent, tiles, share)
     edge = shape((EDGE, channels, LANES), F32)
     slot_blocks = shape((blocks, channels, LANES), F32)
-    edge_rows = shape((2 * STEPS, channels, wide), F32)
-    far_rows, far = call(
-        functools.partial(sum_far, width=width),
+    edges, far, near = call(
+        functools.partial(sum_edges, width=width),
         (received, cells, diffusivity),
-        [shape((STEPS, channels, wide), F32), edge],
+        [shape((2 * STEPS, channels, wide), F32), edge, edge],
     )
     far = lax.ppermute(far, "tile", off_chip)
-    start, near = call(
-        functools.partial(sum_rest, width=width),
-        (received, cells, diffusivity, far_rows),
-        [shape((rows, channels, wide), F32), edge],
-        cost=pl.CostEstimate(flops=2 * slot_count * wide * wide, bytes_accessed=4 << 20, transcendentals=0),
-    )
     near = lax.ppermute(near, "tile", on_chip)
     own = pltpu.VMEM((rows, channels, wide), F32)
-    kept, inner, found = call(
-        functools.partial(diffuse_inner, width=width),
-        (start, diffusivity, cells),
-        [shape((STEPS - 1, 4, channels, wide), F32), shape((rows - 2 * STEPS, channels, wide), F32), slot_blocks],
-        [own, own, pltpu.VMEM((rows, wide), F32)],
+    ends = shape((STEPS, channels, wide), F32)
+    side = pltpu.VMEM((2 * STEPS + 1, channels, wide), F32)
+    side_scratch = [side, side, pltpu.VMEM((2 * STEPS, wide), F32)]
+    start, kept, inner, near_last, found = call(
+        functools.partial(diffuse_most, width=width),
+        (received, edges, near, diffusivity, cells),
+        [
+            shape((rows, channels, wide), F32),
+            shape((STEPS - 1, 4, channels, wide), F32),
+            shape((rows - 2 * STEPS, channels, wide), F32),
+            ends,
+            slot_blocks,
+        ],
+        [own, own, pltpu.VMEM((rows, wide), F32)] + side_scratch,
         cost=pl.CostEstimate(flops=4 * slot_count * wide * wide, bytes_accessed=8 << 20, transcendentals=0),
     )
-    padded = pltpu.VMEM((rows + 2 * STEPS, channels, wide), F32)
-    outer, values = call(
-        functools.partial(diffuse_outer, width=width),
-        (start, near, far, diffusivity, cells, kept, found),
-        [edge_rows, slot_blocks],
-        [padded, padded, pltpu.VMEM((rows + 2 * STEPS, wide), F32)],
+    far_last, values = call(
+        functools.partial(diffuse_last, width=width),
+        (kept, found, start, far, diffusivity, cells),
+        [ends, slot_blocks],
+        side_scratch,
     )
     returned = exchange(values, tiles, share)
     turns = fine // chunk
@@ -383,11 +389,11 @@
     all_of = lambda count: pl.BlockSpec((count, channels, wide), lambda i: (0, 0, 0))
     result, field = call(
         functools.partial(sum_from_slots, plan=plan_of(chunk // LANES)),
-        (returned, slots, tent_weight, inner, outer),
+        (returned, slots, tent_weight, inner, near_last, far_last),
         [shape((channels, fine), F32), shape((rows, channels, width), F32)],
         [pltpu.VMEM((2 * channels * slot_count // PLACES, PLACES), BF16)],
         grid=grid,
-        in_specs=[whole, part(CORNERS), part(CORNERS), all_of(rows - 2 * STEPS), all_of(2 * STEPS)],
+        in_specs=[whole, part(CORNERS), part(CORNERS), all_of(rows - 2 * STEPS), all_of(STEPS), all_of(STEPS)],
         out_specs=[part(channels), pl.BlockSpec((some, channels, width), lambda i: (i, 0, 0))],
         memory=32,
     )

time: 58.1 us -> 58 us (level)
  waiting for transfers between devices: 2.72 us -> 1.6 us
    ppermute x1, waiting for transfers between devices: 2.72 us -> 1.6 us  [body(): far = lax.ppermute(far, 'tile', off_chip)]
    pallas_call x6 -> x5, Pallas kernels: 22.6 us -> 23.1 us  [call(): pl.pallas_call(kernel, grid=grid, out_shape=out, in_specs=[in_specs] * le...]
  transfers between devices with their start and end apart: 2 -> 2, of which waited for: 1 -> 1; matrix products, arithmetic and copies ran while one was open for 0% -> 0% of each run, Pallas kernels for 5% -> 7%
where the time goes in v9:
time: 58 us; the launch traced here: 57.6 us
  blocking collectives  30.5 us (53%)
  Pallas kernels  23.1 us (40%)
  starting transfers between devices  1.74 us (3%)
  waiting for transfers between devices  1.6 us (3%)
  between operations  0.66 us (1%)
    all_to_all x2, blocking collectives, exchange(): lax.all_to_all(blocks, 'tile', split_axis=0, concat_axis=0, tiled=True)  30.5 us
    pallas_call x5, Pallas kernels, call(): pl.pallas_call(kernel, grid=grid, out_shape=out, in_specs=[in_specs] * le...  23.1 us
    ppermute x1, starting transfers between devices, body(): far = lax.ppermute(far, 'tile', off_chip)  1.69 us
    ppermute x1, waiting for transfers between devices, body(): far = lax.ppermute(far, 'tile', off_chip)  1.6 us
  transfers between devices with their start and end apart: 2, of which 1 were waited for; matrix products, arithmetic and copies ran while one was open for 0% of the time, Pallas kernels for 7%

profile of v9, /device:TPU:0, one launch (start us, length us, event | category | flops | bytes accessed | tf_op | source)
XLA Modules:
  0.0 57.6 jit_solution(6507551288225065583)
XLA Ops:
  0.6 10.1 %shard_map.68 = f32[16,32,128]{2,1,0:T(8,128)} custom-call(f32[32,6912]{1,0:T(8,128)} %inc_ref.1, s32[4,6912]{1,0:T(4,128)} %bitcast.3, f32[4,6912]{1,0:T(4,128)} %weight_ref.3), custom_call_target="tpu_custom_call" | custom-call | tf_op jit(solution)/shard_map/pallas_call | solution.py:314
  10.8 0.0 copy-start.2
  10.8 0.0 copy-start.3
  10.8 17.5 %all_to_all.10.rec_ref = f32[16,32,128]{2,1,0:T(8,128)S(1)} all-to-all(f32[16,32,128]{2,1,0:T(8,128)} %shard_map.68), channel_id=1, replica_groups=mesh['group'=2,'tile'=16] {'tile'}, dimensions={0} | all-to-all | bytes 524288 | tf_op jit(solution)/shard_map/all_to_all | solution.py:406
  28.3 0.0 copy-done.2
  28.3 0.0 copy-done.3
  28.3 1.0 %shard_map.69 = (f32[10,32,256]{2,1,0:T(8,128)S(1)}, f32[8,32,128]{2,1,0:T(8,128)S(1)}, f32[8,32,128]{2,1,0:T(8,128)S(1)}) custom-call(f32[16,32,128]{2,1,0:T(8,128)S(1)} %all_to_all.10.rec_ref, s32[16,128]{1,0:T(8,128)S(1)} %bitcast.5, f32[18,192]{1,0:T(8,128)S(1)} %copy-done.2), custom_call_target="tpu_custom_call" | custom-call | tf_op jit(solution)/shard_map/pallas_call | solution.py:314
  29.3 0.0 collective-permute-start
  29.3 1.7 %collective-permute-start.1 = (f32[8,32,128]{2,1,0:T(8,128)S(1)}, f32[8,32,128]{2,1,0:T(8,128)S(1)}, u32[]{:S(2)}, u32[]{:S(2)}) collective-permute-start(f32[8,32,128]{2,1,0:T(8,128)S(1)} %get-tuple-element.19), channel_id=1, source_target_pairs={{0,15},{1,2},{2,1},{3,4},{4,3},{5,6},{6,5},{7,8},{8,7},{9,10},{10,... | collective-permute-start | bytes 393224 | tf_op jit(solution)/shard_map/ppermute | solution.py:361
  31.0 0.0 collective-permute-done.edge_ref
  31.0 3.9 %shard_map.70 = (f32[18,32,256]{2,1,0:T(8,128)S(1)}, f32[4,4,32,256]{3,2,1,0:T(8,128)S(1)}, f32[8,32,256]{2,1,0:T(8,128)S(1)}, f32[5,32,256]{2,1,0:T(8,128)S(1)}, f32[16,32,128]{2,1,0:T(8,128)S(1)}) custom-call(f32[16,32,128]{2,1,0:T(8,128)S(1)} %all_to_all.10.rec_ref, f32[10,32,256]{2,1,0:T(8,128)S(1)} %get-tuple-element.14.edges_ref, ...), custom_call_target="tpu_custom_call" | custom-call | flops 536870912 | bytes 8388608 | tf_op jit(solution)/shard_map/pallas_call | solution.py:314
  34.9 1.6 %collective-permute-done.1.edge_ref = f32[8,32,128]{2,1,0:T(8,128)S(1)} collective-permute-done((f32[8,32,128]{2,1,0:T(8,128)S(1)}, f32[8,32,128]{2,1,0:T(8,128)S(1)}, u32[]{:S(2)}, u32[]{:S(2)}) %collective-permute-start.1) | collective-permute-done | bytes 131104 | tf_op jit(solution)/shard_map/ppermute | solution.py:361
  36.5 1.1 %shard_map.71 = (f32[5,32,256]{2,1,0:T(8,128)S(1)}, f32[16,32,128]{2,1,0:T(8,128)S(1)}) custom-call(f32[4,4,32,256]{3,2,1,0:T(8,128)S(1)} %get-tuple-element.16.kept_ref, f32[16,32,128]{2,1,0:T(8,128)S(1)} %get-tuple-element.17.part_ref, f32[18,32,256]{2,1,0:T(8,128)S(1)} %get-tuple-element.18.start_ref, f32[8,32,128]{2,1,0:T(8,128)S(1)} %collective-permute-done.1.edge_ref, ...), custom_call_target="tpu_custom_call" | custom-call | tf_op jit(solution)/shard_map/pallas_call | solution.py:314
  37.6 0.0 copy-start
  37.6 0.0 copy-start.1
  37.6 13.0 %all_to_all.11.ret_ref = f32[16,32,128]{2,1,0:T(8,128)S(1)} all-to-all(f32[16,32,128]{2,1,0:T(8,128)S(1)} %get-tuple-element.20), channel_id=1, replica_groups=mesh['group'=2,'tile'=16] {'tile'}, dimensions={0} | all-to-all | bytes 524288 | tf_op jit(solution)/shard_map/all_to_all | solution.py:406
  50.6 0.0 copy-done
  50.6 0.0 copy-done.1
  50.6 7.0 %shard_map.72 = (f32[32,6912]{1,0:T(8,128)}, f32[18,32,192]{2,1,0:T(8,128)}) custom-call(f32[16,32,128]{2,1,0:T(8,128)S(1)} %all_to_all.11.ret_ref, s32[4,6912]{1,0:T(4,128)S(1)} %bitcast.4, f32[4,6912]{1,0:T(4,128)S(1)} %copy-done.1, f32[8,32,256]{2,1,0:T(8,128)S(1)} %get-tuple-element.21.inner_ref, f32[5,32,256]{2,1,0:T(8,128)S(1)} %get-tuple-element.22.near_ref, ...), custom_call_target="tpu_custom_call" | custom-call | tf_op jit(solution)/shard_map/pallas_call | solution.py:314
Async XLA Ops:
  10.8 17.5 %copy-start.2 = (f32[18,192]{1,0:T(8,128)S(1)}, f32[18,192]{1,0:T(8,128)}, u32[]{:S(2)}) copy-start(f32[18,192]{1,0:T(8,128)} %own_ref.3) | copy-start | bytes 41476
  10.8 17.5 %copy-start.3 = (s32[2048]{0:T(1024)S(1)}, s32[2048]{0:T(1024)}, u32[]{:S(2)}) copy-start(s32[2048]{0:T(1024)} %param.8) | copy-start | bytes 24580
  29.3 1.8 %collective-permute-start = (f32[8,32,128]{2,1,0:T(8,128)S(1)}, f32[8,32,128]{2,1,0:T(8,128)S(1)}, u32[]{:S(2)}, u32[]{:S(2)}) collective-permute-start(f32[8,32,128]{2,1,0:T(8,128)S(1)} %get-tuple-element.15), channel_id=1, source_target_pairs={{0,1},{1,0},{2,3},{3,2},{4,5},{5,4},{6,7},{7,6},{8,9},{9,8},{10,11... | collective-permute-start | bytes 393224 | tf_op jit(solution)/shard_map/ppermute | solution.py:362
  29.3 7.2 %collective-permute-start.1 = (f32[8,32,128]{2,1,0:T(8,128)S(1)}, f32[8,32,128]{2,1,0:T(8,128)S(1)}, u32[]{:S(2)}, u32[]{:S(2)}) collective-permute-start(f32[8,32,128]{2,1,0:T(8,128)S(1)} %get-tuple-element.19), channel_id=1, source_target_pairs={{0,15},{1,2},{2,1},{3,4},{4,3},{5,6},{6,5},{7,8},{8,7},{9,10},{10,... | collective-permute-start | bytes 393224 | tf_op jit(solution)/shard_map/ppermute | solution.py:361
  37.6 13.0 %copy-start = (s32[6912,4]{0,1:T(4,128)S(1)}, s32[6912,4]{0,1:T(4,128)}, u32[]{:S(2)}) copy-start(s32[6912,4]{0,1:T(4,128)} %param.6) | copy-start | bytes 331780
  37.6 13.0 %copy-start.1 = (f32[4,6912]{1,0:T(4,128)S(1)}, f32[4,6912]{1,0:T(4,128)}, u32[]{:S(2)}) copy-start(f32[4,6912]{1,0:T(4,128)} %weight_ref.3) | copy-start | bytes 331780

commit v10 on v9

--- a/solution.py
+++ b/solution.py
@@ -300,9 +300,7 @@
 
 
 def plan_of(blocks):
-    turns = max(t for t in (3, 2, 1) if blocks % t == 0)
-    size = blocks // turns
-    return [(size - size // 3, size // 3)] * turns
+    return [(blocks - blocks // 3, blocks // 3)]
 
 
 def chunk_of(fine, most):
@@ -336,17 +334,17 @@
     shape = jax.ShapeDtypeStruct
     slots = send_slots.T
     cells = coarse_cell.reshape(blocks, LANES)
-    chunk = chunk_of(fine, 2304)
-    grid = (fine // chunk,)
+    chunk = chunk_of(fine, 3456)
     part = lambda n: pl.BlockSpec((n, chunk), lambda i: (0, i))
+    full = lambda n: pl.BlockSpec((n, fine), lambda i: (0, 0))
     whole = pl.BlockSpec((blocks, channels, LANES), lambda i: (0, 0, 0))
 
     sent = call(
         sum_to_slots,
         (increment, slots, tent_weight),
         shape((blocks, channels, LANES), F32),
-        grid=grid,
-        in_specs=[part(channels), part(CORNERS), part(CORNERS)],
+        grid=(1,),
+        in_specs=[full(channels), full(CORNERS), full(CORNERS)],
         out_specs=whole,
         memory=56,
     )
@@ -392,7 +390,7 @@
         (returned, slots, tent_weight, inner, near_last, far_last),
         [shape((channels, fine), F32), shape((rows, channels, width), F32)],
         [pltpu.VMEM((2 * channels * slot_count // PLACES, PLACES), BF16)],
-        grid=grid,
+        grid=(turns,),
         in_specs=[whole, part(CORNERS), part(CORNERS), all_of(rows - 2 * STEPS), all_of(STEPS), all_of(STEPS)],
         out_specs=[part(channels), pl.BlockSpec((some, channels, width), lambda i: (i, 0, 0))],
         memory=32,

time: 58 us -> 57.2 us (0.986)
  Pallas kernels: 23.1 us -> 22.3 us
    pallas_call x5, Pallas kernels: 23.1 us -> 22.3 us  [call(): pl.pallas_call(kernel, grid=grid, out_shape=out, in_specs=[in_specs] * le...]
where the time goes in v10:
time: 57.2 us; the launch traced here: 56.9 us
  blocking collectives  30.5 us (53%)
  Pallas kernels  22.3 us (39%)
  starting transfers between devices  1.75 us (3%)
  waiting for transfers between devices  1.6 us (3%)
  between operations  0.66 us (1%)
    all_to_all x2, blocking collectives, exchange(): lax.all_to_all(blocks, 'tile', split_axis=0, concat_axis=0, tiled=True)  30.5 us
    pallas_call x5, Pallas kernels, call(): pl.pallas_call(kernel, grid=grid, out_shape=out, in_specs=[in_specs] * le...  22.3 us
    ppermute x1, starting transfers between devices, body(): far = lax.ppermute(far, 'tile', off_chip)  1.7 us
    ppermute x1, waiting for transfers between devices, body(): far = lax.ppermute(far, 'tile', off_chip)  1.6 us
  transfers between devices with their start and end apart: 2, of which 1 were waited for; matrix products, arithmetic and copies ran while one was open for 0% of the time, Pallas kernels for 7%

profile of v10, /device:TPU:0, one launch (start us, length us, event | category | flops | bytes accessed | tf_op | source)
XLA Modules:
  0.0 56.9 jit_solution(6391390218647446679)
XLA Ops:
  0.6 9.8 %shard_map.68 = f32[16,32,128]{2,1,0:T(8,128)} custom-call(f32[32,6912]{1,0:T(8,128)} %inc_ref.1, s32[4,6912]{1,0:T(4,128)} %bitcast.3, f32[4,6912]{1,0:T(4,128)} %weight_ref.3), custom_call_target="tpu_custom_call" | custom-call | tf_op jit(solution)/shard_map/pallas_call | solution.py:312
  10.4 0.0 copy-start.2
  10.4 0.0 copy-start.3
  10.4 17.5 %all_to_all.10.rec_ref = f32[16,32,128]{2,1,0:T(8,128)S(1)} all-to-all(f32[16,32,128]{2,1,0:T(8,128)} %shard_map.68), channel_id=1, replica_groups=mesh['group'=2,'tile'=16] {'tile'}, dimensions={0} | all-to-all | bytes 524288 | tf_op jit(solution)/shard_map/all_to_all | solution.py:404
  28.0 0.0 copy-done.2
  28.0 0.0 copy-done.3
  28.0 0.9 %shard_map.69 = (f32[10,32,256]{2,1,0:T(8,128)S(1)}, f32[8,32,128]{2,1,0:T(8,128)S(1)}, f32[8,32,128]{2,1,0:T(8,128)S(1)}) custom-call(f32[16,32,128]{2,1,0:T(8,128)S(1)} %all_to_all.10.rec_ref, s32[16,128]{1,0:T(8,128)S(1)} %bitcast.5, f32[18,192]{1,0:T(8,128)S(1)} %copy-done.2), custom_call_target="tpu_custom_call" | custom-call | tf_op jit(solution)/shard_map/pallas_call | solution.py:312
  28.9 0.0 collective-permute-start
  29.0 1.7 %collective-permute-start.1 = (f32[8,32,128]{2,1,0:T(8,128)S(1)}, f32[8,32,128]{2,1,0:T(8,128)S(1)}, u32[]{:S(2)}, u32[]{:S(2)}) collective-permute-start(f32[8,32,128]{2,1,0:T(8,128)S(1)} %get-tuple-element.19), channel_id=1, source_target_pairs={{0,15},{1,2},{2,1},{3,4},{4,3},{5,6},{6,5},{7,8},{8,7},{9,10},{10,... | collective-permute-start | bytes 393224 | tf_op jit(solution)/shard_map/ppermute | solution.py:359
  30.7 0.0 collective-permute-done.edge_ref
  30.7 3.9 %shard_map.70 = (f32[18,32,256]{2,1,0:T(8,128)S(1)}, f32[4,4,32,256]{3,2,1,0:T(8,128)S(1)}, f32[8,32,256]{2,1,0:T(8,128)S(1)}, f32[5,32,256]{2,1,0:T(8,128)S(1)}, f32[16,32,128]{2,1,0:T(8,128)S(1)}) custom-call(f32[16,32,128]{2,1,0:T(8,128)S(1)} %all_to_all.10.rec_ref, f32[10,32,256]{2,1,0:T(8,128)S(1)} %get-tuple-element.14.edges_ref, ...), custom_call_target="tpu_custom_call" | custom-call | flops 536870912 | bytes 8388608 | tf_op jit(solution)/shard_map/pallas_call | solution.py:312
  34.5 1.6 %collective-permute-done.1.edge_ref = f32[8,32,128]{2,1,0:T(8,128)S(1)} collective-permute-done((f32[8,32,128]{2,1,0:T(8,128)S(1)}, f32[8,32,128]{2,1,0:T(8,128)S(1)}, u32[]{:S(2)}, u32[]{:S(2)}) %collective-permute-start.1) | collective-permute-done | bytes 131104 | tf_op jit(solution)/shard_map/ppermute | solution.py:359
  36.1 1.1 %shard_map.71 = (f32[5,32,256]{2,1,0:T(8,128)S(1)}, f32[16,32,128]{2,1,0:T(8,128)S(1)}) custom-call(f32[4,4,32,256]{3,2,1,0:T(8,128)S(1)} %get-tuple-element.16.kept_ref, f32[16,32,128]{2,1,0:T(8,128)S(1)} %get-tuple-element.17.part_ref, f32[18,32,256]{2,1,0:T(8,128)S(1)} %get-tuple-element.18.start_ref, f32[8,32,128]{2,1,0:T(8,128)S(1)} %collective-permute-done.1.edge_ref, ...), custom_call_target="tpu_custom_call" | custom-call | tf_op jit(solution)/shard_map/pallas_call | solution.py:312
  37.2 0.0 copy-start
  37.3 0.0 copy-start.1
  37.3 13.0 %all_to_all.11.ret_ref = f32[16,32,128]{2,1,0:T(8,128)S(1)} all-to-all(f32[16,32,128]{2,1,0:T(8,128)S(1)} %get-tuple-element.20), channel_id=1, replica_groups=mesh['group'=2,'tile'=16] {'tile'}, dimensions={0} | all-to-all | bytes 524288 | tf_op jit(solution)/shard_map/all_to_all | solution.py:404
  50.3 0.0 copy-done
  50.3 0.0 copy-done.1
  50.3 6.6 %shard_map.72 = (f32[32,6912]{1,0:T(8,128)}, f32[18,32,192]{2,1,0:T(8,128)}) custom-call(f32[16,32,128]{2,1,0:T(8,128)S(1)} %all_to_all.11.ret_ref, s32[4,6912]{1,0:T(4,128)S(1)} %bitcast.4, f32[4,6912]{1,0:T(4,128)S(1)} %copy-done.1, f32[8,32,256]{2,1,0:T(8,128)S(1)} %get-tuple-element.21.inner_ref, f32[5,32,256]{2,1,0:T(8,128)S(1)} %get-tuple-element.22.near_ref, ...), custom_call_target="tpu_custom_call" | custom-call | tf_op jit(solution)/shard_map/pallas_call | solution.py:312
Async XLA Ops:
  10.4 17.5 %copy-start.2 = (f32[18,192]{1,0:T(8,128)S(1)}, f32[18,192]{1,0:T(8,128)}, u32[]{:S(2)}) copy-start(f32[18,192]{1,0:T(8,128)} %own_ref.3) | copy-start | bytes 41476
  10.4 17.5 %copy-start.3 = (s32[2048]{0:T(1024)S(1)}, s32[2048]{0:T(1024)}, u32[]{:S(2)}) copy-start(s32[2048]{0:T(1024)} %param.8) | copy-start | bytes 24580
  28.9 1.8 %collective-permute-start = (f32[8,32,128]{2,1,0:T(8,128)S(1)}, f32[8,32,128]{2,1,0:T(8,128)S(1)}, u32[]{:S(2)}, u32[]{:S(2)}) collective-permute-start(f32[8,32,128]{2,1,0:T(8,128)S(1)} %get-tuple-element.15), channel_id=1, source_target_pairs={{0,1},{1,0},{2,3},{3,2},{4,5},{5,4},{6,7},{7,6},{8,9},{9,8},{10,11... | collective-permute-start | bytes 393224 | tf_op jit(solution)/shard_map/ppermute | solution.py:360
  29.0 7.2 %collective-permute-start.1 = (f32[8,32,128]{2,1,0:T(8,128)S(1)}, f32[8,32,128]{2,1,0:T(8,128)S(1)}, u32[]{:S(2)}, u32[]{:S(2)}) collective-permute-start(f32[8,32,128]{2,1,0:T(8,128)S(1)} %get-tuple-element.19), channel_id=1, source_target_pairs={{0,15},{1,2},{2,1},{3,4},{4,3},{5,6},{6,5},{7,8},{8,7},{9,10},{10,... | collective-permute-start | bytes 393224 | tf_op jit(solution)/shard_map/ppermute | solution.py:359
  37.2 13.0 %copy-start = (s32[6912,4]{0,1:T(4,128)S(1)}, s32[6912,4]{0,1:T(4,128)}, u32[]{:S(2)}) copy-start(s32[6912,4]{0,1:T(4,128)} %param.6) | copy-start | bytes 331780
  37.3 13.0 %copy-start.1 = (f32[4,6912]{1,0:T(4,128)S(1)}, f32[4,6912]{1,0:T(4,128)}, u32[]{:S(2)}) copy-start(f32[4,6912]{1,0:T(4,128)} %weight_ref.3) | copy-start | bytes 331780

commit v11 on v10

--- a/solution.py
+++ b/solution.py
@@ -138,8 +138,27 @@
     return [first, first + 1, last - 2, last - 1]
 
 
-def read_rows(final_rows, ys, cell_ref, values_ref, base, width):
-    senders, channels, _ = values_ref.shape
+def read_by_lanes(rows_ref, ys, cell_ref, values_ref, part_ref, senders, width):
+    channels = values_ref.shape[1]
+    group = 8
+    for s in senders:
+        cells = jnp.broadcast_to(cell_ref[s : s + 1, :], (group, LANES))
+        y = cells // width
+        x = cells - y * width
+        lanes = x % LANES
+        marks = [[(y == row) & (x // LANES == part) for part in range(2)] for row in ys]
+        for c in range(0, channels, group):
+            out = part_ref[s, c : c + group, :]
+            for k in range(len(ys)):
+                for part in range(2):
+                    side = rows_ref[k, c : c + group, LANES * part : LANES * (part + 1)]
+                    out = jnp.where(marks[k][part], jnp.take_along_axis(side, lanes, axis=1), out)
+            values_ref[s, c : c + group, :] = out
+
+
+def read_rows(final_rows, ys, cell_ref, values_ref, base, width, senders=None):
+    senders = values_ref.shape[0] if senders is None else senders
+    channels = values_ref.shape[1]
     left = jnp.concatenate([jnp.concatenate(halves(row), 0) for row in final_rows], 0)
     for s in range(0, senders, 2):
         cells = jnp.concatenate([cell_ref[s : s + 1, :], cell_ref[s + 1 : s + 2, :]], 1)
@@ -229,7 +248,11 @@
     for k, row in enumerate(side):
         side_ref[k] = row
     base = lambda s: jnp.concatenate([part_ref[s], part_ref[s + 1]], 1)
-    read_rows(side, [first + k for k in range(STEPS)], cell_ref, values_ref, base, width)
+    ys = [first + k for k in range(STEPS)]
+    senders = values_ref.shape[0]
+    products = senders - 2 * (3 * senders // 16)
+    read_rows(side, ys, cell_ref, values_ref, base, width, products)
+    read_by_lanes(side_ref, ys, cell_ref, values_ref, part_ref, range(products, senders), width)
 
 
 def by_product(table_ref, slot_ref, weight_ref, columns, channels):

time: 57.2 us -> 57.2 us (level)
  no operation moved by 1% of the time
where the time goes in v11:
time: 57.2 us; the launch traced here: 56.8 us
  blocking collectives  30.5 us (53%)
  Pallas kernels  22.3 us (39%)
  starting transfers between devices  1.75 us (3%)
  waiting for transfers between devices  1.6 us (3%)
  between operations  0.66 us (1%)
    all_to_all x2, blocking collectives, exchange(): lax.all_to_all(blocks, 'tile', split_axis=0, concat_axis=0, tiled=True)  30.5 us
    pallas_call x5, Pallas kernels, call(): pl.pallas_call(kernel, grid=grid, out_shape=out, in_specs=[in_specs] * le...  22.3 us
    ppermute x1, starting transfers between devices, body(): far = lax.ppermute(far, 'tile', off_chip)  1.7 us
    ppermute x1, waiting for transfers between devices, body(): far = lax.ppermute(far, 'tile', off_chip)  1.6 us
  transfers between devices with their start and end apart: 2, of which 1 were waited for; matrix products, arithmetic and copies ran while one was open for 0% of the time, Pallas kernels for 7%

profile of v11, /device:TPU:0, one launch (start us, length us, event | category | flops | bytes accessed | tf_op | source)
XLA Modules:
  0.0 56.8 jit_solution(794976597583029767)
XLA Ops:
  0.6 9.8 %shard_map.68 = f32[16,32,128]{2,1,0:T(8,128)} custom-call(f32[32,6912]{1,0:T(8,128)} %inc_ref.1, s32[4,6912]{1,0:T(4,128)} %bitcast.3, f32[4,6912]{1,0:T(4,128)} %weight_ref.3), custom_call_target="tpu_custom_call" | custom-call | tf_op jit(solution)/shard_map/pallas_call | solution.py:335
  10.4 0.0 copy-start.2
  10.4 0.0 copy-start.3
  10.4 17.5 %all_to_all.10.rec_ref = f32[16,32,128]{2,1,0:T(8,128)S(1)} all-to-all(f32[16,32,128]{2,1,0:T(8,128)} %shard_map.68), channel_id=1, replica_groups=mesh['group'=2,'tile'=16] {'tile'}, dimensions={0} | all-to-all | bytes 524288 | tf_op jit(solution)/shard_map/all_to_all | solution.py:427
  28.0 0.0 copy-done.2
  28.0 0.0 copy-done.3
  28.0 0.9 %shard_map.69 = (f32[10,32,256]{2,1,0:T(8,128)S(1)}, f32[8,32,128]{2,1,0:T(8,128)S(1)}, f32[8,32,128]{2,1,0:T(8,128)S(1)}) custom-call(f32[16,32,128]{2,1,0:T(8,128)S(1)} %all_to_all.10.rec_ref, s32[16,128]{1,0:T(8,128)S(1)} %bitcast.5, f32[18,192]{1,0:T(8,128)S(1)} %copy-done.2), custom_call_target="tpu_custom_call" | custom-call | tf_op jit(solution)/shard_map/pallas_call | solution.py:335
  28.9 0.0 collective-permute-start
  29.0 1.7 %collective-permute-start.1 = (f32[8,32,128]{2,1,0:T(8,128)S(1)}, f32[8,32,128]{2,1,0:T(8,128)S(1)}, u32[]{:S(2)}, u32[]{:S(2)}) collective-permute-start(f32[8,32,128]{2,1,0:T(8,128)S(1)} %get-tuple-element.19), channel_id=1, source_target_pairs={{0,15},{1,2},{2,1},{3,4},{4,3},{5,6},{6,5},{7,8},{8,7},{9,10},{10,... | collective-permute-start | bytes 393224 | tf_op jit(solution)/shard_map/ppermute | solution.py:382
  30.7 0.0 collective-permute-done.edge_ref
  30.7 3.9 %shard_map.70 = (f32[18,32,256]{2,1,0:T(8,128)S(1)}, f32[4,4,32,256]{3,2,1,0:T(8,128)S(1)}, f32[8,32,256]{2,1,0:T(8,128)S(1)}, f32[5,32,256]{2,1,0:T(8,128)S(1)}, f32[16,32,128]{2,1,0:T(8,128)S(1)}) custom-call(f32[16,32,128]{2,1,0:T(8,128)S(1)} %all_to_all.10.rec_ref, f32[10,32,256]{2,1,0:T(8,128)S(1)} %get-tuple-element.14.edges_ref, ...), custom_call_target="tpu_custom_call" | custom-call | flops 536870912 | bytes 8388608 | tf_op jit(solution)/shard_map/pallas_call | solution.py:335
  34.5 1.6 %collective-permute-done.1.edge_ref = f32[8,32,128]{2,1,0:T(8,128)S(1)} collective-permute-done((f32[8,32,128]{2,1,0:T(8,128)S(1)}, f32[8,32,128]{2,1,0:T(8,128)S(1)}, u32[]{:S(2)}, u32[]{:S(2)}) %collective-permute-start.1) | collective-permute-done | bytes 131104 | tf_op jit(solution)/shard_map/ppermute | solution.py:382
  36.1 1.1 %shard_map.71 = (f32[5,32,256]{2,1,0:T(8,128)S(1)}, f32[16,32,128]{2,1,0:T(8,128)S(1)}) custom-call(f32[4,4,32,256]{3,2,1,0:T(8,128)S(1)} %get-tuple-element.16.kept_ref, f32[16,32,128]{2,1,0:T(8,128)S(1)} %get-tuple-element.17.part_ref, f32[18,32,256]{2,1,0:T(8,128)S(1)} %get-tuple-element.18.start_ref, f32[8,32,128]{2,1,0:T(8,128)S(1)} %collective-permute-done.1.edge_ref, ...), custom_call_target="tpu_custom_call" | custom-call | tf_op jit(solution)/shard_map/pallas_call | solution.py:335
  37.2 0.0 copy-start
  37.2 0.0 copy-start.1
  37.2 13.0 %all_to_all.11.ret_ref = f32[16,32,128]{2,1,0:T(8,128)S(1)} all-to-all(f32[16,32,128]{2,1,0:T(8,128)S(1)} %get-tuple-element.20), channel_id=1, replica_groups=mesh['group'=2,'tile'=16] {'tile'}, dimensions={0} | all-to-all | bytes 524288 | tf_op jit(solution)/shard_map/all_to_all | solution.py:427
  50.2 0.0 copy-done
  50.2 0.0 copy-done.1
  50.2 6.6 %shard_map.72 = (f32[32,6912]{1,0:T(8,128)}, f32[18,32,192]{2,1,0:T(8,128)}) custom-call(f32[16,32,128]{2,1,0:T(8,128)S(1)} %all_to_all.11.ret_ref, s32[4,6912]{1,0:T(4,128)S(1)} %bitcast.4, f32[4,6912]{1,0:T(4,128)S(1)} %copy-done.1, f32[8,32,256]{2,1,0:T(8,128)S(1)} %get-tuple-element.21.inner_ref, f32[5,32,256]{2,1,0:T(8,128)S(1)} %get-tuple-element.22.near_ref, ...), custom_call_target="tpu_custom_call" | custom-call | tf_op jit(solution)/shard_map/pallas_call | solution.py:335
Async XLA Ops:
  10.4 17.5 %copy-start.2 = (f32[18,192]{1,0:T(8,128)S(1)}, f32[18,192]{1,0:T(8,128)}, u32[]{:S(2)}) copy-start(f32[18,192]{1,0:T(8,128)} %own_ref.3) | copy-start | bytes 41476
  10.4 17.5 %copy-start.3 = (s32[2048]{0:T(1024)S(1)}, s32[2048]{0:T(1024)}, u32[]{:S(2)}) copy-start(s32[2048]{0:T(1024)} %param.8) | copy-start | bytes 24580
  28.9 1.8 %collective-permute-start = (f32[8,32,128]{2,1,0:T(8,128)S(1)}, f32[8,32,128]{2,1,0:T(8,128)S(1)}, u32[]{:S(2)}, u32[]{:S(2)}) collective-permute-start(f32[8,32,128]{2,1,0:T(8,128)S(1)} %get-tuple-element.15), channel_id=1, source_target_pairs={{0,1},{1,0},{2,3},{3,2},{4,5},{5,4},{6,7},{7,6},{8,9},{9,8},{10,11... | collective-permute-start | bytes 393224 | tf_op jit(solution)/shard_map/ppermute | solution.py:383
  29.0 7.2 %collective-permute-start.1 = (f32[8,32,128]{2,1,0:T(8,128)S(1)}, f32[8,32,128]{2,1,0:T(8,128)S(1)}, u32[]{:S(2)}, u32[]{:S(2)}) collective-permute-start(f32[8,32,128]{2,1,0:T(8,128)S(1)} %get-tuple-element.19), channel_id=1, source_target_pairs={{0,15},{1,2},{2,1},{3,4},{4,3},{5,6},{6,5},{7,8},{8,7},{9,10},{10,... | collective-permute-start | bytes 393224 | tf_op jit(solution)/shard_map/ppermute | solution.py:382
  37.2 13.0 %copy-start = (s32[6912,4]{0,1:T(4,128)S(1)}, s32[6912,4]{0,1:T(4,128)}, u32[]{:S(2)}) copy-start(s32[6912,4]{0,1:T(4,128)} %param.6) | copy-start | bytes 331780
  37.2 13.0 %copy-start.1 = (f32[4,6912]{1,0:T(4,128)S(1)}, f32[4,6912]{1,0:T(4,128)}, u32[]{:S(2)}) copy-start(f32[4,6912]{1,0:T(4,128)} %weight_ref.3) | copy-start | bytes 331780

commit v12 on v10

--- a/solution.py
+++ b/solution.py
@@ -179,21 +179,17 @@
         coef_ref[pl.ds(place, 1), :] = read_coef(edge_ref, k, width)
         own = own_ref[pl.ds(flip(k, rows - 1 - k), 1), :]
         coef_ref[STEPS + k : STEPS + k + 1, :] = widened([own], own, own, width)
-    held, other = one_ref, two_ref
+    held = {u: one_ref[u] for u in range(STEPS)}
     for turn in range(1, STEPS + 1):
-
-        def row(u):
-            if turn == 1 and u >= STEPS:
-                return start_ref[flip(u - STEPS, rows - 1 - u + STEPS)]
-            if u >= STEPS + turn - 1:
-                k = u - STEPS - turn + 1
-                return kept_ref[turn - 2, flip(k, 3 - k)]
-            return held[u]
-
-        for u in range(turn, turn + STEPS):
-            other[u] = stepped(row(u - 1), row(u), row(u + 1), coef_ref[u : u + 1, :])
-        held, other = other, held
-    return [held[flip(STEPS + k, 2 * STEPS - 1 - k)] for k in range(STEPS)]
+        for u in (STEPS + turn - 1, STEPS + turn):
+            k = u - STEPS - turn + 1
+            inside = start_ref[flip(u - STEPS, rows - 1 - u + STEPS)] if turn == 1 else kept_ref[turn - 2, flip(k, 3 - k)]
+            held[u] = inside
+        ours = range(turn, turn + STEPS)
+        held = {u: stepped(held[u - 1], held[u], held[u + 1], coef_ref[u : u + 1, :]) for u in ours}
+    for u, row in held.items():
+        two_ref[u] = row
+    return [two_ref[flip(STEPS + k, 2 * STEPS - 1 - k)] for k in range(STEPS)]
 
 
 def diffuse_most(

time: 57.2 us -> 57.2 us (level)
  no operation moved by 1% of the time
where the time goes in v12:
time: 57.2 us; the launch traced here: 56.9 us
  blocking collectives  30.5 us (53%)
  Pallas kernels  22.3 us (39%)
  starting transfers between devices  1.75 us (3%)
  waiting for transfers between devices  1.58 us (3%)
  between operations  0.66 us (1%)
    all_to_all x2, blocking collectives, exchange(): lax.all_to_all(blocks, 'tile', split_axis=0, concat_axis=0, tiled=True)  30.5 us
    pallas_call x5, Pallas kernels, call(): pl.pallas_call(kernel, grid=grid, out_shape=out, in_specs=[in_specs] * le...  22.3 us
    ppermute x1, starting transfers between devices, body(): far = lax.ppermute(far, 'tile', off_chip)  1.7 us
    ppermute x1, waiting for transfers between devices, body(): far = lax.ppermute(far, 'tile', off_chip)  1.58 us
  transfers between devices with their start and end apart: 2, of which 1 were waited for; matrix products, arithmetic and copies ran while one was open for 0% of the time, Pallas kernels for 7%

profile of v12, /device:TPU:0, one launch (start us, length us, event | category | flops | bytes accessed | tf_op | source)
XLA Modules:
  0.0 56.9 jit_solution(11178261990344792085)
XLA Ops:
  0.6 9.8 %shard_map.68 = f32[16,32,128]{2,1,0:T(8,128)} custom-call(f32[32,6912]{1,0:T(8,128)} %inc_ref.1, s32[4,6912]{1,0:T(4,128)} %bitcast.3, f32[4,6912]{1,0:T(4,128)} %weight_ref.3), custom_call_target="tpu_custom_call" | custom-call | tf_op jit(solution)/shard_map/pallas_call | solution.py:308
  10.4 0.0 copy-start.2
  10.4 0.0 copy-start.3
  10.4 17.5 %all_to_all.10.rec_ref = f32[16,32,128]{2,1,0:T(8,128)S(1)} all-to-all(f32[16,32,128]{2,1,0:T(8,128)} %shard_map.68), channel_id=1, replica_groups=mesh['group'=2,'tile'=16] {'tile'}, dimensions={0} | all-to-all | bytes 524288 | tf_op jit(solution)/shard_map/all_to_all | solution.py:400
  28.0 0.0 copy-done.2
  28.0 0.0 copy-done.3
  28.0 0.9 %shard_map.69 = (f32[10,32,256]{2,1,0:T(8,128)S(1)}, f32[8,32,128]{2,1,0:T(8,128)S(1)}, f32[8,32,128]{2,1,0:T(8,128)S(1)}) custom-call(f32[16,32,128]{2,1,0:T(8,128)S(1)} %all_to_all.10.rec_ref, s32[16,128]{1,0:T(8,128)S(1)} %bitcast.5, f32[18,192]{1,0:T(8,128)S(1)} %copy-done.2), custom_call_target="tpu_custom_call" | custom-call | tf_op jit(solution)/shard_map/pallas_call | solution.py:308
  28.9 0.0 collective-permute-start
  29.0 1.7 %collective-permute-start.1 = (f32[8,32,128]{2,1,0:T(8,128)S(1)}, f32[8,32,128]{2,1,0:T(8,128)S(1)}, u32[]{:S(2)}, u32[]{:S(2)}) collective-permute-start(f32[8,32,128]{2,1,0:T(8,128)S(1)} %get-tuple-element.19), channel_id=1, source_target_pairs={{0,15},{1,2},{2,1},{3,4},{4,3},{5,6},{6,5},{7,8},{8,7},{9,10},{10,... | collective-permute-start | bytes 393224 | tf_op jit(solution)/shard_map/ppermute | solution.py:355
  30.7 0.0 collective-permute-done.edge_ref
  30.7 3.9 %shard_map.70 = (f32[18,32,256]{2,1,0:T(8,128)S(1)}, f32[4,4,32,256]{3,2,1,0:T(8,128)S(1)}, f32[8,32,256]{2,1,0:T(8,128)S(1)}, f32[5,32,256]{2,1,0:T(8,128)S(1)}, f32[16,32,128]{2,1,0:T(8,128)S(1)}) custom-call(f32[16,32,128]{2,1,0:T(8,128)S(1)} %all_to_all.10.rec_ref, f32[10,32,256]{2,1,0:T(8,128)S(1)} %get-tuple-element.14.edges_ref, ...), custom_call_target="tpu_custom_call" | custom-call | flops 536870912 | bytes 8388608 | tf_op jit(solution)/shard_map/pallas_call | solution.py:308
  34.5 1.6 %collective-permute-done.1.edge_ref = f32[8,32,128]{2,1,0:T(8,128)S(1)} collective-permute-done((f32[8,32,128]{2,1,0:T(8,128)S(1)}, f32[8,32,128]{2,1,0:T(8,128)S(1)}, u32[]{:S(2)}, u32[]{:S(2)}) %collective-permute-start.1) | collective-permute-done | bytes 131104 | tf_op jit(solution)/shard_map/ppermute | solution.py:355
  36.1 1.1 %shard_map.71 = (f32[5,32,256]{2,1,0:T(8,128)S(1)}, f32[16,32,128]{2,1,0:T(8,128)S(1)}) custom-call(f32[4,4,32,256]{3,2,1,0:T(8,128)S(1)} %get-tuple-element.16.kept_ref, f32[16,32,128]{2,1,0:T(8,128)S(1)} %get-tuple-element.17.part_ref, f32[18,32,256]{2,1,0:T(8,128)S(1)} %get-tuple-element.18.start_ref, f32[8,32,128]{2,1,0:T(8,128)S(1)} %collective-permute-done.1.edge_ref, ...), custom_call_target="tpu_custom_call" | custom-call | tf_op jit(solution)/shard_map/pallas_call | solution.py:308
  37.2 0.0 copy-start
  37.3 0.0 copy-start.1
  37.3 13.0 %all_to_all.11.ret_ref = f32[16,32,128]{2,1,0:T(8,128)S(1)} all-to-all(f32[16,32,128]{2,1,0:T(8,128)S(1)} %get-tuple-element.20), channel_id=1, replica_groups=mesh['group'=2,'tile'=16] {'tile'}, dimensions={0} | all-to-all | bytes 524288 | tf_op jit(solution)/shard_map/all_to_all | solution.py:400
  50.3 0.0 copy-done
  50.3 0.0 copy-done.1
  50.3 6.6 %shard_map.72 = (f32[32,6912]{1,0:T(8,128)}, f32[18,32,192]{2,1,0:T(8,128)}) custom-call(f32[16,32,128]{2,1,0:T(8,128)S(1)} %all_to_all.11.ret_ref, s32[4,6912]{1,0:T(4,128)S(1)} %bitcast.4, f32[4,6912]{1,0:T(4,128)S(1)} %copy-done.1, f32[8,32,256]{2,1,0:T(8,128)S(1)} %get-tuple-element.21.inner_ref, f32[5,32,256]{2,1,0:T(8,128)S(1)} %get-tuple-element.22.near_ref, ...), custom_call_target="tpu_custom_call" | custom-call | tf_op jit(solution)/shard_map/pallas_call | solution.py:308
Async XLA Ops:
  10.4 17.5 %copy-start.2 = (f32[18,192]{1,0:T(8,128)S(1)}, f32[18,192]{1,0:T(8,128)}, u32[]{:S(2)}) copy-start(f32[18,192]{1,0:T(8,128)} %own_ref.3) | copy-start | bytes 41476
  10.4 17.5 %copy-start.3 = (s32[2048]{0:T(1024)S(1)}, s32[2048]{0:T(1024)}, u32[]{:S(2)}) copy-start(s32[2048]{0:T(1024)} %param.8) | copy-start | bytes 24580
  28.9 1.8 %collective-permute-start = (f32[8,32,128]{2,1,0:T(8,128)S(1)}, f32[8,32,128]{2,1,0:T(8,128)S(1)}, u32[]{:S(2)}, u32[]{:S(2)}) collective-permute-start(f32[8,32,128]{2,1,0:T(8,128)S(1)} %get-tuple-element.15), channel_id=1, source_target_pairs={{0,1},{1,0},{2,3},{3,2},{4,5},{5,4},{6,7},{7,6},{8,9},{9,8},{10,11... | collective-permute-start | bytes 393224 | tf_op jit(solution)/shard_map/ppermute | solution.py:356
  29.0 7.2 %collective-permute-start.1 = (f32[8,32,128]{2,1,0:T(8,128)S(1)}, f32[8,32,128]{2,1,0:T(8,128)S(1)}, u32[]{:S(2)}, u32[]{:S(2)}) collective-permute-start(f32[8,32,128]{2,1,0:T(8,128)S(1)} %get-tuple-element.19), channel_id=1, source_target_pairs={{0,15},{1,2},{2,1},{3,4},{4,3},{5,6},{6,5},{7,8},{8,7},{9,10},{10,... | collective-permute-start | bytes 393224 | tf_op jit(solution)/shard_map/ppermute | solution.py:355
  37.2 13.0 %copy-start = (s32[6912,4]{0,1:T(4,128)S(1)}, s32[6912,4]{0,1:T(4,128)}, u32[]{:S(2)}) copy-start(s32[6912,4]{0,1:T(4,128)} %param.6) | copy-start | bytes 331780
  37.3 13.0 %copy-start.1 = (f32[4,6912]{1,0:T(4,128)S(1)}, f32[4,6912]{1,0:T(4,128)}, u32[]{:S(2)}) copy-start(f32[4,6912]{1,0:T(4,128)} %weight_ref.3) | copy-start | bytes 331780

commit v13 on v11

--- a/solution.py
+++ b/solution.py
@@ -198,21 +198,17 @@
         coef_ref[pl.ds(place, 1), :] = read_coef(edge_ref, k, width)
         own = own_ref[pl.ds(flip(k, rows - 1 - k), 1), :]
         coef_ref[STEPS + k : STEPS + k + 1, :] = widened([own], own, own, width)
-    held, other = one_ref, two_ref
+    held = {u: one_ref[u] for u in range(STEPS)}
     for turn in range(1, STEPS + 1):
-
-        def row(u):
-            if turn == 1 and u >= STEPS:
-                return start_ref[flip(u - STEPS, rows - 1 - u + STEPS)]
-            if u >= STEPS + turn - 1:
-                k = u - STEPS - turn + 1
-                return kept_ref[turn - 2, flip(k, 3 - k)]
-            return held[u]
-
-        for u in range(turn, turn + STEPS):
-            other[u] = stepped(row(u - 1), row(u), row(u + 1), coef_ref[u : u + 1, :])
-        held, other = other, held
-    return [held[flip(STEPS + k, 2 * STEPS - 1 - k)] for k in range(STEPS)]
+        for u in (STEPS + turn - 1, STEPS + turn):
+            k = u - STEPS - turn + 1
+            inside = start_ref[flip(u - STEPS, rows - 1 - u + STEPS)] if turn == 1 else kept_ref[turn - 2, flip(k, 3 - k)]
+            held[u] = inside
+        ours = range(turn, turn + STEPS)
+        held = {u: stepped(held[u - 1], held[u], held[u + 1], coef_ref[u : u + 1, :]) for u in ours}
+    for u, row in held.items():
+        two_ref[u] = row
+    return [two_ref[flip(STEPS + k, 2 * STEPS - 1 - k)] for k in range(STEPS)]
 
 
 def diffuse_most(

time: 57.2 us -> 57.2 us (level)
  no operation moved by 1% of the time
where the time goes in v13:
time: 57.2 us; the launch traced here: 56.8 us
  blocking collectives  30.5 us (53%)
  Pallas kernels  22.3 us (39%)
  starting transfers between devices  1.75 us (3%)
  waiting for transfers between devices  1.58 us (3%)
  between operations  0.66 us (1%)
    all_to_all x2, blocking collectives, exchange(): lax.all_to_all(blocks, 'tile', split_axis=0, concat_axis=0, tiled=True)  30.5 us
    pallas_call x5, Pallas kernels, call(): pl.pallas_call(kernel, grid=grid, out_shape=out, in_specs=[in_specs] * le...  22.3 us
    ppermute x1, starting transfers between devices, body(): far = lax.ppermute(far, 'tile', off_chip)  1.7 us
    ppermute x1, waiting for transfers between devices, body(): far = lax.ppermute(far, 'tile', off_chip)  1.58 us
  transfers between devices with their start and end apart: 2, of which 1 were waited for; matrix products, arithmetic and copies ran while one was open for 0% of the time, Pallas kernels for 7%

profile of v13, /device:TPU:0, one launch (start us, length us, event | category | flops | bytes accessed | tf_op | source)
XLA Modules:
  0.0 56.8 jit_solution(6590702173925174221)
XLA Ops:
  0.6 9.8 %shard_map.68 = f32[16,32,128]{2,1,0:T(8,128)} custom-call(f32[32,6912]{1,0:T(8,128)} %inc_ref.1, s32[4,6912]{1,0:T(4,128)} %bitcast.3, f32[4,6912]{1,0:T(4,128)} %weight_ref.3), custom_call_target="tpu_custom_call" | custom-call | tf_op jit(solution)/shard_map/pallas_call | solution.py:331
  10.4 0.0 copy-start.2
  10.4 0.0 copy-start.3
  10.4 17.5 %all_to_all.10.rec_ref = f32[16,32,128]{2,1,0:T(8,128)S(1)} all-to-all(f32[16,32,128]{2,1,0:T(8,128)} %shard_map.68), channel_id=1, replica_groups=mesh['group'=2,'tile'=16] {'tile'}, dimensions={0} | all-to-all | bytes 524288 | tf_op jit(solution)/shard_map/all_to_all | solution.py:423
  28.0 0.0 copy-done.2
  28.0 0.0 copy-done.3
  28.0 0.9 %shard_map.69 = (f32[10,32,256]{2,1,0:T(8,128)S(1)}, f32[8,32,128]{2,1,0:T(8,128)S(1)}, f32[8,32,128]{2,1,0:T(8,128)S(1)}) custom-call(f32[16,32,128]{2,1,0:T(8,128)S(1)} %all_to_all.10.rec_ref, s32[16,128]{1,0:T(8,128)S(1)} %bitcast.5, f32[18,192]{1,0:T(8,128)S(1)} %copy-done.2), custom_call_target="tpu_custom_call" | custom-call | tf_op jit(solution)/shard_map/pallas_call | solution.py:331
  28.9 0.0 collective-permute-start
  29.0 1.7 %collective-permute-start.1 = (f32[8,32,128]{2,1,0:T(8,128)S(1)}, f32[8,32,128]{2,1,0:T(8,128)S(1)}, u32[]{:S(2)}, u32[]{:S(2)}) collective-permute-start(f32[8,32,128]{2,1,0:T(8,128)S(1)} %get-tuple-element.19), channel_id=1, source_target_pairs={{0,15},{1,2},{2,1},{3,4},{4,3},{5,6},{6,5},{7,8},{8,7},{9,10},{10,... | collective-permute-start | bytes 393224 | tf_op jit(solution)/shard_map/ppermute | solution.py:378
  30.7 0.0 collective-permute-done.edge_ref
  30.7 3.9 %shard_map.70 = (f32[18,32,256]{2,1,0:T(8,128)S(1)}, f32[4,4,32,256]{3,2,1,0:T(8,128)S(1)}, f32[8,32,256]{2,1,0:T(8,128)S(1)}, f32[5,32,256]{2,1,0:T(8,128)S(1)}, f32[16,32,128]{2,1,0:T(8,128)S(1)}) custom-call(f32[16,32,128]{2,1,0:T(8,128)S(1)} %all_to_all.10.rec_ref, f32[10,32,256]{2,1,0:T(8,128)S(1)} %get-tuple-element.14.edges_ref, ...), custom_call_target="tpu_custom_call" | custom-call | flops 536870912 | bytes 8388608 | tf_op jit(solution)/shard_map/pallas_call | solution.py:331
  34.5 1.6 %collective-permute-done.1.edge_ref = f32[8,32,128]{2,1,0:T(8,128)S(1)} collective-permute-done((f32[8,32,128]{2,1,0:T(8,128)S(1)}, f32[8,32,128]{2,1,0:T(8,128)S(1)}, u32[]{:S(2)}, u32[]{:S(2)}) %collective-permute-start.1) | collective-permute-done | bytes 131104 | tf_op jit(solution)/shard_map/ppermute | solution.py:378
  36.1 1.1 %shard_map.71 = (f32[5,32,256]{2,1,0:T(8,128)S(1)}, f32[16,32,128]{2,1,0:T(8,128)S(1)}) custom-call(f32[4,4,32,256]{3,2,1,0:T(8,128)S(1)} %get-tuple-element.16.kept_ref, f32[16,32,128]{2,1,0:T(8,128)S(1)} %get-tuple-element.17.part_ref, f32[18,32,256]{2,1,0:T(8,128)S(1)} %get-tuple-element.18.start_ref, f32[8,32,128]{2,1,0:T(8,128)S(1)} %collective-permute-done.1.edge_ref, ...), custom_call_target="tpu_custom_call" | custom-call | tf_op jit(solution)/shard_map/pallas_call | solution.py:331
  37.2 0.0 copy-start
  37.2 0.0 copy-start.1
  37.2 13.0 %all_to_all.11.ret_ref = f32[16,32,128]{2,1,0:T(8,128)S(1)} all-to-all(f32[16,32,128]{2,1,0:T(8,128)S(1)} %get-tuple-element.20), channel_id=1, replica_groups=mesh['group'=2,'tile'=16] {'tile'}, dimensions={0} | all-to-all | bytes 524288 | tf_op jit(solution)/shard_map/all_to_all | solution.py:423
  50.2 0.0 copy-done
  50.2 0.0 copy-done.1
  50.2 6.6 %shard_map.72 = (f32[32,6912]{1,0:T(8,128)}, f32[18,32,192]{2,1,0:T(8,128)}) custom-call(f32[16,32,128]{2,1,0:T(8,128)S(1)} %all_to_all.11.ret_ref, s32[4,6912]{1,0:T(4,128)S(1)} %bitcast.4, f32[4,6912]{1,0:T(4,128)S(1)} %copy-done.1, f32[8,32,256]{2,1,0:T(8,128)S(1)} %get-tuple-element.21.inner_ref, f32[5,32,256]{2,1,0:T(8,128)S(1)} %get-tuple-element.22.near_ref, ...), custom_call_target="tpu_custom_call" | custom-call | tf_op jit(solution)/shard_map/pallas_call | solution.py:331
Async XLA Ops:
  10.4 17.5 %copy-start.2 = (f32[18,192]{1,0:T(8,128)S(1)}, f32[18,192]{1,0:T(8,128)}, u32[]{:S(2)}) copy-start(f32[18,192]{1,0:T(8,128)} %own_ref.3) | copy-start | bytes 41476
  10.4 17.5 %copy-start.3 = (s32[2048]{0:T(1024)S(1)}, s32[2048]{0:T(1024)}, u32[]{:S(2)}) copy-start(s32[2048]{0:T(1024)} %param.8) | copy-start | bytes 24580
  28.9 1.8 %collective-permute-start = (f32[8,32,128]{2,1,0:T(8,128)S(1)}, f32[8,32,128]{2,1,0:T(8,128)S(1)}, u32[]{:S(2)}, u32[]{:S(2)}) collective-permute-start(f32[8,32,128]{2,1,0:T(8,128)S(1)} %get-tuple-element.15), channel_id=1, source_target_pairs={{0,1},{1,0},{2,3},{3,2},{4,5},{5,4},{6,7},{7,6},{8,9},{9,8},{10,11... | collective-permute-start | bytes 393224 | tf_op jit(solution)/shard_map/ppermute | solution.py:379
  29.0 7.2 %collective-permute-start.1 = (f32[8,32,128]{2,1,0:T(8,128)S(1)}, f32[8,32,128]{2,1,0:T(8,128)S(1)}, u32[]{:S(2)}, u32[]{:S(2)}) collective-permute-start(f32[8,32,128]{2,1,0:T(8,128)S(1)} %get-tuple-element.19), channel_id=1, source_target_pairs={{0,15},{1,2},{2,1},{3,4},{4,3},{5,6},{6,5},{7,8},{8,7},{9,10},{10,... | collective-permute-start | bytes 393224 | tf_op jit(solution)/shard_map/ppermute | solution.py:378
  37.2 13.0 %copy-start = (s32[6912,4]{0,1:T(4,128)S(1)}, s32[6912,4]{0,1:T(4,128)}, u32[]{:S(2)}) copy-start(s32[6912,4]{0,1:T(4,128)} %param.6) | copy-start | bytes 331780
  37.2 13.0 %copy-start.1 = (f32[4,6912]{1,0:T(4,128)S(1)}, f32[4,6912]{1,0:T(4,128)}, u32[]{:S(2)}) copy-start(f32[4,6912]{1,0:T(4,128)} %weight_ref.3) | copy-start | bytes 331780

commit v14 on v10

--- a/solution.py
+++ b/solution.py
@@ -291,11 +291,11 @@
 
     at = 0
     for product, single in plan:
-        columns = slice(at, at + product * LANES)
-        result_ref[:, columns] = by_product(table_ref, slot_ref, weight_ref, columns, channels)
-        for k in range(product, product + single):
+        for k in range(single):
             columns = slice(at + k * LANES, at + (k + 1) * LANES)
             result_ref[:, columns] = by_lanes(ret_ref, slot_ref, weight_ref, columns)
+        columns = slice(at + single * LANES, at + (single + product) * LANES)
+        result_ref[:, columns] = by_product(table_ref, slot_ref, weight_ref, columns, channels)
         at += (product + single) * LANES
 
 

time: 57.2 us -> 57.2 us (level)
  no operation moved by 1% of the time
where the time goes in v14:
time: 57.2 us; the launch traced here: 56.9 us
  blocking collectives  30.5 us (53%)
  Pallas kernels  22.3 us (39%)
  starting transfers between devices  1.75 us (3%)
  waiting for transfers between devices  1.6 us (3%)
  between operations  0.66 us (1%)
    all_to_all x2, blocking collectives, exchange(): lax.all_to_all(blocks, 'tile', split_axis=0, concat_axis=0, tiled=True)  30.5 us
    pallas_call x5, Pallas kernels, call(): pl.pallas_call(kernel, grid=grid, out_shape=out, in_specs=[in_specs] * le...  22.3 us
    ppermute x1, starting transfers between devices, body(): far = lax.ppermute(far, 'tile', off_chip)  1.7 us
    ppermute x1, waiting for transfers between devices, body(): far = lax.ppermute(far, 'tile', off_chip)  1.6 us
  transfers between devices with their start and end apart: 2, of which 1 were waited for; matrix products, arithmetic and copies ran while one was open for 0% of the time, Pallas kernels for 7%

profile of v14, /device:TPU:0, one launch (start us, length us, event | category | flops | bytes accessed | tf_op | source)
XLA Modules:
  0.0 56.9 jit_solution(11799490114452202556)
XLA Ops:
  0.6 9.8 %shard_map.68 = f32[16,32,128]{2,1,0:T(8,128)} custom-call(f32[32,6912]{1,0:T(8,128)} %inc_ref.1, s32[4,6912]{1,0:T(4,128)} %bitcast.3, f32[4,6912]{1,0:T(4,128)} %weight_ref.3), custom_call_target="tpu_custom_call" | custom-call | tf_op jit(solution)/shard_map/pallas_call | solution.py:312
  10.4 0.0 copy-start.2
  10.4 0.0 copy-start.3
  10.4 17.5 %all_to_all.10.rec_ref = f32[16,32,128]{2,1,0:T(8,128)S(1)} all-to-all(f32[16,32,128]{2,1,0:T(8,128)} %shard_map.68), channel_id=1, replica_groups=mesh['group'=2,'tile'=16] {'tile'}, dimensions={0} | all-to-all | bytes 524288 | tf_op jit(solution)/shard_map/all_to_all | solution.py:404
  28.0 0.0 copy-done.2
  28.0 0.0 copy-done.3
  28.0 0.9 %shard_map.69 = (f32[10,32,256]{2,1,0:T(8,128)S(1)}, f32[8,32,128]{2,1,0:T(8,128)S(1)}, f32[8,32,128]{2,1,0:T(8,128)S(1)}) custom-call(f32[16,32,128]{2,1,0:T(8,128)S(1)} %all_to_all.10.rec_ref, s32[16,128]{1,0:T(8,128)S(1)} %bitcast.5, f32[18,192]{1,0:T(8,128)S(1)} %copy-done.2), custom_call_target="tpu_custom_call" | custom-call | tf_op jit(solution)/shard_map/pallas_call | solution.py:312
  28.9 0.0 collective-permute-start
  29.0 1.7 %collective-permute-start.1 = (f32[8,32,128]{2,1,0:T(8,128)S(1)}, f32[8,32,128]{2,1,0:T(8,128)S(1)}, u32[]{:S(2)}, u32[]{:S(2)}) collective-permute-start(f32[8,32,128]{2,1,0:T(8,128)S(1)} %get-tuple-element.19), channel_id=1, source_target_pairs={{0,15},{1,2},{2,1},{3,4},{4,3},{5,6},{6,5},{7,8},{8,7},{9,10},{10,... | collective-permute-start | bytes 393224 | tf_op jit(solution)/shard_map/ppermute | solution.py:359
  30.7 0.0 collective-permute-done.edge_ref
  30.7 3.9 %shard_map.70 = (f32[18,32,256]{2,1,0:T(8,128)S(1)}, f32[4,4,32,256]{3,2,1,0:T(8,128)S(1)}, f32[8,32,256]{2,1,0:T(8,128)S(1)}, f32[5,32,256]{2,1,0:T(8,128)S(1)}, f32[16,32,128]{2,1,0:T(8,128)S(1)}) custom-call(f32[16,32,128]{2,1,0:T(8,128)S(1)} %all_to_all.10.rec_ref, f32[10,32,256]{2,1,0:T(8,128)S(1)} %get-tuple-element.14.edges_ref, ...), custom_call_target="tpu_custom_call" | custom-call | flops 536870912 | bytes 8388608 | tf_op jit(solution)/shard_map/pallas_call | solution.py:312
  34.5 1.6 %collective-permute-done.1.edge_ref = f32[8,32,128]{2,1,0:T(8,128)S(1)} collective-permute-done((f32[8,32,128]{2,1,0:T(8,128)S(1)}, f32[8,32,128]{2,1,0:T(8,128)S(1)}, u32[]{:S(2)}, u32[]{:S(2)}) %collective-permute-start.1) | collective-permute-done | bytes 131104 | tf_op jit(solution)/shard_map/ppermute | solution.py:359
  36.1 1.1 %shard_map.71 = (f32[5,32,256]{2,1,0:T(8,128)S(1)}, f32[16,32,128]{2,1,0:T(8,128)S(1)}) custom-call(f32[4,4,32,256]{3,2,1,0:T(8,128)S(1)} %get-tuple-element.16.kept_ref, f32[16,32,128]{2,1,0:T(8,128)S(1)} %get-tuple-element.17.part_ref, f32[18,32,256]{2,1,0:T(8,128)S(1)} %get-tuple-element.18.start_ref, f32[8,32,128]{2,1,0:T(8,128)S(1)} %collective-permute-done.1.edge_ref, ...), custom_call_target="tpu_custom_call" | custom-call | tf_op jit(solution)/shard_map/pallas_call | solution.py:312
  37.2 0.0 copy-start
  37.3 0.0 copy-start.1
  37.3 13.0 %all_to_all.11.ret_ref = f32[16,32,128]{2,1,0:T(8,128)S(1)} all-to-all(f32[16,32,128]{2,1,0:T(8,128)S(1)} %get-tuple-element.20), channel_id=1, replica_groups=mesh['group'=2,'tile'=16] {'tile'}, dimensions={0} | all-to-all | bytes 524288 | tf_op jit(solution)/shard_map/all_to_all | solution.py:404
  50.3 0.0 copy-done
  50.3 0.0 copy-done.1
  50.3 6.6 %shard_map.72 = (f32[32,6912]{1,0:T(8,128)}, f32[18,32,192]{2,1,0:T(8,128)}) custom-call(f32[16,32,128]{2,1,0:T(8,128)S(1)} %all_to_all.11.ret_ref, s32[4,6912]{1,0:T(4,128)S(1)} %bitcast.4, f32[4,6912]{1,0:T(4,128)S(1)} %copy-done.1, f32[8,32,256]{2,1,0:T(8,128)S(1)} %get-tuple-element.21.inner_ref, f32[5,32,256]{2,1,0:T(8,128)S(1)} %get-tuple-element.22.near_ref, ...), custom_call_target="tpu_custom_call" | custom-call | tf_op jit(solution)/shard_map/pallas_call | solution.py:312
Async XLA Ops:
  10.4 17.5 %copy-start.2 = (f32[18,192]{1,0:T(8,128)S(1)}, f32[18,192]{1,0:T(8,128)}, u32[]{:S(2)}) copy-start(f32[18,192]{1,0:T(8,128)} %own_ref.3) | copy-start | bytes 41476
  10.4 17.5 %copy-start.3 = (s32[2048]{0:T(1024)S(1)}, s32[2048]{0:T(1024)}, u32[]{:S(2)}) copy-start(s32[2048]{0:T(1024)} %param.8) | copy-start | bytes 24580
  28.9 1.8 %collective-permute-start = (f32[8,32,128]{2,1,0:T(8,128)S(1)}, f32[8,32,128]{2,1,0:T(8,128)S(1)}, u32[]{:S(2)}, u32[]{:S(2)}) collective-permute-start(f32[8,32,128]{2,1,0:T(8,128)S(1)} %get-tuple-element.15), channel_id=1, source_target_pairs={{0,1},{1,0},{2,3},{3,2},{4,5},{5,4},{6,7},{7,6},{8,9},{9,8},{10,11... | collective-permute-start | bytes 393224 | tf_op jit(solution)/shard_map/ppermute | solution.py:360
  29.0 7.2 %collective-permute-start.1 = (f32[8,32,128]{2,1,0:T(8,128)S(1)}, f32[8,32,128]{2,1,0:T(8,128)S(1)}, u32[]{:S(2)}, u32[]{:S(2)}) collective-permute-start(f32[8,32,128]{2,1,0:T(8,128)S(1)} %get-tuple-element.19), channel_id=1, source_target_pairs={{0,15},{1,2},{2,1},{3,4},{4,3},{5,6},{6,5},{7,8},{8,7},{9,10},{10,... | collective-permute-start | bytes 393224 | tf_op jit(solution)/shard_map/ppermute | solution.py:359
  37.2 13.0 %copy-start = (s32[6912,4]{0,1:T(4,128)S(1)}, s32[6912,4]{0,1:T(4,128)}, u32[]{:S(2)}) copy-start(s32[6912,4]{0,1:T(4,128)} %param.6) | copy-start | bytes 331780
  37.3 13.0 %copy-start.1 = (f32[4,6912]{1,0:T(4,128)S(1)}, f32[4,6912]{1,0:T(4,128)}, u32[]{:S(2)}) copy-start(f32[4,6912]{1,0:T(4,128)} %weight_ref.3) | copy-start | bytes 331780
